TPU v7x, 32 devices: a whole 2x2x4 slice. The times are simulated.
32 devices in a mesh: fsdp: 4 (over y, x), tp: 4 (over z), rep: 2 (over core).
Axes of the slice: x: 2, y: 2, z: 4, core: 2. Of those that a mesh axis runs over, the one named last changes fastest.
Arguments:
- hidden_in: bfloat16 [2, 1024, 5120], P(None, ('fsdp', 'rep')), may hold values from -6 to 6
- norm_gain: float32 [5120], replicated, may hold values from 0.1 to 1.9
- q_weight: bfloat16 [1024, 5120], P('tp'), may hold values from -0.078125 to 0.078125
- q_bias: bfloat16 [1024], P('tp'), may hold values from -3 to 3
- kv_weight: bfloat16 [2, 256, 5120], P(None, 'tp'), may hold values from -0.078125 to 0.078125
- kv_bias: bfloat16 [2, 256], P(None, 'tp'), may hold values from -3 to 3
- o_weight: bfloat16 [5120, 1024], P(None, 'tp'), may hold values from -0.1875 to 0.1875
- q_delta: bfloat16 [1024, 5120], P('tp', ('fsdp', 'rep')), may hold values from -4 to 4
- q_scale_exp: int32 [1024, 160], P('tp', ('fsdp', 'rep')), may hold values from -9 to -5
- kv_delta: bfloat16 [2, 256, 5120], P(None, 'tp', ('fsdp', 'rep')), may hold values from -4 to 4
- kv_scale_exp: int32 [2, 256, 160], P(None, 'tp', ('fsdp', 'rep')), may hold values from -9 to -5
- o_delta: bfloat16 [5120, 1024], P(('fsdp', 'rep'), 'tp'), may hold values from -4 to 4
- o_scale_exp: int32 [5120, 32], P(('fsdp', 'rep'), 'tp'), may hold values from -9 to -5
- key_cache: bfloat16 [1024, 4, 32, 128], P(('fsdp', 'rep'), 'tp'), may hold values from -2000 to 2000
- value_cache: bfloat16 [1024, 4, 32, 128], P(('fsdp', 'rep'), 'tp'), may hold values from -5 to 5
- cache_lengths: int32 [1024], P(('fsdp', 'rep')), may hold values from 1 to 64
Outputs:
- decoded: bfloat16 [2, 1024, 5120], P(None, ('fsdp', 'rep'), 'tp')
All inputs are finite; a program needn't handle non-finite values.
Results may differ from a plain program's by a relative error of at most 0.009.
The roundings to bfloat16 on the way count: a program that leaves them out, or rounds other values in their place, can miss the bound.
Values may be sent and summed in bfloat16 or wider, within the bound.
No kernel may reach another device: no remote copies, remote signals or barrier semaphores. Data moves between devices by JAX's collectives and lax.ppermute only.
A program may use at most 128 MiB of HBM per device.

v0:
```python
import jax
import jax.numpy as jnp
from jax import lax
from jax.sharding import PartitionSpec as P

HD = 128
BLOCK = 32


def swapped(x, axis, stride):
    return lax.ppermute(x, axis, [(i, i ^ 1 << stride) for i in range(lax.axis_size(axis))])


def powers(exponents):
    return jnp.exp2(exponents.astype(jnp.float32)).astype(jnp.bfloat16)


def refresh(base_matrix, delta, factors):
    full_shape = delta.shape
    blocks = delta.astype(jnp.float32).reshape(full_shape[:-1] + (full_shape[-1] // BLOCK, BLOCK))
    change = (blocks * factors.astype(jnp.float32)[..., None]).reshape(full_shape)
    return (base_matrix.astype(jnp.float32) + change).astype(jnp.bfloat16)


def rms_norm(hidden, gain_vector):
    values = hidden.astype(jnp.float32)
    inv_root = lax.rsqrt(jnp.mean(values * values, axis=-1, keepdims=True) + 1e-06)
    return (values * inv_root * gain_vector).astype(jnp.bfloat16)


def rotate(vectors, position):
    half_size = vectors.shape[-1] // 2
    frequency = 1000000.0 ** (-jnp.arange(half_size, dtype=jnp.float32) * 2.0 / vectors.shape[-1])
    angles = position[..., None] * frequency
    cosine = jnp.cos(angles)
    sine_part = jnp.sin(angles)
    lower_half = vectors[..., :half_size]
    upper_half = vectors[..., half_size:]
    return jnp.concatenate(
        [
            lower_half * cosine - upper_half * sine_part,
            upper_half * cosine + lower_half * sine_part,
        ],
        axis=-1,
    )


def shards(
    hidden_in,
    norm_gain,
    q_weight,
    q_bias,
    kv_weight,
    kv_bias,
    o_weight,
    q_delta,
    q_scale_exp,
    kv_delta,
    kv_scale_exp,
    o_delta,
    o_scale_exp,
    key_cache,
    value_cache,
    cache_lengths,
):
    step_count = hidden_in.shape[0]
    row_count = hidden_in.shape[1]
    model_width = hidden_in.shape[2]
    q_width = q_weight.shape[0]
    own_heads = q_width // HD
    half_head = HD // 2
    half_span = key_cache.shape[2]
    delta_rows = jnp.concatenate([q_delta, kv_delta.reshape(-1, q_delta.shape[1])], axis=0)
    delta_factors = jnp.concatenate(
        [powers(q_scale_exp), powers(kv_scale_exp).reshape(-1, q_scale_exp.shape[1])], axis=0
    )
    full_rows, full_factors = (
        lax.all_gather(delta_rows, ("fsdp", "rep"), axis=1, tiled=True),
        lax.all_gather(delta_factors, ("fsdp", "rep"), axis=1, tiled=True),
    )
    base_rows = jnp.concatenate([q_weight, kv_weight.reshape(-1, model_width)], axis=0)
    fresh_qkv = refresh(base_rows, full_rows, full_factors)
    normed = rms_norm(hidden_in, norm_gain).reshape(step_count * row_count, model_width)
    projected = jnp.dot(normed, fresh_qkv.T, preferred_element_type=jnp.float32)
    position = (
        cache_lengths.astype(jnp.float32)[None, :]
        + jnp.arange(step_count, dtype=jnp.float32)[:, None]
    )
    query_part = (projected[:, :q_width] + q_bias.astype(jnp.float32)).reshape(
        step_count, row_count, own_heads, HD
    )
    query_rot = rotate(query_part, position[:, :, None])
    kv_half = (projected[:, q_width:] + kv_bias.reshape(-1).astype(jnp.float32)).reshape(
        step_count, row_count, 2, half_head
    )
    partner_query, partner_kv = swapped((query_rot, kv_half), "tp", 0)
    parity = lax.axis_index("tp") % 2
    is_even = parity == 0
    key_joined = jnp.where(
        is_even,
        jnp.concatenate([kv_half[:, :, 0], partner_kv[:, :, 0]], axis=-1),
        jnp.concatenate([partner_kv[:, :, 0], kv_half[:, :, 0]], axis=-1),
    )
    value_joined = jnp.where(
        is_even,
        jnp.concatenate([kv_half[:, :, 1], partner_kv[:, :, 1]], axis=-1),
        jnp.concatenate([partner_kv[:, :, 1], kv_half[:, :, 1]], axis=-1),
    )
    new_keys = rotate(key_joined, position).astype(jnp.bfloat16)
    new_values = value_joined.astype(jnp.bfloat16)
    queries = jnp.concatenate([query_rot, partner_query], axis=2).astype(jnp.bfloat16)
    inv_root = HD ** (-0.5)
    local_keys = key_cache[:, 0]
    local_values = value_cache[:, 0]
    cache_scores = (
        jnp.einsum("srhd,rpd->srhp", queries, local_keys, preferred_element_type=jnp.float32)
        * inv_root
    )
    fresh_scores = (
        jnp.einsum("srhd,trd->srht", queries, new_keys, preferred_element_type=jnp.float32)
        * inv_root
    )
    slot_ids = parity * half_span + jnp.arange(half_span, dtype=jnp.int32)
    cache_valid = (slot_ids[None, :] < cache_lengths[:, None])[None, :, None, :]
    step_ids = jnp.arange(step_count, dtype=jnp.int32)
    fresh_valid = jnp.logical_and(step_ids[None, :] <= step_ids[:, None], is_even)[:, None, None, :]
    scores = jnp.concatenate([cache_scores, fresh_scores], axis=-1)
    valid = jnp.concatenate(
        [
            jnp.broadcast_to(cache_valid, cache_scores.shape),
            jnp.broadcast_to(fresh_valid, fresh_scores.shape),
        ],
        axis=-1,
    )
    masked = jnp.where(valid, scores, -1e30)
    top_score = jnp.max(masked, axis=-1)
    weights = jnp.where(valid, jnp.exp(masked - top_score[..., None]), 0.0)
    totals = jnp.sum(weights, axis=-1)
    rounded = weights.astype(jnp.bfloat16)
    accum = jnp.einsum(
        "srhp,rpd->srhd", rounded[..., :half_span], local_values, preferred_element_type=jnp.float32
    )
    accum = accum + jnp.einsum(
        "srht,trd->srhd", rounded[..., half_span:], new_values, preferred_element_type=jnp.float32
    )
    recv_accum, recv_top, recv_total = swapped(
        (accum[:, :, own_heads:], top_score[:, :, own_heads:], totals[:, :, own_heads:]), "tp", 0
    )
    own_top = top_score[:, :, :own_heads]
    top_all = jnp.maximum(own_top, recv_top)
    factor_own = jnp.exp(own_top - top_all)
    factor_recv = jnp.exp(recv_top - top_all)
    numerator = (
        factor_own[..., None] * accum[:, :, :own_heads] + factor_recv[..., None] * recv_accum
    )
    denominator = factor_own * totals[:, :, :own_heads] + factor_recv * recv_total
    attention = (
        (numerator / denominator[..., None])
        .astype(jnp.bfloat16)
        .reshape(step_count * row_count, q_width)
    )
    col_width = model_width // lax.axis_size("tp")
    col_start = lax.axis_index("tp") * col_width
    residual = lax.dynamic_slice_in_dim(hidden_in, col_start, col_width, 2).astype(jnp.float32)
    o_rows, o_factors = (
        lax.all_gather(o_delta, ("fsdp", "rep"), axis=0, tiled=True),
        lax.all_gather(powers(o_scale_exp), ("fsdp", "rep"), axis=0, tiled=True),
    )
    fresh_o = refresh(o_weight, o_rows, o_factors)
    partial_value = jnp.dot(attention, fresh_o.T, preferred_element_type=jnp.float32)
    partial_value = partial_value.reshape(step_count, row_count, model_width)
    summed = lax.psum_scatter(partial_value, "tp", scatter_dimension=2, tiled=True)
    result = (residual + summed).astype(jnp.bfloat16)
    return result


def solution(mesh):
    placed = (
        P(None, ("fsdp", "rep"), None),
        P(),
        P("tp", None),
        P("tp"),
        P(None, "tp", None),
        P(None, "tp"),
        P(None, "tp"),
        P("tp", ("fsdp", "rep")),
        P("tp", ("fsdp", "rep")),
        P(None, "tp", ("fsdp", "rep")),
        P(None, "tp", ("fsdp", "rep")),
        P(("fsdp", "rep"), "tp"),
        P(("fsdp", "rep"), "tp"),
        P(("fsdp", "rep"), "tp", None, None),
        P(("fsdp", "rep"), "tp", None, None),
        P(("fsdp", "rep")),
    )
    return jax.shard_map(
        shards,
        mesh=mesh,
        in_specs=placed,
        out_specs=P(None, ("fsdp", "rep"), "tp"),
        check_vma=False,
    )
```

profile of v0, /device:TPU:0, one launch (start us, length us, event | category | flops | bytes accessed | tf_op | source)
XLA Modules:
  0.0 206.8 jit_solution(3678391585215100292)
XLA Ops:
  6.5 1.2 copy.126
  7.8 1.1 copy.127
  8.8 0.8 pad_maximum_fusion
  9.8 1.9 copy.151
  11.7 0.5 multiply_power_fusion
  12.2 4.5 %copy.124 = bf16[256,5120]{0,1:T(8,128)(2,1)} copy(bf16[256,5120]{1,0:T(8,128)(2,1)} %param.18) | data formatting | bytes 5242880 | tf_op args[2]
  16.7 1.8 copy.125
  18.7 10.9 %all-gather = bf16[8,20,384]{2,1,0:T(8,128)(2,1)S(1)} all-gather(bf16[1,20,384]{2,1,0:T(8,128)(2,1)S(1)} %maximum_bitcast_fusion.1), channel_id=1, replica_groups=mesh['fsdp'=4,'tp'=4,'rep'=2] {'fsdp','rep'}, dimensions={0}, use_global_device_ids=true | all-gather | bytes 138240 | tf_op jit(solution)/shard_map/all_gather | solution.py:79
  29.7 2.3 %fusion.2 = f32[2,128]{1,0:T(2,128)S(1)} fusion(bf16[2,128,5120]{2,1,0:T(8,128)(2,1)} %param.16), kind=kLoop, calls=%fused_computation.5 | loop fusion | flops 3931904 | bytes 2622464 | tf_op jit(solution)/shard_map/reduce_sum | solution.py:27
  32.2 0.5 convert_element_type.92
  32.9 0.3 copy.138
  33.3 4.6 %fusion.4 = bf16[2,128,5120]{2,1,0:T(8,128)(2,1)} fusion(bf16[2,128,5120]{2,1,0:T(8,128)(2,1)} %param.16, f32[5120]{0:T(1024)S(1)} %copy-done.4, f32[2,128]{1,0:T(2,128)S(1)} %add_rsqrt_fusion), kind=kLoop, calls=%fused_computation.7 | loop fusion | flops 5242880 | bytes 5264384 | tf_op jit(solution)/shard_map/convert_element_type | solution.py:28
  37.9 10.7 %all-gather.4.cloned.1.call-done = bf16[384,5120]{0,1:T(8,128)(2,1)} async-done(((bf16[384,640]{0,1:T(8,128)(2,1)}), bf16[384,5120]{0,1:T(8,128)(2,1)}) %all-gather.4.cloned.1.call-update) | async-done | bytes 3932176 | tf_op jit(solution)/shard_map/all_gather | solution.py:78
  48.6 4.4 %fusion.1 = bf16[384,5120]{0,1:T(8,128)(2,1)S(1)} fusion(bf16[384,5120]{0,1:T(8,128)(2,1)} %all-gather.4.cloned.1.call-done, bf16[128,5120]{0,1:T(8,128)(2,1)S(1)} %copy.125, bf16[256,5120]{0,1:T(8,128)(2,1)} %copy.124, f32[384,160]{0,1:T(8,128)S(1)} %bitcast.67), kind=kLoop, calls=%fused_computation.2 | loop fusion | flops 15728640 | bytes 12042240 | tf_op jit(solution)/shard_map/convert_element_type | solution.py:22
  53.0 1.6 fusion.34
  54.6 0.2 reshape.165
  55.0 1.6 collective-permute-start.1
  56.7 0.3 fusion.31
  57.0 3.7 %collective-permute-done.1 = f32[2,128,2,64]{1,3,0,2:T(8,128)} collective-permute-done((f32[2,128,2,64]{1,3,0,2:T(8,128)S(1)}, f32[2,128,2,64]{1,3,0,2:T(8,128)}, u32[]{:S(2)}, u32[]{:S(2)}) %collective-permute-start.1) | collective-permute-done | bytes 131104 | tf_op jit(solution)/shard_map/ppermute | solution.py:11
  60.8 0.8 slice_bitcast_fusion.2
  61.7 0.9 multiply_cosine_fusion
  62.8 0.3 multiply_subtract_fusion
  63.1 0.4 pad_maximum_fusion.1
  63.5 1.6 collective-permute-start
  65.0 0.8 slice_bitcast_fusion
  66.2 2.3 %collective-permute-done = bf16[2,128,2,128]{3,2,0,1:T(2,128)(2,1)S(1)} collective-permute-done((bf16[2,128,2,128]{3,2,0,1:T(2,128)(2,1)S(1)}, bf16[2,128,2,128]{3,2,0,1:T(2,128)(2,1)S(1)}, u32[]{:S(2)}, u32[]{:S(2)}) %collective-permute-start) | collective-permute-done | bytes 131104 | tf_op jit(solution)/shard_map/ppermute | solution.py:11
  68.5 2.4 %fusion.22 = f32[128,2,2,4]{3,1,2,0:T(2,128)S(1)} fusion(bf16[2,128,128,1]{2,0,3,1:T(2,128)(2,1)S(1)} %copy.155, bf16[2,128,2,128]{3,2,0,1:T(2,128)(2,1)S(1)} %collective-permute-done, bf16[2,128,2,128]{3,2,0,1:T(2,128)(2,1)S(1)} %pad_maximum_fusion.1), kind=kOutput, calls=%fused_computation.45 | convolution fusion | flops 1048576 | bytes 335872 | tf_op jit(solution)/shard_map/srhd,trd->srht/dot_general | solution.py:120
  71.0 0.3 copy.137
  71.4 0.7 fusion.9
  72.0 0.8 fusion.28
  72.9 1.2 fusion.13
  74.1 0.4 convolution_bitcast_fusion
  74.4 0.6 fusion.10
  75.2 1.6 collective-permute-start.3
  76.7 0.2 fusion.32
  76.9 0.2 fusion.33
  77.2 0.6 collective-permute-start.4
  77.8 1.5 collective-permute-start.2
  79.4 9.2 %all_gather.15 = bf16[5120,8]{0,1:T(8,128)(2,1)S(1)} all-gather(bf16[640,8]{0,1:T(8,128)(2,1)S(1)} %exponential_convert_fusion.1), channel_id=1, replica_groups=mesh['fsdp'=4,'tp'=4,'rep'=2] {'fsdp','rep'}, dimensions={0}, use_global_device_ids=true | all-gather | bytes 92160 | tf_op jit(solution)/shard_map/all_gather | solution.py:167
  88.6 4.5 %copy.150 = bf16[5120,256]{0,1:T(8,128)(2,1)} copy(bf16[5120,256]{1,0:T(8,128)(2,1)} %param.22) | data formatting | bytes 5242880 | tf_op args[6]
  93.1 5.0 %fusion.6 = bf16[5120,256]{0,1:T(8,128)(2,1)} fusion(bf16[5120,256]{0,1:T(8,128)(2,1)} %all-gather.6.cloned.1.call-done, bf16[5120,256]{0,1:T(8,128)(2,1)} %copy.150, f32[5120,8]{0,1:T(8,128)S(1)} %convert_element_type.103), kind=kLoop, calls=%fused_computation.10 | loop fusion | flops 6553600 | bytes 8028160 | tf_op jit(solution)/shard_map/convert_element_type | solution.py:22
  98.3 0.2 copy.141
  98.5 0.2 copy.146
  98.6 0.2 copy.149
  98.8 1.0 fusion.19
  99.9 4.9 %fusion.7 = f32[2,128,5120]{2,1,0:T(8,128)} fusion(bf16[5120,256]{0,1:T(8,128)(2,1)} %fusion.6, bf16[2,128,256]{2,0,1:T(2,128)(2,1)S(1)} %dot_general.25), kind=kOutput, calls=%fused_computation.11 | convolution fusion | flops 671088640 | bytes 7995392 | tf_op jit(solution)/shard_map/dot_general | solution.py:170
  104.8 93.0 %reduce-scatter.2.cloned.1.call-done = f32[2,128,1280]{2,1,0:T(8,128)} async-done(((f32[2,128,5120]{2,1,0:T(8,128)}), f32[2,128,1280]{2,1,0:T(8,128)}) %reduce-scatter.2.cloned.1.call-update) | async-done | bytes 1310736 | tf_op jit(solution)/shard_map/reduce_scatter | solution.py:172
  197.9 2.4 %add_convert_fusion = bf16[2,128,1280]{2,1,0:T(8,128)(2,1)} fusion(f32[2,128,1280]{2,1,0:T(8,128)} %reduce-scatter.2.cloned.1.call-done, bf16[2,128,5120]{2,1,0:T(8,128)(2,1)} %param.16, s32[]{:T(128)S(6)} %select_n.29), kind=kLoop, calls=%fused_computation.13 | loop fusion | flops 983040 | bytes 2621444 | tf_op jit(solution)/shard_map/convert_element_type | solution.py:173
  (71 shorter events, 2.2 us)
Async XLA Ops:
  6.5 67.9 %copy-start = (bf16[128,1,32,128]{3,2,1,0:T(8,128)(2,1)S(1)}, bf16[128,1,32,128]{3,2,1,0:T(8,128)(2,1)}, u32[]{:S(2)}) copy-start(bf16[128,1,32,128]{3,2,1,0:T(8,128)(2,1)} %param.30) | copy-start | bytes 3145732
  6.5 42.0 %all-gather.4.cloned.1.call-start = ((), (), s32[]{:S(2)}) async-start(), calls=%async_computation.1 | async-start | bytes 4423680 | tf_op jit(solution)/shard_map/all_gather | solution.py:78
  9.7 83.3 %all-gather.6.cloned.1.call-start = ((), (), s32[]{:S(2)}) async-start(), calls=%async_computation.2 | async-start | bytes 2949120 | tf_op jit(solution)/shard_map/all_gather | solution.py:166
  11.6 186.2 %reduce-scatter.2.cloned.1.call-start = ((), (), s32[]{:S(2)}) async-start(), calls=%async_computation.3 | async-start | bytes 6553600 | tf_op jit(solution)/shard_map/reduce_scatter | solution.py:172
  12.2 6.3 %copy-start.5 = (s32[2,64,20]{1,0,2:T(2,128)S(1)}, s32[2,64,20]{1,0,2:T(2,128)}, u32[]{:S(2)}) copy-start(s32[2,64,20]{1,0,2:T(2,128)} %param.26) | copy-start | bytes 30724
  12.2 6.5 %copy-start.3 = (s32[256,20]{0,1:T(8,128)S(1)}, s32[256,20]{0,1:T(8,128)}, u32[]{:S(2)}) copy-start(s32[256,20]{0,1:T(8,128)} %param.24) | copy-start | bytes 61444
  16.7 15.3 %copy-start.9 = (bf16[2,64]{1,0:T(2,128)(2,1)S(1)}, bf16[2,64]{1,0:T(2,128)(2,1)}, u32[]{:S(2)}) copy-start(bf16[2,64]{1,0:T(2,128)(2,1)} %param.21) | copy-start | bytes 772
  16.7 15.4 %copy-start.8 = (s32[128]{0:T(128)S(1)}, s32[128]{0:T(128)}, u32[]{:S(2)}) copy-start(s32[128]{0:T(128)} %param.31) | copy-start | bytes 1540
  16.7 15.4 %copy-start.10 = (bf16[256]{0:T(256)(128)(2,1)S(1)}, bf16[256]{0:T(256)(128)(2,1)}, u32[]{:S(2)}) copy-start(bf16[256]{0:T(256)(128)(2,1)} %param.19) | copy-start | bytes 1540
  16.7 16.5 %copy-start.6 = (s32[640,8]{0,1:T(8,128)S(1)}, s32[640,8]{0,1:T(8,128)}, u32[]{:S(2)}) copy-start(s32[640,8]{0,1:T(8,128)} %param.28) | copy-start | bytes 61444
  16.7 16.5 %copy-start.4 = (f32[5120]{0:T(1024)S(1)}, f32[5120]{0:T(1024)}, u32[]{:S(2)}) copy-start(f32[5120]{0:T(1024)} %param.17) | copy-start | bytes 61444
  48.6 4.4 %copy-start.1 = (bf16[2,128,5120]{2,1,0:T(8,128)(2,1)S(1)}, bf16[2,128,5120]{2,1,0:T(8,128)(2,1)}, u32[]{:S(2)}) copy-start(bf16[2,128,5120]{2,1,0:T(8,128)(2,1)} %fusion.4) | copy-start | bytes 7864324
  53.0 3.5 %copy-start.7 = (f32[256]{0:T(256)S(1)}, f32[256]{0:T(256)}, u32[]{:S(2)}) copy-start(f32[256]{0:T(256)} %convert_element_type.92) | copy-start | bytes 3076
  54.6 16.7 %copy-start.2 = (bf16[128,1,32,128]{3,2,1,0:T(8,128)(2,1)S(1)}, bf16[128,1,32,128]{3,2,1,0:T(8,128)(2,1)}, u32[]{:S(2)}) copy-start(bf16[128,1,32,128]{3,2,1,0:T(8,128)(2,1)} %param.29) | copy-start | bytes 3145732
  55.0 5.8 %collective-permute-start.1 = (f32[2,128,2,64]{1,3,0,2:T(8,128)S(1)}, f32[2,128,2,64]{1,3,0,2:T(8,128)}, u32[]{:S(2)}, u32[]{:S(2)}) collective-permute-start(f32[2,128,2,64]{1,3,0,2:T(8,128)S(1)} %copy.133), channel_id=1, source_target_pairs={{0,2},{2,0},{4,6},{6,4},{1,3},{3,1},{5,7},{7,5},{8,10},{10,8},{12,... | collective-permute-start | bytes 393224 | tf_op jit(solution)/shard_map/ppermute | solution.py:11
  63.5 5.0 %collective-permute-start = (bf16[2,128,2,128]{3,2,0,1:T(2,128)(2,1)S(1)}, bf16[2,128,2,128]{3,2,0,1:T(2,128)(2,1)S(1)}, u32[]{:S(2)}, u32[]{:S(2)}) collective-permute-start(bf16[2,128,2,128]{3,2,0,1:T(2,128)(2,1)S(1)} %pad_maximum_fusion.1), channel_id=1, source_target_pairs={{0,2},{2,0},{4,6},{6,4},{1,3},{3,1},{5,7},{7,5},{8,10},{10,8},{12,... | collective-permute-start | bytes 393224 | tf_op jit(solution)/shard_map/ppermute | solution.py:11
  75.2 23.6 %collective-permute-start.3 = (f32[2,128,2,128]{3,2,0,1:T(2,128)S(1)}, f32[2,128,2,128]{3,2,0,1:T(2,128)S(1)}, u32[]{:S(2)}, u32[]{:S(2)}) collective-permute-start(f32[2,128,2,128]{3,2,0,1:T(2,128)S(1)} %slice.91), channel_id=1, source_target_pairs={{0,2},{2,0},{4,6},{6,4},{1,3},{3,1},{5,7},{7,5},{8,10},{10,8},{12,... | collective-permute-start | bytes 786440 | tf_op jit(solution)/shard_map/ppermute | solution.py:11
  77.2 21.1 %collective-permute-start.4 = (f32[2,128,2]{1,2,0:T(2,128)S(1)}, f32[2,128,2]{1,2,0:T(2,128)S(1)}, u32[]{:S(2)}, u32[]{:S(2)}) collective-permute-start(f32[2,128,2]{1,2,0:T(2,128)S(1)} %copy.172), channel_id=1, source_target_pairs={{0,2},{2,0},{4,6},{6,4},{1,3},{3,1},{5,7},{7,5},{8,10},{10,8},{12,... | collective-permute-start | bytes 6152 | tf_op jit(solution)/shard_map/ppermute | solution.py:11
  77.8 20.4 %collective-permute-start.2 = (f32[2,128,2]{1,2,0:T(2,128)S(1)}, f32[2,128,2]{1,2,0:T(2,128)S(1)}, u32[]{:S(2)}, u32[]{:S(2)}) collective-permute-start(f32[2,128,2]{1,2,0:T(2,128)S(1)} %copy.170), channel_id=1, source_target_pairs={{0,2},{2,0},{4,6},{6,4},{1,3},{3,1},{5,7},{7,5},{8,10},{10,8},{12,... | collective-permute-start | bytes 6152 | tf_op jit(solution)/shard_map/ppermute | solution.py:11
Sparse Core Ops, SparseCore 0:
  9.8 38.6 all-gather.3
  50.5 30.0 all-gather.5
  105.0 92.8 reduce-scatter.1
where the time goes:
time: 207 us
  waiting for transfers between devices  110 us (53%)
  other arithmetic  25.6 us (12%)
  local copies, waits for them, and re-layouts  20.4 us (10%)
  blocking collectives  20.1 us (10%)
  between operations  13.5 us (7%)
  matrix products  10.5 us (5%)
  starting transfers between devices  6.82 us (3%)
    reduce_scatter x1, waiting for transfers between devices, shards(): lax.psum_scatter(partial_value, 'tp', scatter_dimension=2, tiled=True)  93 us
    unnamed x30, local copies, waits for them, and re-layouts  12.4 us
    all_gather x1, blocking collectives, shards(): lax.all_gather(delta_factors, ('fsdp', 'rep'), axis=1, tiled=True)  10.9 us
    all_gather x1, waiting for transfers between devices, shards(): lax.all_gather(delta_rows, ('fsdp', 'rep'), axis=1, tiled=True)  10.7 us
    convert_element_type x2, other arithmetic, refresh(): return (base_matrix.astype(jnp.float32) + change).astype(jnp.bfloat16)  9.46 us
    all_gather x1, blocking collectives, shards(): lax.all_gather(powers(o_scale_exp), ('fsdp', 'rep'), axis=0, tiled=True)  9.2 us
    ppermute x5, starting transfers between devices, swapped(): lax.ppermute(x, axis, [(i, i ^ 1 << stride) for i in range(lax.axis_size(...  6.74 us
    ppermute x5, waiting for transfers between devices, swapped(): lax.ppermute(x, axis, [(i, i ^ 1 << stride) for i in range(lax.axis_size(...  6.1 us
  transfers between devices with their start and end apart: 8, of which 4 were waited for; matrix products, arithmetic and copies ran while one was open for 22% of the time, Pallas kernels for 0%

commit v1 on v0

v1 whole, which is shorter than its diff:
```python
import functools

import jax
import jax.numpy as jnp
from jax import lax
from jax.experimental import pallas as pl
from jax.experimental.pallas import tpu as pltpu
from jax.sharding import PartitionSpec as P

HD = 128
BLOCK = 32
F32 = jnp.float32
BF16 = jnp.bfloat16
FR = ("fsdp", "rep")
MB = 1 << 20


def swap(x, axis, xor):
    return lax.ppermute(x, axis, [(i, i ^ xor) for i in range(lax.axis_size(axis))])


def nt_dot(a, b):
    return lax.dot_general(a, b, (((1,), (1,)), ((), ())), preferred_element_type=F32)


def params(mib):
    return pltpu.CompilerParams(vmem_limit_bytes=mib * MB)


def expand(exponents, width):
    blocks = exponents.shape[1]
    factor = jnp.exp2(exponents.astype(F32)).astype(BF16)
    row = lax.broadcasted_iota(jnp.int32, (blocks, width), 0)
    col = lax.broadcasted_iota(jnp.int32, (blocks, width), 1)
    spread = jnp.where((col >> 5) == row, 1.0, 0.0).astype(BF16)
    return jnp.dot(factor, spread, preferred_element_type=F32)


def refreshed(base, delta, exponents):
    change = delta.astype(F32) * expand(exponents, delta.shape[1])
    return (base.astype(F32) + change).astype(BF16)


def fresh_qkv_kernel(at, qw, kvw, qd, qe, kvd, kve, first, second):
    half = qw.shape[0] // 2
    query = refreshed(qw[...], qd[...], qe[...])
    first[:half] = query[:half]
    second[:half] = query[half:]
    first[half:] = refreshed(kvw[0], kvd[0], kve[0])
    second[half:] = refreshed(kvw[1], kvd[1], kve[1])


def fresh_qkv(place, q_weight, kv_weight, q_delta, q_exp, kv_delta, kv_exp):
    rows, width = q_delta.shape
    narrow = kv_delta.shape[1]
    if width % 128:
        start = place[0] * width
        q_weight = lax.dynamic_slice_in_dim(q_weight, start, width, 1)
        kv_weight = lax.dynamic_slice_in_dim(kv_weight, start, width, 2)
        place = jnp.zeros_like(place)
    whole = lambda a: pl.BlockSpec(a.shape, lambda i, at: (0,) * a.ndim)
    out = jax.ShapeDtypeStruct((rows // 2 + narrow, width), BF16)
    return pl.pallas_call(
        fresh_qkv_kernel,
        out_shape=(out, out),
        grid_spec=pltpu.PrefetchScalarGridSpec(
            num_scalar_prefetch=1,
            grid=(1,),
            in_specs=[
                pl.BlockSpec((rows, width), lambda i, at: (0, at[0])),
                pl.BlockSpec((2, narrow, width), lambda i, at: (0, 0, at[0])),
                whole(q_delta),
                whole(q_exp),
                whole(kv_delta),
                whole(kv_exp),
            ],
            out_specs=(whole(out), whole(out)),
        ),
        compiler_params=params(16),
        name="fresh_qkv",
    )(place, q_weight, kv_weight, q_delta, q_exp, kv_delta, kv_exp)


def fresh_o_kernel(at, ow, od, oe, *outs):
    rows = outs[0].shape[0]
    for i, out in enumerate(outs):
        part = slice(i * rows, (i + 1) * rows)
        out[...] = refreshed(ow[part], od[part], oe[part])


def fresh_o(place, o_weight, o_delta, o_exp, parts):
    rows, width = o_delta.shape
    whole = lambda a: pl.BlockSpec(a.shape, lambda i, at: (0,) * a.ndim)
    out = jax.ShapeDtypeStruct((rows // parts, width), BF16)
    return pl.pallas_call(
        fresh_o_kernel,
        out_shape=(out,) * parts,
        grid_spec=pltpu.PrefetchScalarGridSpec(
            num_scalar_prefetch=1,
            grid=(1,),
            in_specs=[
                pl.BlockSpec((rows, width), lambda i, at: (at[0], 0)),
                whole(o_delta),
                whole(o_exp),
            ],
            out_specs=(whole(out),) * parts,
        ),
        compiler_params=params(16),
        name="fresh_o",
    )(place, o_weight, o_delta, o_exp)


def norm_kernel(hidden, gain, out):
    values = hidden[0].astype(F32)
    root = lax.rsqrt(jnp.mean(values * values, axis=-1, keepdims=True) + 1e-06)
    out[...] = (values * root * gain[...]).astype(BF16)


def normalize(hidden, gain):
    steps, rows, width = hidden.shape
    tile = min(rows, 64)
    return pl.pallas_call(
        norm_kernel,
        out_shape=jax.ShapeDtypeStruct((steps * rows, width), BF16),
        grid=(steps, rows // tile),
        in_specs=[
            pl.BlockSpec((1, tile, width), lambda s, r: (s, r, 0)),
            pl.BlockSpec((1, width), lambda s, r: (0, 0)),
        ],
        out_specs=pl.BlockSpec((tile, width), lambda s, r: (s * (rows // tile) + r, 0)),
        compiler_params=params(16),
        name="norm",
    )(hidden, gain.reshape(1, width))


def project_kernel(count, at, normed, *refs):
    shards, (out0, out1) = refs[: 2 * count], refs[2 * count :]
    for half, out in enumerate((out0, out1)):
        total = None
        for n in range(count):
            shard = shards[2 * n + half][...]
            width = shard.shape[1]
            cols = pl.ds(pl.multiple_of(at[n] * width, 128), width)
            term = nt_dot(normed[:, cols], shard)
            total = term if total is None else total + term
        out[...] = total


def project(places, normed, shards):
    count = len(shards)
    out = jax.ShapeDtypeStruct((normed.shape[0], shards[0][0].shape[0]), F32)
    vmem = pl.BlockSpec(memory_space=pltpu.VMEM)
    return pl.pallas_call(
        functools.partial(project_kernel, count),
        out_shape=(out, out),
        in_specs=[pl.BlockSpec(memory_space=pltpu.SMEM)] + [vmem] * (1 + 2 * count),
        out_specs=(vmem, vmem),
        compiler_params=params(24),
        name="project",
    )(places, normed, *[a for pair in shards for a in pair])


def finish_kernel(
    count, steps, at, parity, normed, total0, total1, qb, kvb, cosine, sine, *refs
):
    shards, (own, other, packed) = refs[: 2 * count], refs[2 * count :]
    totals = [total0[...], total1[...]]
    for n in range(count):
        width = shards[2 * n].shape[1]
        cols = pl.ds(pl.multiple_of(at[n] * width, 128), width)
        for half in range(2):
            totals[half] = totals[half] + nt_dot(normed[:, cols], shards[2 * n + half][...])
    span = qb.shape[1] // 2
    for half in range(2):
        for head in range(span // HD):
            lanes = slice(head * HD, (head + 1) * HD)
            cols = slice(half * span + head * HD, half * span + (head + 1) * HD)
            query = totals[half][:, lanes] + qb[:, cols].astype(F32)
            turned = query * cosine[...] + pltpu.roll(query, HD // 2, 1) * sine[...]
            packed[:, cols] = turned.astype(BF16)
    key = totals[0][:, span:] + kvb[0:1].astype(F32)
    value = totals[1][:, span:] + kvb[1:2].astype(F32)
    high = key.astype(BF16)
    rest = key - high.astype(F32)
    middle = rest.astype(BF16)
    low = (rest - middle.astype(F32)).astype(BF16)
    packed[:, 2 * span : 2 * span + HD] = jnp.concatenate([high, middle], axis=1)
    packed[:, 2 * span + HD :] = jnp.concatenate([low, value.astype(BF16)], axis=1)
    rows = packed.shape[0] // steps
    near = pl.multiple_of(parity[0] * (rows // 2), 16)
    far = pl.multiple_of((1 - parity[0]) * (rows // 2), 16)
    for s in range(steps):
        own[s] = packed[pl.ds(s * rows + near, rows // 2), :]
        other[s] = packed[pl.ds(s * rows + far, rows // 2), :]


def finish(places, parity, normed, totals, q_bias, kv_bias, cosine, sine, shards, steps):
    count = len(shards)
    rows = normed.shape[0] // steps
    width = q_bias.shape[0] + 2 * HD
    vmem = pl.BlockSpec(memory_space=pltpu.VMEM)
    smem = pl.BlockSpec(memory_space=pltpu.SMEM)
    out = jax.ShapeDtypeStruct((steps, rows // 2, width), BF16)
    return pl.pallas_call(
        functools.partial(finish_kernel, count, steps),
        out_shape=(out, out),
        in_specs=[smem, smem] + [vmem] * (7 + 2 * count),
        out_specs=(vmem, vmem),
        scratch_shapes=[pltpu.VMEM((steps * rows, width), BF16)],
        compiler_params=params(24),
        name="finish",
    )(
        places, parity, normed, *totals, q_bias.reshape(1, -1), kv_bias, cosine, sine,
        *[a for pair in shards for a in pair],
    )


GROUP = 16


def attend_kernel(
    parity, own, other, cosine, sine, keys, values, swapped, near_ok, far_ok, out, new_k, new_v
):
    steps, rows, width = own.shape
    heads = (width - 2 * HD) // HD
    half = HD // 2
    even = parity[0] == 0
    scale = HD ** (-0.5)
    base = width - 2 * HD

    def key_of(ref, s):
        top = ref[s, :, base : base + HD].astype(F32)
        rest = ref[s, :, base + HD :].astype(F32)
        return top[:, :half] + (top[:, half:] + rest[:, :half]), rest[:, half:]

    for s in range(steps):
        key_a, value_a = key_of(own, s)
        key_b, value_b = key_of(other, s)
        key = jnp.where(
            even,
            jnp.concatenate([key_a, key_b], axis=1),
            jnp.concatenate([key_b, key_a], axis=1),
        )
        value = jnp.where(
            even,
            jnp.concatenate([value_a, value_b], axis=1),
            jnp.concatenate([value_b, value_a], axis=1),
        )
        at = pl.ds(pl.multiple_of(s * 2 * rows + parity[0] * rows, 16), rows)
        turned = key * cosine[at, :] + pltpu.roll(key, half, 1) * sine[at, :]
        new_k[s] = turned.astype(BF16)
        new_v[s] = value.astype(BF16)

    span = keys.shape[1]
    count = steps * 2 * heads * GROUP
    lane = GROUP * span
    row_of = lax.broadcasted_iota(jnp.int32, (count, lane), 0) & (GROUP - 1)
    diagonal = row_of == lax.broadcasted_iota(jnp.int32, (count, lane), 1) // span
    fresh = GROUP * steps
    fresh_row = lax.broadcasted_iota(jnp.int32, (count, fresh), 0)
    fresh_col = lax.broadcasted_iota(jnp.int32, (count, fresh), 1)
    fresh_ok = jnp.logical_and(
        (fresh_row & (GROUP - 1)) == (fresh_col & (GROUP - 1)),
        fresh_col // GROUP <= fresh_row // (2 * heads * GROUP),
    )
    lowest = -1e30
    for g in range(rows // GROUP):
        at = slice(g * GROUP, (g + 1) * GROUP)
        query = jnp.concatenate(
            [
                ref[s, at, h * HD : (h + 1) * HD]
                for s in range(steps)
                for ref in (own, other)
                for h in range(heads)
            ],
            axis=0,
        )
        near_k = keys[at].reshape(lane, HD)
        near_v = values[at].reshape(lane, HD)
        far_k = swapped[0, at].reshape(lane, HD)
        far_v = swapped[1, at].reshape(lane, HD)
        fresh_k = jnp.concatenate([new_k[s, at] for s in range(steps)], axis=0)
        fresh_v = jnp.concatenate([new_v[s, at] for s in range(steps)], axis=0)
        ok_n = jnp.logical_and(diagonal, near_ok[g : g + 1, :] > 0)
        ok_f = jnp.logical_and(diagonal, far_ok[g : g + 1, :] > 0)
        score_n = jnp.where(ok_n, nt_dot(query, near_k) * scale, lowest)
        score_f = jnp.where(ok_f, nt_dot(query, far_k) * scale, lowest)
        score_x = jnp.where(fresh_ok, nt_dot(query, fresh_k) * scale, lowest)
        top_n = jnp.max(score_n, axis=1, keepdims=True)
        top_f = jnp.max(score_f, axis=1, keepdims=True)
        top_x = jnp.max(score_x, axis=1, keepdims=True)
        top_n = jnp.where(even, jnp.maximum(top_n, top_x), top_n)
        top_f = jnp.where(even, top_f, jnp.maximum(top_f, top_x))
        top_x = jnp.where(even, top_n, top_f)
        weight_n = jnp.where(ok_n, jnp.exp(score_n - top_n), 0.0)
        weight_f = jnp.where(ok_f, jnp.exp(score_f - top_f), 0.0)
        weight_x = jnp.where(fresh_ok, jnp.exp(score_x - top_x), 0.0)
        top_all = jnp.maximum(top_n, top_f)
        factor_n = jnp.exp(top_n - top_all)
        factor_f = jnp.exp(top_f - top_all)
        factor_x = jnp.where(even, factor_n, factor_f)
        acc = (
            factor_n * jnp.dot(weight_n.astype(BF16), near_v, preferred_element_type=F32)
            + factor_f * jnp.dot(weight_f.astype(BF16), far_v, preferred_element_type=F32)
            + factor_x * jnp.dot(weight_x.astype(BF16), fresh_v, preferred_element_type=F32)
        )
        total = (
            factor_n * jnp.sum(weight_n, axis=1, keepdims=True)
            + factor_f * jnp.sum(weight_f, axis=1, keepdims=True)
            + factor_x * jnp.sum(weight_x, axis=1, keepdims=True)
        )
        result = (acc / total).astype(BF16)
        for s in range(steps):
            for h in range(2 * heads):
                first = (s * 2 * heads + h) * GROUP
                out[s, at, h * HD : (h + 1) * HD] = result[first : first + GROUP]


def attend(parity, own, other, cosine, sine, keys, values, swapped, near_ok, far_ok):
    steps, rows, width = own.shape
    span = keys.shape[1]
    whole = lambda a: pl.BlockSpec(a.shape, lambda i, at: (0,) * a.ndim)
    half = pl.BlockSpec((rows, span, HD), lambda i, at: (at[0], 0, 0))
    out = jax.ShapeDtypeStruct((steps, rows, 2 * (width - 2 * HD)), BF16)
    return pl.pallas_call(
        attend_kernel,
        out_shape=out,
        grid_spec=pltpu.PrefetchScalarGridSpec(
            num_scalar_prefetch=1,
            grid=(1,),
            in_specs=[
                whole(own), whole(other), whole(cosine), whole(sine), half, half,
                whole(swapped), whole(near_ok), whole(far_ok),
            ],
            out_specs=whole(out),
            scratch_shapes=[pltpu.VMEM((steps, rows, HD), BF16)] * 2,
        ),
        compiler_params=params(24),
        name="attend",
    )(parity, own, other, cosine, sine, keys, values, swapped, near_ok, far_ok)


def pick_kernel(at, *refs):
    count = len(refs) // 2
    for k in range(count):
        for i in range(count):

            @pl.when((at[0] ^ k) == i)
            def _(k=k, i=i):
                refs[count + k][...] = refs[i][...]


def pick(where, blocks):
    vmem = pl.BlockSpec(memory_space=pltpu.VMEM)
    return pl.pallas_call(
        pick_kernel,
        out_shape=tuple(jax.ShapeDtypeStruct(b.shape, b.dtype) for b in blocks),
        in_specs=[pl.BlockSpec(memory_space=pltpu.SMEM)] + [vmem] * len(blocks),
        out_specs=(vmem,) * len(blocks),
        compiler_params=params(8),
        name="pick",
    )(where, *blocks)


def output_kernel(count, at, parity, a0, a1, a2, a3, hidden, *refs):
    shards, out, weight = refs[:count], refs[count], refs[count + 1]
    rows = shards[0].shape[0] // 4
    width = shards[0].shape[1]
    for n, shard in enumerate(shards):
        place = pl.ds(pl.multiple_of(at[n] * rows, 16), rows)
        for k in range(4):
            weight[place, k * width : (k + 1) * width] = shard[k * rows : (k + 1) * rows]
    steps, half = a0.shape[:2]
    near = pl.multiple_of(parity[0] * half, 16)
    far = pl.multiple_of((1 - parity[0]) * half, 16)
    flat = lambda ref: ref[...].reshape(steps * half, 2 * width)
    b1, b3 = flat(a1), flat(a3)
    top = nt_dot(flat(a0), weight[:, : 2 * width]) + nt_dot(flat(a2), weight[:, 2 * width :])
    low = (
        nt_dot(b1[:, :width], weight[:, width : 2 * width])
        + nt_dot(b1[:, width:], weight[:, :width])
        + nt_dot(b3[:, :width], weight[:, 3 * width :])
        + nt_dot(b3[:, width:], weight[:, 2 * width : 3 * width])
    )
    for start, total in ((near, top), (far, low)):
        for s in range(steps):
            place = pl.ds(start, half)
            mixed = total[s * half : (s + 1) * half]
            out[s, place, :] = (hidden[s, place, :].astype(F32) + mixed).astype(BF16)


def output(places, parity, column, parts, hidden, shards):
    steps, half, _ = parts[0].shape
    rows = hidden.shape[1]
    width = shards[0].shape[0] // 4 * len(shards)
    depth = shards[0].shape[1]
    whole = lambda a: pl.BlockSpec(a.shape, lambda i, *at: (0,) * a.ndim)
    out = jax.ShapeDtypeStruct((steps, rows, width), BF16)
    return pl.pallas_call(
        lambda at, parity, column, *refs: output_kernel(len(shards), at, parity, *refs),
        out_shape=out,
        grid_spec=pltpu.PrefetchScalarGridSpec(
            num_scalar_prefetch=3,
            grid=(1,),
            in_specs=[whole(p) for p in parts]
            + [pl.BlockSpec((steps, rows, width), lambda i, at, p, c: (0, 0, c[0]))]
            + [whole(s) for s in shards],
            out_specs=whole(out),
            scratch_shapes=[pltpu.VMEM((width, 4 * depth), BF16)],
        ),
        compiler_params=params(32),
        name="output",
    )(places, parity, column, *parts, hidden, *shards)


def one(value):
    return jnp.asarray(value, jnp.int32).reshape(1)


def shards(
    hidden_in,
    norm_gain,
    q_weight,
    q_bias,
    kv_weight,
    kv_bias,
    o_weight,
    q_delta,
    q_scale_exp,
    kv_delta,
    kv_scale_exp,
    o_delta,
    o_scale_exp,
    key_cache,
    value_cache,
    cache_lengths,
):
    steps, rows, model_width = hidden_in.shape
    q_width = q_weight.shape[0]
    span = key_cache.shape[2]
    half = rows // 2
    fsdp, tp, rep = (lax.axis_size(a) for a in ("fsdp", "tp", "rep"))
    f, t, r = (lax.axis_index(a) for a in ("fsdp", "tp", "rep"))
    shard_width = q_delta.shape[1]
    col_width = model_width // tp
    small = fsdp == 4 and tp == 4 and rep == 2 and shard_width % 128 == 0 and col_width % 128 == 0
    parity = t % 2
    parity_ref = one(parity)
    place = one(f * rep + r)

    far_start = (1 - parity) * half
    far_cache = jnp.stack(
        [lax.dynamic_slice_in_dim(c[:, 0], far_start, half, 0) for c in (key_cache, value_cache)]
    )
    swapped = swap(far_cache, "tp", 1)

    first, second = fresh_qkv(
        place, q_weight, kv_weight, q_delta, q_scale_exp, kv_delta, kv_scale_exp
    )
    normed = normalize(hidden_in, norm_gain)

    position = (
        cache_lengths.astype(F32)[None, :] + jnp.arange(steps, dtype=F32)[:, None]
    ).reshape(-1, 1)
    frequency = 1000000.0 ** (-jnp.arange(HD // 2, dtype=F32) * 2.0 / HD)
    angles = position * frequency
    cosine, sine = jnp.cos(angles), jnp.sin(angles)
    cosine = jnp.concatenate([cosine, cosine], axis=1)
    sine = jnp.concatenate([-sine, sine], axis=1)

    own_lengths = lax.dynamic_slice_in_dim(cache_lengths, parity * half, half, 0)
    slot = jnp.arange(span, dtype=jnp.int32)[None, :]
    near_ok = (slot + parity * span < own_lengths[:, None]).astype(jnp.int32)
    far_ok = (slot + (1 - parity) * span < own_lengths[:, None]).astype(jnp.int32)
    near_ok = near_ok.reshape(half // GROUP, GROUP * span)
    far_ok = far_ok.reshape(half // GROUP, GROUP * span)

    if small:
        o_parts = fresh_o(place, o_weight, o_delta, o_scale_exp, 4)
        x1, y2 = swap(first, "fsdp", 1), swap(second, "fsdp", 2)
        x2, y1 = swap(second, "fsdp", 1), swap(first, "fsdp", 2)
        d1, d2 = swap(x1, "fsdp", 2), swap(y2, "fsdp", 1)
        near = [(first, second), (x1, x2), (y1, y2)]
        across = [tuple(swap(a, "rep", 1) for a in pair) for pair in near]
        last = [(d1, d2), (swap(d1, "rep", 1), swap(d2, "rep", 1))]
        at = lambda i, j: (f ^ i) * rep + (r ^ j)
        early_at = jnp.stack([at(i, j) for j in (0, 1) for i in (0, 1, 2)]).astype(jnp.int32)
        last_at = jnp.stack([at(3, 0), at(3, 1)]).astype(jnp.int32)
        totals = project(early_at, normed, near + across)
        own, other = finish(
            last_at, parity_ref, normed, totals, q_bias, kv_bias, cosine, sine, last, steps
        )
    else:
        full = [lax.all_gather(a, FR, axis=1, tiled=True) for a in (first, second)]
        totals = [jnp.dot(normed, a.T, preferred_element_type=F32) for a in full]
        own, other = finish(
            place, parity_ref, normed, totals, q_bias, kv_bias, cosine, sine, [], steps
        )

    received = swap(other, "tp", 1)
    attention = attend(
        parity_ref, own, received, cosine, sine, key_cache[:, 0], value_cache[:, 0], swapped,
        near_ok, far_ok,
    )

    if small:
        quarters = [o_parts[0]] + [swap(o_parts[i], "fsdp", i) for i in (1, 2, 3)]
        picked = pick(one(f ^ t), quarters)
        blocks = [picked[0]] + [swap(picked[k], "tp", k) for k in (1, 2, 3)]
        stacked = jnp.concatenate(blocks, axis=0)
        o_near = [stacked] + [swap(stacked, "fsdp", i) for i in (1, 2, 3)]
        o_far = [swap(a, "rep", 1) for a in o_near]
        spot = lambda i, j: (r ^ j) * 4 + (f ^ i ^ t)
        o_at = jnp.stack([spot(i, j) for j in (0, 1) for i in range(4)]).astype(jnp.int32)
        parts = [attention] + [swap(attention, "tp", k) for k in (1, 2, 3)]
        return output(o_at, parity_ref, one(t), parts, hidden_in, o_near + o_far)

    own_o = fresh_o(place, o_weight, o_delta, o_scale_exp, 1)[0]
    full_o = lax.all_gather(own_o, FR, axis=0, tiled=True)
    own_cols = lax.all_to_all(
        full_o.reshape(tp, col_width, q_width), "tp", split_axis=0, concat_axis=2, tiled=True
    ).reshape(col_width, tp * q_width)
    everyone = lax.all_gather(attention, "tp", axis=0)
    everyone = everyone.reshape(tp // 2, 2, steps, half, 2, q_width)
    odd = everyone[:, 1][:, :, :, ::-1]
    everyone = jnp.stack([everyone[:, 0], odd], axis=0)
    features = everyone.transpose(2, 0, 3, 1, 4, 5).reshape(steps * rows, tp * q_width)
    mixed = jnp.dot(features, own_cols.T, preferred_element_type=F32)
    residual = lax.dynamic_slice_in_dim(hidden_in, t * col_width, col_width, 2).astype(F32)
    return (residual + mixed.reshape(steps, rows, col_width)).astype(BF16)


def solution(mesh):
    placed = (
        P(None, ("fsdp", "rep"), None),
        P(),
        P("tp", None),
        P("tp"),
        P(None, "tp", None),
        P(None, "tp"),
        P(None, "tp"),
        P("tp", ("fsdp", "rep")),
        P("tp", ("fsdp", "rep")),
        P(None, "tp", ("fsdp", "rep")),
        P(None, "tp", ("fsdp", "rep")),
        P(("fsdp", "rep"), "tp"),
        P(("fsdp", "rep"), "tp"),
        P(("fsdp", "rep"), "tp", None, None),
        P(("fsdp", "rep"), "tp", None, None),
        P(("fsdp", "rep")),
    )
    return jax.shard_map(
        shards,
        mesh=mesh,
        in_specs=placed,
        out_specs=P(None, ("fsdp", "rep"), "tp"),
        check_vma=False,
    )
```

time: 207 us -> 102 us (0.49)
  waiting for transfers between devices: 110 us -> 26.3 us
  starting transfers between devices: 6.82 us -> 31 us
  other arithmetic: 25.6 us -> 3.74 us
  blocking collectives: 20.1 us -> 0 us
  Pallas kernels: 0 us -> 16.5 us
  between operations: 13.5 us -> 0.3 us
  matrix products: 10.5 us -> 0 us
  local copies, waits for them, and re-layouts: 20.4 us -> 22.9 us
    reduce_scatter x1 -> x0, waiting for transfers between devices: 93 us -> none  [shards(): lax.psum_scatter(partial_value, 'tp', scatter_dimension=2, tiled=True)]
    ppermute x5 -> x32, starting transfers between devices: 6.74 us -> 31 us  [swap(): lax.ppermute(x, axis, [(i, i ^ xor) for i in range(lax.axis_size(axis))])]
    ppermute x5 -> x32, waiting for transfers between devices: 6.1 us -> 26.3 us  [swap(): lax.ppermute(x, axis, [(i, i ^ xor) for i in range(lax.axis_size(axis))])]
    all_gather x2 -> x0, blocking collectives: 20.1 us -> none  [the longest x1 10.9 us: shards(): lax.all_gather(delta_factors, ('fsdp', 'rep'), axis=1, tiled=True)]
    convert_element_type x12 -> x2, other arithmetic: 18.1 us -> 0.01 us  [the longest x1 0.01 us: shards(): (slot + (1 - parity) * span < own_lengths[:, None]).astype(jnp.int32)]
    pallas_call x0 -> x8, Pallas kernels: none -> 16.5 us  [the longest x1 5.06 us: output(): pl.pallas_call(lambda at, parity, column, *refs: output_kernel(len(shards...]
    all_gather x2 -> x0, waiting for transfers between devices: 10.7 us -> none  [the longest x1 10.7 us: shards(): lax.all_gather(delta_rows, ('fsdp', 'rep'), axis=1, tiled=True)]
    dot_general x6 -> x0, matrix products: 10.5 us -> none  [the longest x1 4.91 us: shards(): jnp.dot(attention, fresh_o.T, preferred_element_type=jnp.float32)]
  transfers between devices with their start and end apart: 8 -> 32, of which waited for: 4 -> 10; matrix products, arithmetic and copies ran while one was open for 22% -> 8% of each run, Pallas kernels for 0% -> 11%
where the time goes in v1:
time: 102 us; the launch traced here: 101 us
  starting transfers between devices  31 us (30%)
  waiting for transfers between devices  26.3 us (26%)
  local copies, waits for them, and re-layouts  22.9 us (22%)
  Pallas kernels  16.5 us (16%)
  other arithmetic  3.74 us (4%)
    ppermute x32, starting transfers between devices, swap(): lax.ppermute(x, axis, [(i, i ^ xor) for i in range(lax.axis_size(axis))])  31 us
    ppermute x32, waiting for transfers between devices, swap(): lax.ppermute(x, axis, [(i, i ^ xor) for i in range(lax.axis_size(axis))])  26.3 us
    unnamed x64, local copies, waits for them, and re-layouts  20.1 us
    pallas_call x1, Pallas kernels, output(): pl.pallas_call(lambda at, parity, column, *refs: output_kernel(len(shards...  5.06 us
    pallas_call x1, Pallas kernels, attend(): pl.pallas_call(attend_kernel, out_shape=out, grid_spec=pltpu.PrefetchScal...  3.38 us
    pallas_call x1, Pallas kernels, project(): pl.pallas_call(functools.partial(project_kernel, count), out_shape=(out,...  2.88 us
    pallas_call x1, Pallas kernels, finish(): pl.pallas_call(functools.partial(finish_kernel, count, steps), out_shape=...  2.32 us
  transfers between devices with their start and end apart: 32, of which 10 were waited for; matrix products, arithmetic and copies ran while one was open for 8% of the time, Pallas kernels for 11%

profile of v1, /device:TPU:0, one launch (start us, length us, event | category | flops | bytes accessed | tf_op | source)
XLA Modules:
  0.0 100.8 jit_solution(4963511558495731076)
XLA Ops:
  1.7 1.7 %copy-done.2 = bf16[256,5120]{1,0:T(8,128)(2,1)S(1)} copy-done((bf16[256,5120]{1,0:T(8,128)(2,1)S(1)}, bf16[256,5120]{1,0:T(8,128)(2,1)}, u32[]{:S(2)}) %copy-start.2) | copy-done | bytes 2621464
  3.4 1.3 %copy-done.6 = bf16[2,64,5120]{2,1,0:T(8,128)(2,1)S(1)} copy-done((bf16[2,64,5120]{2,1,0:T(8,128)(2,1)S(1)}, bf16[2,64,5120]{2,1,0:T(8,128)(2,1)}, u32[]{:S(2)}) %copy-start.6) | copy-done | bytes 1310744
  4.7 1.0 copy-done.7
  5.7 0.9 copy-done.17
  7.6 2.9 %collective-permute-start = (bf16[192,640]{1,0:T(8,128)(2,1)S(1)}, bf16[192,640]{1,0:T(8,128)(2,1)}, u32[]{:S(2)}, u32[]{:S(2)}) collective-permute-start(bf16[192,640]{1,0:T(8,128)(2,1)S(1)} %get-tuple-element.19.refs_0_), channel_id=1, source_target_pairs={{0,8},{8,0},{16,24},{24,16},{1,9},{9,1},{17,25},{25,17},{2,10},{10... | collective-permute-start | bytes 737288 | tf_op jit(solution)/shard_map/ppermute | solution.py:19
  10.6 1.5 %collective-permute-start.2 = (bf16[192,640]{1,0:T(8,128)(2,1)S(1)}, bf16[192,640]{1,0:T(8,128)(2,1)}, u32[]{:S(2)}, u32[]{:S(2)}) collective-permute-start(bf16[192,640]{1,0:T(8,128)(2,1)S(1)} %get-tuple-element.19.refs_0_), channel_id=1, source_target_pairs={{0,16},{8,24},{16,0},{24,8},{1,17},{9,25},{17,1},{25,9},{2,18},{10... | collective-permute-start | bytes 737288 | tf_op jit(solution)/shard_map/ppermute | solution.py:19
  12.3 0.9 fresh_o.1
  14.5 2.9 %collective-permute-start.21 = (bf16[160,256]{1,0:T(8,128)(2,1)}, bf16[160,256]{1,0:T(8,128)(2,1)S(1)}, u32[]{:S(2)}, u32[]{:S(2)}) collective-permute-start(bf16[160,256]{1,0:T(8,128)(2,1)} %get-tuple-element.28), channel_id=1, source_target_pairs={{0,24},{8,16},{16,8},{24,0},{1,25},{9,17},{17,9},{25,1},{2,26},{10... | collective-permute-start | bytes 245768 | tf_op jit(solution)/shard_map/ppermute | solution.py:19
  17.4 1.8 %collective-permute-done.19.refs_1_ = bf16[160,256]{1,0:T(8,128)(2,1)S(1)} collective-permute-done((bf16[160,256]{1,0:T(8,128)(2,1)}, bf16[160,256]{1,0:T(8,128)(2,1)S(1)}, u32[]{:S(2)}, u32[]{:S(2)}) %collective-permute-start.19) | collective-permute-done | bytes 81952 | tf_op jit(solution)/shard_map/ppermute | solution.py:19
  19.2 1.7 %collective-permute-start.1 = (bf16[192,640]{1,0:T(8,128)(2,1)}, bf16[192,640]{1,0:T(8,128)(2,1)S(1)}, u32[]{:S(2)}, u32[]{:S(2)}) collective-permute-start(bf16[192,640]{1,0:T(8,128)(2,1)} %copy-done.11), channel_id=1, source_target_pairs={{0,8},{8,0},{16,24},{24,16},{1,9},{9,1},{17,25},{25,17},{2,10},{10... | collective-permute-start | bytes 737288 | tf_op jit(solution)/shard_map/ppermute | solution.py:19
  21.5 0.9 copy-done.21
  22.5 1.7 %collective-permute-start.22 = (bf16[160,256]{1,0:T(8,128)(2,1)S(1)}, bf16[160,256]{1,0:T(8,128)(2,1)}, u32[]{:S(2)}, u32[]{:S(2)}) collective-permute-start(bf16[160,256]{1,0:T(8,128)(2,1)S(1)} %get-tuple-element.30), channel_id=1, source_target_pairs={{0,2},{2,0},{4,6},{6,4},{1,3},{3,1},{5,7},{7,5},{8,10},{10,8},{12,... | collective-permute-start | bytes 245768 | tf_op jit(solution)/shard_map/ppermute | solution.py:19
  24.2 2.6 %collective-permute-start.23 = (bf16[160,256]{1,0:T(8,128)(2,1)S(1)}, bf16[160,256]{1,0:T(8,128)(2,1)S(1)}, u32[]{:S(2)}, u32[]{:S(2)}) collective-permute-start(bf16[160,256]{1,0:T(8,128)(2,1)S(1)} %get-tuple-element.31), channel_id=1, source_target_pairs={{0,4},{2,6},{4,0},{6,2},{1,5},{3,7},{5,1},{7,3},{8,12},{10,14},{12... | collective-permute-start | bytes 245768 | tf_op jit(solution)/shard_map/ppermute | solution.py:19
  27.5 1.1 %collective-permute-start.3 = (bf16[192,640]{1,0:T(8,128)(2,1)}, bf16[192,640]{1,0:T(8,128)(2,1)S(1)}, u32[]{:S(2)}, u32[]{:S(2)}) collective-permute-start(bf16[192,640]{1,0:T(8,128)(2,1)} %copy-done.11), channel_id=1, source_target_pairs={{0,16},{8,24},{16,0},{24,8},{1,17},{9,25},{17,1},{25,9},{2,18},{10... | collective-permute-start | bytes 737288 | tf_op jit(solution)/shard_map/ppermute | solution.py:19
  28.7 1.7 %collective-permute-done.23 = bf16[160,256]{1,0:T(8,128)(2,1)S(1)} collective-permute-done((bf16[160,256]{1,0:T(8,128)(2,1)S(1)}, bf16[160,256]{1,0:T(8,128)(2,1)S(1)}, u32[]{:S(2)}, u32[]{:S(2)}) %collective-permute-start.23) | collective-permute-done | bytes 81952 | tf_op jit(solution)/shard_map/ppermute | solution.py:19
  30.4 1.9 %collective-permute-start.24 = (bf16[160,256]{1,0:T(8,128)(2,1)S(1)}, bf16[160,256]{1,0:T(8,128)(2,1)S(1)}, u32[]{:S(2)}, u32[]{:S(2)}) collective-permute-start(bf16[160,256]{1,0:T(8,128)(2,1)S(1)} %get-tuple-element.32), channel_id=1, source_target_pairs={{0,6},{2,4},{4,2},{6,0},{1,7},{3,5},{5,3},{7,1},{8,14},{10,12},{12... | collective-permute-start | bytes 245768 | tf_op jit(solution)/shard_map/ppermute | solution.py:19
  32.3 1.3 %fusion = (f32[256,64]{1,0:T(8,128)}, f32[256,64]{1,0:T(8,128)}, f32[256,64]{1,0:T(8,128)}) fusion(f32[64]{0:T(128)S(1)} %multiply_power_fusion, f32[256]{0:T(256)S(1)} %add_bitcast_fusion), kind=kLoop, calls=%fused_computation.7 | loop fusion | flops 32768 | bytes 197888 | tf_op jit(solution)/shard_map/neg | solution.py:469
  33.6 3.1 %collective-permute-done.24 = bf16[160,256]{1,0:T(8,128)(2,1)S(1)} collective-permute-done((bf16[160,256]{1,0:T(8,128)(2,1)S(1)}, bf16[160,256]{1,0:T(8,128)(2,1)S(1)}, u32[]{:S(2)}, u32[]{:S(2)}) %collective-permute-start.24) | collective-permute-done | bytes 81952 | tf_op jit(solution)/shard_map/ppermute | solution.py:19
  37.1 1.3 %dynamic-slice_bitcast_fusion = (bf16[1,64,32,128]{3,2,1,0:T(8,128)(2,1)S(1)}, bf16[1,64,32,128]{3,2,1,0:T(8,128)(2,1)S(1)}) fusion(bf16[128,1,32,128]{3,2,1,0:T(8,128)(2,1)} %param.30, s32[]{:T(128)S(6)} %select_n.15, bf16[128,1,32,128]{3,2,1,0:T(8,128)(2,1)} %param.29), kind=kLoop, calls=%fused_computation.1 | loop fusion | bytes 2097156 | tf_op jit(solution)/shard_map/stack | solution.py:452
  38.6 1.9 %collective-permute-start.10 = (bf16[192,640]{1,0:T(8,128)(2,1)}, bf16[192,640]{1,0:T(8,128)(2,1)}, u32[]{:S(2)}, u32[]{:S(2)}) collective-permute-start(bf16[192,640]{1,0:T(8,128)(2,1)} %collective-permute-done.refs_2_), channel_id=1, source_target_pairs={{0,16},{8,24},{16,0},{24,8},{1,17},{9,25},{17,1},{25,9},{2,18},{10... | collective-permute-start | bytes 737288 | tf_op jit(solution)/shard_map/ppermute | solution.py:19
  40.7 1.1 %pad_maximum_fusion = bf16[2,64,32,128]{3,2,1,0:T(8,128)(2,1)} fusion(bf16[1,64,32,128]{3,2,1,0:T(8,128)(2,1)S(1)} %get-tuple-element.40, bf16[1,64,32,128]{3,2,1,0:T(8,128)(2,1)S(1)} %get-tuple-element.41), kind=kLoop, calls=%fused_computation | loop fusion | flops 524288 | bytes 2097152 | tf_op jit(solution)/shard_map/stack | solution.py:452
  41.8 1.7 %copy-done = bf16[2,128,5120]{2,1,0:T(8,128)(2,1)S(1)} copy-done((bf16[2,128,5120]{2,1,0:T(8,128)(2,1)S(1)}, bf16[2,128,5120]{2,1,0:T(8,128)(2,1)}, u32[]{:S(2)}) %copy-start) | copy-done | bytes 2621464
  44.3 1.5 %norm.1.normed = bf16[256,5120]{1,0:T(8,128)(2,1)S(1)} custom-call(bf16[2,128,5120]{2,1,0:T(8,128)(2,1)S(1)} %copy-done, f32[1,5120]{1,0:T(1,128)S(1)} %bitcast.30), custom_call_target="tpu_custom_call" | custom-call | tf_op jit(solution)/shard_map/norm/pallas_call | solution.py:122
  46.8 0.9 constant_dynamic-update-slice_fusion.2
  48.0 0.9 constant_dynamic-update-slice_fusion.1
  48.9 5.6 %collective-permute-done.11.refs_1_ = bf16[192,640]{1,0:T(8,128)(2,1)S(1)} collective-permute-done((bf16[192,640]{1,0:T(8,128)(2,1)}, bf16[192,640]{1,0:T(8,128)(2,1)S(1)}, u32[]{:S(2)}, u32[]{:S(2)}) %collective-permute-start.11) | collective-permute-done | bytes 245792 | tf_op jit(solution)/shard_map/ppermute | solution.py:19
  54.5 0.9 constant_dynamic-update-slice_fusion.refs_5_
  55.7 1.1 %collective-permute-start.26 = (bf16[640,256]{1,0:T(8,128)(2,1)S(1)}, bf16[640,256]{1,0:T(8,128)(2,1)}, u32[]{:S(2)}, u32[]{:S(2)}) collective-permute-start(bf16[640,256]{1,0:T(8,128)(2,1)S(1)} %constant_dynamic-update-slice_fusion.refs_5_), channel_id=1, source_target_pairs={{0,16},{8,24},{16,0},{24,8},{1,17},{9,25},{17,1},{25,9},{2,18},{10... | collective-permute-start | bytes 983048 | tf_op jit(solution)/shard_map/ppermute | solution.py:19
  56.8 1.2 %pad_maximum_fusion.1 = (f32[256,128]{1,0:T(8,128)S(1)}, f32[256,128]{1,0:T(8,128)S(1)}) fusion(f32[256,64]{1,0:T(8,128)} %get-tuple-element.37, f32[256,64]{1,0:T(8,128)} %get-tuple-element.36, f32[256,64]{1,0:T(8,128)} %get-tuple-element.35), kind=kLoop, calls=%fused_computation.5 | loop fusion | flops 65536 | bytes 458752 | tf_op jit(solution)/shard_map/concatenate | solution.py:468
  58.0 2.2 %collective-permute-start.27 = (bf16[640,256]{1,0:T(8,128)(2,1)S(1)}, bf16[640,256]{1,0:T(8,128)(2,1)}, u32[]{:S(2)}, u32[]{:S(2)}) collective-permute-start(bf16[640,256]{1,0:T(8,128)(2,1)S(1)} %constant_dynamic-update-slice_fusion.refs_5_), channel_id=1, source_target_pairs={{0,24},{8,16},{16,8},{24,0},{1,25},{9,17},{17,9},{25,1},{2,26},{10... | collective-permute-start | bytes 983048 | tf_op jit(solution)/shard_map/ppermute | solution.py:19
  60.3 0.9 copy-done.10
  61.3 0.9 copy-done.14
  62.2 0.9 copy-done.16
  63.2 2.9 %project.1 = (f32[256,192]{1,0:T(8,128)S(1)}, f32[256,192]{1,0:T(8,128)S(1)}) custom-call(s32[6]{0:T(128)S(1)} %stack.84.at, bf16[256,5120]{1,0:T(8,128)(2,1)S(1)} %norm.1.normed, bf16[192,640]{1,0:T(8,128)(2,1)S(1)} %copy-done.10, bf16[192,640]{1,0:T(8,128)(2,1)S(1)} %copy-done.12, bf16[192,640]{1,0:T(8,128)(2,1)} %collective-permute-done.refs_2_, ...), custom_call_target="tpu_custom_call" | custom-call | tf_op jit(solution)/shard_map/project/pallas_call | solution.py:153
  66.1 2.3 %finish.1 = (bf16[2,64,512]{2,1,0:T(8,128)(2,1)S(1)}, bf16[2,64,512]{2,1,0:T(8,128)(2,1)}) custom-call(s32[2]{0:T(128)S(1)} %pad_add_fusion.at, s32[1]{0:T(128)} %bitcast.8.parity, bf16[256,5120]{1,0:T(8,128)(2,1)S(1)} %norm.1.normed, f32[256,192]{1,0:T(8,128)S(1)} %get-tuple-element.21.total0, f32[256,192]{1,0:T(8,128)S(1)} %get-tuple-element.22.total1, ...), custom_call_target="tpu_custom_call" | custom-call | tf_op jit(solution)/shard_map/finish/pallas_call | solution.py:204
  68.4 1.7 %collective-permute-start.14 = (bf16[2,64,512]{2,1,0:T(8,128)(2,1)}, bf16[2,64,512]{2,1,0:T(8,128)(2,1)S(1)}, u32[]{:S(2)}, u32[]{:S(2)}) collective-permute-start(bf16[2,64,512]{2,1,0:T(8,128)(2,1)} %get-tuple-element.24), channel_id=1, source_target_pairs={{0,2},{2,0},{4,6},{6,4},{1,3},{3,1},{5,7},{7,5},{8,10},{10,8},{12,... | collective-permute-start | bytes 393224 | tf_op jit(solution)/shard_map/ppermute | solution.py:19
  70.5 2.3 %collective-permute-done.26.refs_7_ = bf16[640,256]{1,0:T(8,128)(2,1)} collective-permute-done((bf16[640,256]{1,0:T(8,128)(2,1)S(1)}, bf16[640,256]{1,0:T(8,128)(2,1)}, u32[]{:S(2)}, u32[]{:S(2)}) %collective-permute-start.26) | collective-permute-done | bytes 327712 | tf_op jit(solution)/shard_map/ppermute | solution.py:19
  73.4 1.0 %collective-permute-done.14.other = bf16[2,64,512]{2,1,0:T(8,128)(2,1)S(1)} collective-permute-done((bf16[2,64,512]{2,1,0:T(8,128)(2,1)}, bf16[2,64,512]{2,1,0:T(8,128)(2,1)S(1)}, u32[]{:S(2)}, u32[]{:S(2)}) %collective-permute-start.14) | collective-permute-done | bytes 131104 | tf_op jit(solution)/shard_map/ppermute | solution.py:19
  75.1 1.2 %copy-done.4 = bf16[128,1,32,128]{3,2,1,0:T(8,128)(2,1)S(1)} copy-done((bf16[128,1,32,128]{3,2,1,0:T(8,128)(2,1)S(1)}, bf16[128,1,32,128]{3,2,1,0:T(8,128)(2,1)}, u32[]{:S(2)}) %copy-start.4) | copy-done | bytes 1048600
  76.3 1.2 %copy-done.5 = bf16[128,1,32,128]{3,2,1,0:T(8,128)(2,1)S(1)} copy-done((bf16[128,1,32,128]{3,2,1,0:T(8,128)(2,1)S(1)}, bf16[128,1,32,128]{3,2,1,0:T(8,128)(2,1)}, u32[]{:S(2)}) %copy-start.5) | copy-done | bytes 1048600
  77.5 0.9 copy-done.19
  78.4 3.4 %attend.1.refs_0_ = bf16[2,64,512]{2,1,0:T(8,128)(2,1)S(1)} custom-call(s32[1]{0:T(128)} %bitcast.8.parity, bf16[2,64,512]{2,1,0:T(8,128)(2,1)S(1)} %get-tuple-element.23.own, bf16[2,64,512]{2,1,0:T(8,128)(2,1)S(1)} %copy-done.19, f32[256,128]{1,0:T(8,128)S(1)} %get-tuple-element.38.cosine, f32[256,128]{1,0:T(8,128)S(1)} %get-tuple-element.39.sine, ...), custom_call_target="tpu_custom_call" | custom-call | tf_op jit(solution)/shard_map/attend/pallas_call | solution.py:325
  81.8 1.0 collective-permute-start.16
  82.8 1.1 %collective-permute-start.17 = (bf16[2,64,512]{2,1,0:T(8,128)(2,1)S(1)}, bf16[2,64,512]{2,1,0:T(8,128)(2,1)S(1)}, u32[]{:S(2)}, u32[]{:S(2)}) collective-permute-start(bf16[2,64,512]{2,1,0:T(8,128)(2,1)S(1)} %attend.1.refs_0_), channel_id=1, source_target_pairs={{0,4},{2,6},{4,0},{6,2},{1,5},{3,7},{5,1},{7,3},{8,12},{10,14},{12... | collective-permute-start | bytes 393224 | tf_op jit(solution)/shard_map/ppermute | solution.py:19
  83.9 2.3 %collective-permute-start.18 = (bf16[2,64,512]{2,1,0:T(8,128)(2,1)S(1)}, bf16[2,64,512]{2,1,0:T(8,128)(2,1)S(1)}, u32[]{:S(2)}, u32[]{:S(2)}) collective-permute-start(bf16[2,64,512]{2,1,0:T(8,128)(2,1)S(1)} %attend.1.refs_0_), channel_id=1, source_target_pairs={{0,6},{2,4},{4,2},{6,0},{1,7},{3,5},{5,3},{7,1},{8,14},{10,12},{12... | collective-permute-start | bytes 393224 | tf_op jit(solution)/shard_map/ppermute | solution.py:19
  86.4 3.1 %collective-permute-done.16.refs_1_ = bf16[2,64,512]{2,1,0:T(8,128)(2,1)S(1)} collective-permute-done((bf16[2,64,512]{2,1,0:T(8,128)(2,1)S(1)}, bf16[2,64,512]{2,1,0:T(8,128)(2,1)S(1)}, u32[]{:S(2)}, u32[]{:S(2)}) %collective-permute-start.16) | collective-permute-done | bytes 131104 | tf_op jit(solution)/shard_map/ppermute | solution.py:19
  89.5 6.2 %collective-permute-done.17.refs_2_ = bf16[2,64,512]{2,1,0:T(8,128)(2,1)S(1)} collective-permute-done((bf16[2,64,512]{2,1,0:T(8,128)(2,1)S(1)}, bf16[2,64,512]{2,1,0:T(8,128)(2,1)S(1)}, u32[]{:S(2)}, u32[]{:S(2)}) %collective-permute-start.17) | collective-permute-done | bytes 131104 | tf_op jit(solution)/shard_map/ppermute | solution.py:19
  95.7 5.1 %output.1 = bf16[2,128,1280]{2,1,0:T(8,128)(2,1)} custom-call(s32[8]{0:T(128)S(1)} %stack.74.at, s32[1]{0:T(128)} %bitcast.8.parity, s32[1]{0:T(128)} %bitcast.9.column, bf16[2,64,512]{2,1,0:T(8,128)(2,1)S(1)} %attend.1.refs_0_, bf16[2,64,512]{2,1,0:T(8,128)(2,1)S(1)} %collective-permute-done.16.refs_1_, ...), custom_call_target="tpu_custom_call" | custom-call | tf_op jit(solution)/shard_map/output/pallas_call | solution.py:399
  (111 shorter events, 10.7 us)
Async XLA Ops:
  0.0 12.1 %copy-start.26 = (s32[640,8]{0,1:T(8,128)S(1)}, s32[640,8]{0,1:T(8,128)}, u32[]{:S(2)}) copy-start(s32[640,8]{0,1:T(8,128)} %param.28) | copy-start | bytes 61444
  1.7 1.7 %copy-start.2 = (bf16[256,5120]{1,0:T(8,128)(2,1)S(1)}, bf16[256,5120]{1,0:T(8,128)(2,1)}, u32[]{:S(2)}) copy-start(bf16[256,5120]{1,0:T(8,128)(2,1)} %qw.1) | copy-start | bytes 7864324
  3.4 1.3 %copy-start.6 = (bf16[2,64,5120]{2,1,0:T(8,128)(2,1)S(1)}, bf16[2,64,5120]{2,1,0:T(8,128)(2,1)}, u32[]{:S(2)}) copy-start(bf16[2,64,5120]{2,1,0:T(8,128)(2,1)} %kvw.1) | copy-start | bytes 3932164
  6.6 5.7 %copy-start.3 = (bf16[5120,256]{1,0:T(8,128)(2,1)S(1)}, bf16[5120,256]{1,0:T(8,128)(2,1)}, u32[]{:S(2)}) copy-start(bf16[5120,256]{1,0:T(8,128)(2,1)} %ow.1) | copy-start | bytes 7864324
  6.6 5.7 %copy-start.8 = (bf16[640,256]{1,0:T(8,128)(2,1)S(1)}, bf16[640,256]{1,0:T(8,128)(2,1)}, u32[]{:S(2)}) copy-start(bf16[640,256]{1,0:T(8,128)(2,1)} %od.1) | copy-start | bytes 983044
  7.6 30.8 %copy-start.9 = (bf16[192,640]{1,0:T(8,128)(2,1)}, bf16[192,640]{1,0:T(8,128)(2,1)S(1)}, u32[]{:S(2)}) copy-start(bf16[192,640]{1,0:T(8,128)(2,1)S(1)} %get-tuple-element.19.refs_0_) | copy-start | bytes 737284
  7.6 9.7 %copy-start.28 = (s32[128]{0:T(128)S(1)}, s32[128]{0:T(128)}, u32[]{:S(2)}) copy-start(s32[128]{0:T(128)} %param.31) | copy-start | bytes 1540
  7.6 29.0 %collective-permute-start = (bf16[192,640]{1,0:T(8,128)(2,1)S(1)}, bf16[192,640]{1,0:T(8,128)(2,1)}, u32[]{:S(2)}, u32[]{:S(2)}) collective-permute-start(bf16[192,640]{1,0:T(8,128)(2,1)S(1)} %get-tuple-element.19.refs_0_), channel_id=1, source_target_pairs={{0,8},{8,0},{16,24},{24,16},{1,9},{9,1},{17,25},{25,17},{2,10},{10... | collective-permute-start | bytes 737288 | tf_op jit(solution)/shard_map/ppermute | solution.py:19
  10.6 28.0 %collective-permute-start.2 = (bf16[192,640]{1,0:T(8,128)(2,1)S(1)}, bf16[192,640]{1,0:T(8,128)(2,1)}, u32[]{:S(2)}, u32[]{:S(2)}) collective-permute-start(bf16[192,640]{1,0:T(8,128)(2,1)S(1)} %get-tuple-element.19.refs_0_), channel_id=1, source_target_pairs={{0,16},{8,24},{16,0},{24,8},{1,17},{9,25},{17,1},{25,9},{2,18},{10... | collective-permute-start | bytes 737288 | tf_op jit(solution)/shard_map/ppermute | solution.py:19
  13.8 27.9 %copy-start.27 = (bf16[256]{0:T(256)(128)(2,1)S(1)}, bf16[256]{0:T(256)(128)(2,1)}, u32[]{:S(2)}) copy-start(bf16[256]{0:T(256)(128)(2,1)} %param.19) | copy-start | bytes 1540
  13.8 5.3 %collective-permute-start.19 = (bf16[160,256]{1,0:T(8,128)(2,1)}, bf16[160,256]{1,0:T(8,128)(2,1)S(1)}, u32[]{:S(2)}, u32[]{:S(2)}) collective-permute-start(bf16[160,256]{1,0:T(8,128)(2,1)} %get-tuple-element.26), channel_id=1, source_target_pairs={{0,8},{8,0},{16,24},{24,16},{1,9},{9,1},{17,25},{25,17},{2,10},{10... | collective-permute-start | bytes 245768 | tf_op jit(solution)/shard_map/ppermute | solution.py:19
  14.4 7.1 %collective-permute-start.20 = (bf16[160,256]{1,0:T(8,128)(2,1)}, bf16[160,256]{1,0:T(8,128)(2,1)S(1)}, u32[]{:S(2)}, u32[]{:S(2)}) collective-permute-start(bf16[160,256]{1,0:T(8,128)(2,1)} %get-tuple-element.27), channel_id=1, source_target_pairs={{0,16},{8,24},{16,0},{24,8},{1,17},{9,25},{17,1},{25,9},{2,18},{10... | collective-permute-start | bytes 245768 | tf_op jit(solution)/shard_map/ppermute | solution.py:19
  14.5 7.0 %collective-permute-start.21 = (bf16[160,256]{1,0:T(8,128)(2,1)}, bf16[160,256]{1,0:T(8,128)(2,1)S(1)}, u32[]{:S(2)}, u32[]{:S(2)}) collective-permute-start(bf16[160,256]{1,0:T(8,128)(2,1)} %get-tuple-element.28), channel_id=1, source_target_pairs={{0,24},{8,16},{16,8},{24,0},{1,25},{9,17},{17,9},{25,1},{2,26},{10... | collective-permute-start | bytes 245768 | tf_op jit(solution)/shard_map/ppermute | solution.py:19
  19.2 19.3 %collective-permute-start.1 = (bf16[192,640]{1,0:T(8,128)(2,1)}, bf16[192,640]{1,0:T(8,128)(2,1)S(1)}, u32[]{:S(2)}, u32[]{:S(2)}) collective-permute-start(bf16[192,640]{1,0:T(8,128)(2,1)} %copy-done.11), channel_id=1, source_target_pairs={{0,8},{8,0},{16,24},{24,16},{1,9},{9,1},{17,25},{25,17},{2,10},{10... | collective-permute-start | bytes 737288 | tf_op jit(solution)/shard_map/ppermute | solution.py:19
  22.5 5.0 %collective-permute-start.22 = (bf16[160,256]{1,0:T(8,128)(2,1)S(1)}, bf16[160,256]{1,0:T(8,128)(2,1)}, u32[]{:S(2)}, u32[]{:S(2)}) collective-permute-start(bf16[160,256]{1,0:T(8,128)(2,1)S(1)} %get-tuple-element.30), channel_id=1, source_target_pairs={{0,2},{2,0},{4,6},{6,4},{1,3},{3,1},{5,7},{7,5},{8,10},{10,8},{12,... | collective-permute-start | bytes 245768 | tf_op jit(solution)/shard_map/ppermute | solution.py:19
  24.2 6.2 %collective-permute-start.23 = (bf16[160,256]{1,0:T(8,128)(2,1)S(1)}, bf16[160,256]{1,0:T(8,128)(2,1)S(1)}, u32[]{:S(2)}, u32[]{:S(2)}) collective-permute-start(bf16[160,256]{1,0:T(8,128)(2,1)S(1)} %get-tuple-element.31), channel_id=1, source_target_pairs={{0,4},{2,6},{4,0},{6,2},{1,5},{3,7},{5,1},{7,3},{8,12},{10,14},{12... | collective-permute-start | bytes 245768 | tf_op jit(solution)/shard_map/ppermute | solution.py:19
  27.5 13.0 %collective-permute-start.3 = (bf16[192,640]{1,0:T(8,128)(2,1)}, bf16[192,640]{1,0:T(8,128)(2,1)S(1)}, u32[]{:S(2)}, u32[]{:S(2)}) collective-permute-start(bf16[192,640]{1,0:T(8,128)(2,1)} %copy-done.11), channel_id=1, source_target_pairs={{0,16},{8,24},{16,0},{24,8},{1,17},{9,25},{17,1},{25,9},{2,18},{10... | collective-permute-start | bytes 737288 | tf_op jit(solution)/shard_map/ppermute | solution.py:19
  30.4 6.3 %copy-start.24 = (bf16[160,256]{1,0:T(8,128)(2,1)}, bf16[160,256]{1,0:T(8,128)(2,1)S(1)}, u32[]{:S(2)}) copy-start(bf16[160,256]{1,0:T(8,128)(2,1)S(1)} %collective-permute-done.23) | copy-start | bytes 245764
  30.4 6.2 %collective-permute-start.24 = (bf16[160,256]{1,0:T(8,128)(2,1)S(1)}, bf16[160,256]{1,0:T(8,128)(2,1)S(1)}, u32[]{:S(2)}, u32[]{:S(2)}) collective-permute-start(bf16[160,256]{1,0:T(8,128)(2,1)S(1)} %get-tuple-element.32), channel_id=1, source_target_pairs={{0,6},{2,4},{4,2},{6,0},{1,7},{3,5},{5,3},{7,1},{8,14},{10,12},{12... | collective-permute-start | bytes 245768 | tf_op jit(solution)/shard_map/ppermute | solution.py:19
  36.6 5.2 %copy-start.25 = (bf16[160,256]{1,0:T(8,128)(2,1)}, bf16[160,256]{1,0:T(8,128)(2,1)S(1)}, u32[]{:S(2)}) copy-start(bf16[160,256]{1,0:T(8,128)(2,1)S(1)} %collective-permute-done.24) | copy-start | bytes 245764
  36.6 9.3 %collective-permute-start.4 = (bf16[192,640]{1,0:T(8,128)(2,1)S(1)}, bf16[192,640]{1,0:T(8,128)(2,1)}, u32[]{:S(2)}, u32[]{:S(2)}) collective-permute-start(bf16[192,640]{1,0:T(8,128)(2,1)S(1)} %get-tuple-element.19.refs_0_), channel_id=1, source_target_pairs={{0,1},{1,0},{2,3},{3,2},{4,5},{5,4},{6,7},{7,6},{8,9},{9,8},{10,11... | collective-permute-start | bytes 737288 | tf_op jit(solution)/shard_map/ppermute | solution.py:19
  36.6 9.3 %collective-permute-start.5 = (bf16[192,640]{1,0:T(8,128)(2,1)}, bf16[192,640]{1,0:T(8,128)(2,1)}, u32[]{:S(2)}, u32[]{:S(2)}) collective-permute-start(bf16[192,640]{1,0:T(8,128)(2,1)} %copy-done.11), channel_id=1, source_target_pairs={{0,1},{1,0},{2,3},{3,2},{4,5},{5,4},{6,7},{7,6},{8,9},{9,8},{10,11... | collective-permute-start | bytes 737288 | tf_op jit(solution)/shard_map/ppermute | solution.py:19
  38.4 7.4 %copy-start.13 = (bf16[192,640]{1,0:T(8,128)(2,1)}, bf16[192,640]{1,0:T(8,128)(2,1)S(1)}, u32[]{:S(2)}) copy-start(bf16[192,640]{1,0:T(8,128)(2,1)S(1)} %collective-permute-done.1.refs_3_) | copy-start | bytes 737284
  38.4 7.7 %collective-permute-start.6 = (bf16[192,640]{1,0:T(8,128)(2,1)}, bf16[192,640]{1,0:T(8,128)(2,1)}, u32[]{:S(2)}, u32[]{:S(2)}) collective-permute-start(bf16[192,640]{1,0:T(8,128)(2,1)} %collective-permute-done.refs_2_), channel_id=1, source_target_pairs={{0,1},{1,0},{2,3},{3,2},{4,5},{5,4},{6,7},{7,6},{8,9},{9,8},{10,11... | collective-permute-start | bytes 737288 | tf_op jit(solution)/shard_map/ppermute | solution.py:19
  38.6 9.1 %collective-permute-start.10 = (bf16[192,640]{1,0:T(8,128)(2,1)}, bf16[192,640]{1,0:T(8,128)(2,1)}, u32[]{:S(2)}, u32[]{:S(2)}) collective-permute-start(bf16[192,640]{1,0:T(8,128)(2,1)} %collective-permute-done.refs_2_), channel_id=1, source_target_pairs={{0,16},{8,24},{16,0},{24,8},{1,17},{9,25},{17,1},{25,9},{2,18},{10... | collective-permute-start | bytes 737288 | tf_op jit(solution)/shard_map/ppermute | solution.py:19
  40.5 1.3 %copy-start.15 = (bf16[192,640]{1,0:T(8,128)(2,1)}, bf16[192,640]{1,0:T(8,128)(2,1)S(1)}, u32[]{:S(2)}) copy-start(bf16[192,640]{1,0:T(8,128)(2,1)S(1)} %collective-permute-done.3.refs_5_) | copy-start | bytes 737284
  40.5 6.0 %collective-permute-start.7 = (bf16[192,640]{1,0:T(8,128)(2,1)S(1)}, bf16[192,640]{1,0:T(8,128)(2,1)}, u32[]{:S(2)}, u32[]{:S(2)}) collective-permute-start(bf16[192,640]{1,0:T(8,128)(2,1)S(1)} %collective-permute-done.1.refs_3_), channel_id=1, source_target_pairs={{0,1},{1,0},{2,3},{3,2},{4,5},{5,4},{6,7},{7,6},{8,9},{9,8},{10,11... | collective-permute-start | bytes 737288 | tf_op jit(solution)/shard_map/ppermute | solution.py:19
  41.8 1.7 %copy-start = (bf16[2,128,5120]{2,1,0:T(8,128)(2,1)S(1)}, bf16[2,128,5120]{2,1,0:T(8,128)(2,1)}, u32[]{:S(2)}) copy-start(bf16[2,128,5120]{2,1,0:T(8,128)(2,1)} %refs_4_.1) | copy-start | bytes 7864324
  44.3 16.0 %copy-start.12 = (bf16[192,640]{1,0:T(8,128)(2,1)S(1)}, bf16[192,640]{1,0:T(8,128)(2,1)}, u32[]{:S(2)}) copy-start(bf16[192,640]{1,0:T(8,128)(2,1)} %copy-done.11) | copy-start | bytes 737284
  45.9 29.1 %collective-permute-start.15 = (bf16[2,64,32,128]{3,2,1,0:T(8,128)(2,1)}, bf16[2,64,32,128]{3,2,1,0:T(8,128)(2,1)}, u32[]{:S(2)}, u32[]{:S(2)}) collective-permute-start(bf16[2,64,32,128]{3,2,1,0:T(8,128)(2,1)} %pad_maximum_fusion), channel_id=1, source_target_pairs={{0,2},{2,0},{4,6},{6,4},{1,3},{3,1},{5,7},{7,5},{8,10},{10,8},{12,... | collective-permute-start | bytes 3145736 | tf_op jit(solution)/shard_map/ppermute | solution.py:19
  46.0 8.5 %collective-permute-start.11 = (bf16[192,640]{1,0:T(8,128)(2,1)}, bf16[192,640]{1,0:T(8,128)(2,1)S(1)}, u32[]{:S(2)}, u32[]{:S(2)}) collective-permute-start(bf16[192,640]{1,0:T(8,128)(2,1)} %copy-done.15), channel_id=1, source_target_pairs={{0,8},{8,0},{16,24},{24,16},{1,9},{9,1},{17,25},{25,17},{2,10},{10... | collective-permute-start | bytes 737288 | tf_op jit(solution)/shard_map/ppermute | solution.py:19
  46.2 9.5 %collective-permute-start.9 = (bf16[192,640]{1,0:T(8,128)(2,1)}, bf16[192,640]{1,0:T(8,128)(2,1)S(1)}, u32[]{:S(2)}, u32[]{:S(2)}) collective-permute-start(bf16[192,640]{1,0:T(8,128)(2,1)} %copy-done.15), channel_id=1, source_target_pairs={{0,1},{1,0},{2,3},{3,2},{4,5},{5,4},{6,7},{7,6},{8,9},{9,8},{10,11... | collective-permute-start | bytes 737288 | tf_op jit(solution)/shard_map/ppermute | solution.py:19
  46.5 8.9 %collective-permute-start.8 = (bf16[192,640]{1,0:T(8,128)(2,1)}, bf16[192,640]{1,0:T(8,128)(2,1)S(1)}, u32[]{:S(2)}, u32[]{:S(2)}) collective-permute-start(bf16[192,640]{1,0:T(8,128)(2,1)} %collective-permute-done.2.refs_4_), channel_id=1, source_target_pairs={{0,1},{1,0},{2,3},{3,2},{4,5},{5,4},{6,7},{7,6},{8,9},{9,8},{10,11... | collective-permute-start | bytes 737288 | tf_op jit(solution)/shard_map/ppermute | solution.py:19
  47.7 10.4 %collective-permute-start.12 = (bf16[192,640]{1,0:T(8,128)(2,1)}, bf16[192,640]{1,0:T(8,128)(2,1)S(1)}, u32[]{:S(2)}, u32[]{:S(2)}) collective-permute-start(bf16[192,640]{1,0:T(8,128)(2,1)} %collective-permute-done.10.refs_0_), channel_id=1, source_target_pairs={{0,1},{1,0},{2,3},{3,2},{4,5},{5,4},{6,7},{7,6},{8,9},{9,8},{10,11... | collective-permute-start | bytes 737288 | tf_op jit(solution)/shard_map/ppermute | solution.py:19
  54.5 11.6 %collective-permute-start.13 = (bf16[192,640]{1,0:T(8,128)(2,1)S(1)}, bf16[192,640]{1,0:T(8,128)(2,1)S(1)}, u32[]{:S(2)}, u32[]{:S(2)}) collective-permute-start(bf16[192,640]{1,0:T(8,128)(2,1)S(1)} %collective-permute-done.11.refs_1_), channel_id=1, source_target_pairs={{0,1},{1,0},{2,3},{3,2},{4,5},{5,4},{6,7},{7,6},{8,9},{9,8},{10,11... | collective-permute-start | bytes 737288 | tf_op jit(solution)/shard_map/ppermute | solution.py:19
  55.4 15.1 %collective-permute-start.25 = (bf16[640,256]{1,0:T(8,128)(2,1)S(1)}, bf16[640,256]{1,0:T(8,128)(2,1)}, u32[]{:S(2)}, u32[]{:S(2)}) collective-permute-start(bf16[640,256]{1,0:T(8,128)(2,1)S(1)} %constant_dynamic-update-slice_fusion.refs_5_), channel_id=1, source_target_pairs={{0,8},{8,0},{16,24},{24,16},{1,9},{9,1},{17,25},{25,17},{2,10},{10... | collective-permute-start | bytes 983048 | tf_op jit(solution)/shard_map/ppermute | solution.py:19
  55.7 17.1 %collective-permute-start.26 = (bf16[640,256]{1,0:T(8,128)(2,1)S(1)}, bf16[640,256]{1,0:T(8,128)(2,1)}, u32[]{:S(2)}, u32[]{:S(2)}) collective-permute-start(bf16[640,256]{1,0:T(8,128)(2,1)S(1)} %constant_dynamic-update-slice_fusion.refs_5_), channel_id=1, source_target_pairs={{0,16},{8,24},{16,0},{24,8},{1,17},{9,25},{17,1},{25,9},{2,18},{10... | collective-permute-start | bytes 983048 | tf_op jit(solution)/shard_map/ppermute | solution.py:19
  58.0 14.8 %collective-permute-start.27 = (bf16[640,256]{1,0:T(8,128)(2,1)S(1)}, bf16[640,256]{1,0:T(8,128)(2,1)}, u32[]{:S(2)}, u32[]{:S(2)}) collective-permute-start(bf16[640,256]{1,0:T(8,128)(2,1)S(1)} %constant_dynamic-update-slice_fusion.refs_5_), channel_id=1, source_target_pairs={{0,24},{8,16},{16,8},{24,0},{1,25},{9,17},{17,9},{25,1},{2,26},{10... | collective-permute-start | bytes 983048 | tf_op jit(solution)/shard_map/ppermute | solution.py:19
  63.2 2.9 %copy-start.23 = (bf16[2,64]{1,0:T(2,128)(2,1)S(1)}, bf16[2,64]{1,0:T(2,128)(2,1)}, u32[]{:S(2)}) copy-start(bf16[2,64]{1,0:T(2,128)(2,1)} %kvb.1) | copy-start | bytes 772
  68.4 27.3 %copy-start.1 = (bf16[2,128,5120]{2,1,0:T(8,128)(2,1)S(1)}, bf16[2,128,5120]{2,1,0:T(8,128)(2,1)}, u32[]{:S(2)}) copy-start(bf16[2,128,5120]{2,1,0:T(8,128)(2,1)} %refs_4_.1) | copy-start | bytes 7864324
  68.4 6.0 %collective-permute-start.14 = (bf16[2,64,512]{2,1,0:T(8,128)(2,1)}, bf16[2,64,512]{2,1,0:T(8,128)(2,1)S(1)}, u32[]{:S(2)}, u32[]{:S(2)}) collective-permute-start(bf16[2,64,512]{2,1,0:T(8,128)(2,1)} %get-tuple-element.24), channel_id=1, source_target_pairs={{0,2},{2,0},{4,6},{6,4},{1,3},{3,1},{5,7},{7,5},{8,10},{10,8},{12,... | collective-permute-start | bytes 393224 | tf_op jit(solution)/shard_map/ppermute | solution.py:19
  70.5 12.4 %collective-permute-start.28 = (bf16[640,256]{1,0:T(8,128)(2,1)S(1)}, bf16[640,256]{1,0:T(8,128)(2,1)}, u32[]{:S(2)}, u32[]{:S(2)}) collective-permute-start(bf16[640,256]{1,0:T(8,128)(2,1)S(1)} %constant_dynamic-update-slice_fusion.refs_5_), channel_id=1, source_target_pairs={{0,1},{1,0},{2,3},{3,2},{4,5},{5,4},{6,7},{7,6},{8,9},{9,8},{10,11... | collective-permute-start | bytes 983048 | tf_op jit(solution)/shard_map/ppermute | solution.py:19
  72.8 11.2 %collective-permute-start.29 = (bf16[640,256]{1,0:T(8,128)(2,1)}, bf16[640,256]{1,0:T(8,128)(2,1)}, u32[]{:S(2)}, u32[]{:S(2)}) collective-permute-start(bf16[640,256]{1,0:T(8,128)(2,1)} %collective-permute-done.25.refs_6_), channel_id=1, source_target_pairs={{0,1},{1,0},{2,3},{3,2},{4,5},{5,4},{6,7},{7,6},{8,9},{9,8},{10,11... | collective-permute-start | bytes 983048 | tf_op jit(solution)/shard_map/ppermute | solution.py:19
  72.9 13.5 %collective-permute-start.30 = (bf16[640,256]{1,0:T(8,128)(2,1)}, bf16[640,256]{1,0:T(8,128)(2,1)}, u32[]{:S(2)}, u32[]{:S(2)}) collective-permute-start(bf16[640,256]{1,0:T(8,128)(2,1)} %collective-permute-done.26.refs_7_), channel_id=1, source_target_pairs={{0,1},{1,0},{2,3},{3,2},{4,5},{5,4},{6,7},{7,6},{8,9},{9,8},{10,11... | collective-permute-start | bytes 983048 | tf_op jit(solution)/shard_map/ppermute | solution.py:19
  75.1 11.3 %collective-permute-start.31 = (bf16[640,256]{1,0:T(8,128)(2,1)}, bf16[640,256]{1,0:T(8,128)(2,1)}, u32[]{:S(2)}, u32[]{:S(2)}) collective-permute-start(bf16[640,256]{1,0:T(8,128)(2,1)} %collective-permute-done.27.refs_8_), channel_id=1, source_target_pairs={{0,1},{1,0},{2,3},{3,2},{4,5},{5,4},{6,7},{7,6},{8,9},{9,8},{10,11... | collective-permute-start | bytes 983048 | tf_op jit(solution)/shard_map/ppermute | solution.py:19
  81.8 7.7 %collective-permute-start.16 = (bf16[2,64,512]{2,1,0:T(8,128)(2,1)S(1)}, bf16[2,64,512]{2,1,0:T(8,128)(2,1)S(1)}, u32[]{:S(2)}, u32[]{:S(2)}) collective-permute-start(bf16[2,64,512]{2,1,0:T(8,128)(2,1)S(1)} %attend.1.refs_0_), channel_id=1, source_target_pairs={{0,2},{2,0},{4,6},{6,4},{1,3},{3,1},{5,7},{7,5},{8,10},{10,8},{12,... | collective-permute-start | bytes 393224 | tf_op jit(solution)/shard_map/ppermute | solution.py:19
  82.8 12.9 %collective-permute-start.17 = (bf16[2,64,512]{2,1,0:T(8,128)(2,1)S(1)}, bf16[2,64,512]{2,1,0:T(8,128)(2,1)S(1)}, u32[]{:S(2)}, u32[]{:S(2)}) collective-permute-start(bf16[2,64,512]{2,1,0:T(8,128)(2,1)S(1)} %attend.1.refs_0_), channel_id=1, source_target_pairs={{0,4},{2,6},{4,0},{6,2},{1,5},{3,7},{5,1},{7,3},{8,12},{10,14},{12... | collective-permute-start | bytes 393224 | tf_op jit(solution)/shard_map/ppermute | solution.py:19
  83.9 11.8 %collective-permute-start.18 = (bf16[2,64,512]{2,1,0:T(8,128)(2,1)S(1)}, bf16[2,64,512]{2,1,0:T(8,128)(2,1)S(1)}, u32[]{:S(2)}, u32[]{:S(2)}) collective-permute-start(bf16[2,64,512]{2,1,0:T(8,128)(2,1)S(1)} %attend.1.refs_0_), channel_id=1, source_target_pairs={{0,6},{2,4},{4,2},{6,0},{1,7},{3,5},{5,3},{7,1},{8,14},{10,12},{12... | collective-permute-start | bytes 393224 | tf_op jit(solution)/shard_map/ppermute | solution.py:19
  (13 other events, 11.7 us)

commit v2 on v0

v2 whole, which is shorter than its diff:
```python
import functools
import math

import jax
import jax.numpy as jnp
from jax import lax
from jax.experimental import pallas as pl
from jax.experimental.pallas import tpu as pltpu
from jax.sharding import PartitionSpec as P

HD = 128
BLOCK = 32
F32 = jnp.float32
BEGIN_MIB = 61.8
BF16 = jnp.bfloat16
FR = ("fsdp", "rep")
MB = 1 << 20


def swap(x, axis, xor):
    return lax.ppermute(x, axis, [(i, i ^ xor) for i in range(lax.axis_size(axis))])


def nt_dot(a, b):
    return lax.dot_general(a, b, (((1,), (1,)), ((), ())), preferred_element_type=F32)


def call(kernel, name, mib, weight=1024, **kw):
    return pl.pallas_call(
        kernel,
        compiler_params=pltpu.CompilerParams(vmem_limit_bytes=int(mib * MB)),
        cost_estimate=pl.CostEstimate(flops=1024, bytes_accessed=weight, transcendentals=0),
        name=name,
        **kw,
    )


def sds(shape, dtype):
    return jax.ShapeDtypeStruct(shape, dtype)


HBM = pl.BlockSpec(memory_space=pltpu.HBM)
VMEM = pl.BlockSpec(memory_space=pltpu.VMEM)
ANY = pl.BlockSpec(memory_space=pl.ANY)
DMA = pltpu.SemaphoreType.DMA


def shard_index():
    return lax.axis_index("fsdp") * lax.axis_size("rep") + lax.axis_index("rep")


def half_rows(which, half):
    return pl.multiple_of(((lax.axis_index("tp") % 2) ^ which) * half, 16)


def refreshed(base, delta, exponents):
    blocks, width = exponents.shape[0], delta.shape[1]
    factor = jnp.exp2(exponents.astype(F32)).astype(BF16)
    row = lax.broadcasted_iota(jnp.int32, (blocks, width), 0)
    col = lax.broadcasted_iota(jnp.int32, (blocks, width), 1)
    spread = jnp.where((col >> 5) == row, 1.0, 0.0).astype(BF16)
    scale = lax.dot_general(factor, spread, (((0,), (0,)), ((), ())), preferred_element_type=F32)
    return (base.astype(F32) + delta.astype(F32) * scale).astype(BF16)


def begin_kernel(
    sliced, parts, qw, kvw, ow, qd, kvd, od, kc, vc, qe, kve, oe, fresh, far, *refs
):
    outs, (qw_v, kvw_v, ow_v, qd_v, kvd_v, od_v, sem) = refs[:parts], refs[parts:]
    rows, width = qd.shape
    cols = pl.ds(0 if sliced else pl.multiple_of(shard_index() * width, 128), width)
    far_rows = pl.ds(half_rows(1, far.shape[1]), far.shape[1])
    o_rows = od.shape[0]
    place = pl.ds(pl.multiple_of(shard_index() * o_rows, 16), o_rows)
    loads = [
        pltpu.make_async_copy(src, dst, sem.at[n])
        for n, (src, dst) in enumerate(
            [
                (qw.at[:, cols], qw_v),
                (qd, qd_v),
                (kvw.at[:, :, cols], kvw_v),
                (kvd, kvd_v),
                (ow.at[place], ow_v),
                (od, od_v),
                (kc.at[far_rows], far.at[0]),
                (vc.at[far_rows], far.at[1]),
            ]
        )
    ]
    for load in loads:
        load.start()
    loads[0].wait()
    loads[1].wait()
    fresh[:rows] = refreshed(qw_v[...], qd_v[...], qe[...])
    loads[2].wait()
    loads[3].wait()
    narrow = kvd.shape[1]
    for n in range(2):
        part = slice(rows + n * narrow, rows + (n + 1) * narrow)
        fresh[part] = refreshed(kvw_v[n], kvd_v[n], kve[:, n, :])
    loads[4].wait()
    loads[5].wait()
    result = refreshed(ow_v[...], od_v[...], oe[...])
    if parts == 1:
        outs[0][...] = result
    else:
        quarter = [result[n * o_rows // 4 : (n + 1) * o_rows // 4] for n in range(4)]
        outs[0][...] = quarter[0]
        outs[1][...] = jnp.concatenate([quarter[1], quarter[3]], axis=0)
        outs[2][...] = quarter[2]
    loads[6].wait()
    loads[7].wait()


def begin(
    parts, q_weight, kv_weight, o_weight, q_delta, q_exp, kv_delta, kv_exp, o_delta, o_exp,
    keys, values,
):
    rows, width = q_delta.shape
    narrow = kv_delta.shape[1]
    sliced = width % 128 != 0
    if sliced:
        start = shard_index() * width
        q_weight = lax.dynamic_slice_in_dim(q_weight, start, width, 1)
        kv_weight = lax.dynamic_slice_in_dim(kv_weight, start, width, 2)
    sizes = (4,) if parts == 1 else (1, 2, 1)
    pair = lambda a: [pltpu.VMEM(a.shape, BF16)]
    return call(
        functools.partial(begin_kernel, sliced, parts),
        "begin",
        BEGIN_MIB,
        out_shape=(
            sds((rows + 2 * narrow, width), BF16),
            sds((2, keys.shape[0] // 2) + keys.shape[1:], BF16),
        )
        + tuple(sds((o_delta.shape[0] * n // 4, o_delta.shape[1]), BF16) for n in sizes),
        in_specs=[HBM] * 8 + [VMEM] * 3,
        out_specs=(VMEM,) * (2 + parts),
        scratch_shapes=(pair(q_delta) + pair(kv_delta) + pair(o_delta)) * 2 + [DMA((8,))],
    )(
        q_weight, kv_weight, o_weight, q_delta, kv_delta, o_delta, keys, values,
        q_exp.T, kv_exp.transpose(2, 0, 1), o_exp.T,
    )


CHUNKS = 8


def prepare_kernel(hidden, gain, lengths, after, normed, cosine, sine, hidden_v, gain_v, sem):
    steps, rows, _ = hidden.shape
    tile = steps * rows // CHUNKS
    per_step = rows // tile
    loads = []
    for n in range(CHUNKS):
        s, at = n // per_step, pl.ds(n % per_step * tile, tile)
        loads.append(pltpu.make_async_copy(hidden.at[s, at], hidden_v.at[n], sem.at[n]))
    loads.append(pltpu.make_async_copy(gain, gain_v, sem.at[CHUNKS]))
    for load in loads:
        load.start()
    lane = lax.broadcasted_iota(jnp.int32, (1, HD), 1) & (HD // 2 - 1)
    frequency = jnp.exp(lane.astype(F32) * (-2.0 / HD * math.log(1000000.0)))
    length = jnp.broadcast_to(lengths[...].astype(F32), (HD, rows)).T
    low = lax.broadcasted_iota(jnp.int32, (1, HD), 1) < HD // 2
    for s in range(steps):
        angles = (length + float(s)) * frequency
        at = slice(s * rows, (s + 1) * rows)
        cosine[at] = jnp.cos(angles)
        turned = jnp.sin(angles)
        sine[at] = jnp.where(low, -turned, turned)
    loads[CHUNKS].wait()
    for n in range(CHUNKS):
        loads[n].wait()
        values = hidden_v[n].astype(F32)
        root = lax.rsqrt(jnp.mean(values * values, axis=-1, keepdims=True) + 1e-06)
        normed[n * tile : (n + 1) * tile] = (values * root * gain_v[...]).astype(BF16)


def prepare(hidden, gain, lengths, after):
    steps, rows, width = hidden.shape
    table = sds((steps * rows, HD), F32)
    return call(
        prepare_kernel,
        "prepare",
        16,
        weight=10 * MB,
        out_shape=(sds((steps * rows, width), BF16), table, table),
        in_specs=[HBM, HBM, VMEM, ANY],
        out_specs=(VMEM,) * 3,
        scratch_shapes=[
            pltpu.VMEM((CHUNKS, steps * rows // CHUNKS, width), BF16),
            pltpu.VMEM((1, width), F32),
            DMA((CHUNKS + 1,)),
        ],
    )(hidden, gain.reshape(1, width), lengths.reshape(1, rows), after)


def halves_kernel(along_x, along_y, *refs):
    first, second, both = refs[-3:]
    rows = along_x.shape[0]
    first[...] = along_x[: rows // 2]
    second[...] = along_y[rows // 2 :]
    both[:rows] = along_x[...]
    both[rows:] = along_y[...]


def halves(along_x, along_y, after):
    rows, width = along_x.shape
    out = sds((rows // 2, width), BF16)
    return call(
        halves_kernel,
        "halves",
        8,
        out_shape=(out, out, sds((2 * rows, width), BF16)),
        in_specs=[VMEM, VMEM] + [ANY] * len(after),
        out_specs=(VMEM,) * 3,
    )(along_x, along_y, *after)


def term(place, normed, shard):
    width = shard.shape[1]
    owner = (lax.axis_index("fsdp") ^ place[0]) * lax.axis_size("rep")
    owner += lax.axis_index("rep") ^ place[1]
    return nt_dot(normed[:, pl.ds(pl.multiple_of(owner * width, 128), width)], shard)


def project_kernel(places, rows, normed, *refs):
    total = None
    for group, ref in zip(places, refs):
        for n, place in enumerate(group):
            part = term(place, normed, ref[n * rows : (n + 1) * rows])
            total = part if total is None else total + part
    refs[-1][...] = total


def project(places, normed, shards):
    rows = shards[0].shape[0]
    return call(
        functools.partial(project_kernel, places, rows),
        "project",
        16,
        out_shape=sds((normed.shape[0], rows), F32),
        in_specs=[VMEM] * (1 + len(shards)),
        out_specs=VMEM,
    )(normed, *shards)


def finish_kernel(places, steps, normed, total_in, qb, kvb, cosine, sine, *refs):
    own, other, packed = refs[-3:]
    total = total_in[...]
    for n, place in enumerate(places):
        shard = jnp.concatenate([refs[2 * n][...], refs[2 * n + 1][...]], axis=0)
        total += term(place, normed, shard)
    span = qb.shape[1]
    for head in range(span // HD):
        cols = slice(head * HD, (head + 1) * HD)
        query = total[:, cols] + qb[:, cols].astype(F32)
        turned = query * cosine[...] + pltpu.roll(query, HD // 2, 1) * sine[...]
        packed[:, cols] = turned.astype(BF16)
    key = total[:, span : span + HD // 2] + kvb[0:1].astype(F32)
    value = total[:, span + HD // 2 :] + kvb[1:2].astype(F32)
    high = key.astype(BF16)
    rest = key - high.astype(F32)
    middle = rest.astype(BF16)
    low = (rest - middle.astype(F32)).astype(BF16)
    packed[:, span : span + HD] = jnp.concatenate([high, middle], axis=1)
    packed[:, span + HD :] = jnp.concatenate([low, value.astype(BF16)], axis=1)
    rows = packed.shape[0] // steps
    for s in range(steps):
        own[s] = packed[pl.ds(s * rows + half_rows(0, rows // 2), rows // 2), :]
        other[s] = packed[pl.ds(s * rows + half_rows(1, rows // 2), rows // 2), :]


def finish(places, steps, normed, total, q_bias, kv_bias, cosine, sine, shards):
    rows = normed.shape[0] // steps
    width = q_bias.shape[0] + 2 * HD
    out = sds((steps, rows // 2, width), BF16)
    return call(
        functools.partial(finish_kernel, places, steps),
        "finish",
        16,
        out_shape=(out, out),
        in_specs=[VMEM] * (6 + len(shards)),
        out_specs=(VMEM, VMEM),
        scratch_shapes=[pltpu.VMEM((steps * rows, width), BF16)],
    )(normed, total, q_bias.reshape(1, -1), kv_bias, cosine, sine, *shards)


GROUP = 16


def attend_kernel(
    own, other, cosine, sine, swapped, lengths, keys, values,
    out, new_k, new_v, near_kv, limits, sem
):
    steps, rows, width = own.shape
    heads = (width - 2 * HD) // HD
    half = HD // 2
    parity = lax.axis_index("tp") % 2
    even = parity == 0
    first = half_rows(0, rows)
    loads = [
        pltpu.make_async_copy(src.at[pl.ds(first, rows)], near_kv.at[n], sem.at[n])
        for n, src in enumerate((keys, values))
    ]
    for load in loads:
        load.start()
    limits[...] = jnp.broadcast_to(lengths[...], (HD, lengths.shape[1])).T
    scale = HD ** (-0.5)
    base = width - 2 * HD

    def key_of(ref, s):
        top = ref[s, :, base : base + HD].astype(F32)
        rest = ref[s, :, base + HD :].astype(F32)
        return top[:, :half] + (top[:, half:] + rest[:, :half]), rest[:, half:]

    for s in range(steps):
        key_a, value_a = key_of(own, s)
        key_b, value_b = key_of(other, s)
        key = jnp.where(
            even,
            jnp.concatenate([key_a, key_b], axis=1),
            jnp.concatenate([key_b, key_a], axis=1),
        )
        value = jnp.where(
            even,
            jnp.concatenate([value_a, value_b], axis=1),
            jnp.concatenate([value_b, value_a], axis=1),
        )
        at = pl.ds(pl.multiple_of(s * 2 * rows + first, 16), rows)
        turned = key * cosine[at, :] + pltpu.roll(key, half, 1) * sine[at, :]
        new_k[s] = turned.astype(BF16)
        new_v[s] = value.astype(BF16)

    span = keys.shape[1]
    count = steps * 2 * heads * GROUP
    lane = GROUP * span
    row_of = lax.broadcasted_iota(jnp.int32, (count, lane), 0) & (GROUP - 1)
    column = lax.broadcasted_iota(jnp.int32, (count, lane), 1)
    diagonal = row_of == column // span
    slot = column % span
    fresh = GROUP * steps
    fresh_row = lax.broadcasted_iota(jnp.int32, (count, fresh), 0)
    fresh_col = lax.broadcasted_iota(jnp.int32, (count, fresh), 1)
    fresh_ok = jnp.logical_and(
        (fresh_row & (GROUP - 1)) == (fresh_col & (GROUP - 1)),
        fresh_col // GROUP <= fresh_row // (2 * heads * GROUP),
    )
    lowest = -1e30
    for load in loads:
        load.wait()
    for g in range(rows // GROUP):
        at = slice(g * GROUP, (g + 1) * GROUP)
        query = jnp.concatenate(
            [
                ref[s, at, h * HD : (h + 1) * HD]
                for s in range(steps)
                for ref in (own, other)
                for h in range(heads)
            ],
            axis=0,
        )
        near_k = near_kv[0, at].reshape(lane, HD)
        near_v = near_kv[1, at].reshape(lane, HD)
        far_k = swapped[0, at].reshape(lane, HD)
        far_v = swapped[1, at].reshape(lane, HD)
        fresh_k = jnp.concatenate([new_k[s, at] for s in range(steps)], axis=0)
        fresh_v = jnp.concatenate([new_v[s, at] for s in range(steps)], axis=0)
        limit = limits[pl.ds(first + g * GROUP, GROUP), :1]
        limit = jnp.concatenate([limit] * (count // GROUP), axis=0)
        ok_n = jnp.logical_and(diagonal, slot + parity * span < limit)
        ok_f = jnp.logical_and(diagonal, slot + (1 - parity) * span < limit)
        score_n = jnp.where(ok_n, nt_dot(query, near_k) * scale, lowest)
        score_f = jnp.where(ok_f, nt_dot(query, far_k) * scale, lowest)
        score_x = jnp.where(fresh_ok, nt_dot(query, fresh_k) * scale, lowest)
        top_n = jnp.max(score_n, axis=1, keepdims=True)
        top_f = jnp.max(score_f, axis=1, keepdims=True)
        top_x = jnp.max(score_x, axis=1, keepdims=True)
        top_n = jnp.where(even, jnp.maximum(top_n, top_x), top_n)
        top_f = jnp.where(even, top_f, jnp.maximum(top_f, top_x))
        top_x = jnp.where(even, top_n, top_f)
        weight_n = jnp.where(ok_n, jnp.exp(score_n - top_n), 0.0)
        weight_f = jnp.where(ok_f, jnp.exp(score_f - top_f), 0.0)
        weight_x = jnp.where(fresh_ok, jnp.exp(score_x - top_x), 0.0)
        top_all = jnp.maximum(top_n, top_f)
        factor_n = jnp.exp(top_n - top_all)
        factor_f = jnp.exp(top_f - top_all)
        factor_x = jnp.where(even, factor_n, factor_f)
        acc = (
            factor_n * jnp.dot(weight_n.astype(BF16), near_v, preferred_element_type=F32)
            + factor_f * jnp.dot(weight_f.astype(BF16), far_v, preferred_element_type=F32)
            + factor_x * jnp.dot(weight_x.astype(BF16), fresh_v, preferred_element_type=F32)
        )
        total = (
            factor_n * jnp.sum(weight_n, axis=1, keepdims=True)
            + factor_f * jnp.sum(weight_f, axis=1, keepdims=True)
            + factor_x * jnp.sum(weight_x, axis=1, keepdims=True)
        )
        result = (acc / total).astype(BF16)
        for s in range(steps):
            for h in range(2 * heads):
                place = (s * 2 * heads + h) * GROUP
                out[s, at, h * HD : (h + 1) * HD] = result[place : place + GROUP]


def attend(own, other, cosine, sine, swapped, lengths, keys, values):
    steps, rows, width = own.shape
    return call(
        attend_kernel,
        "attend",
        24,
        out_shape=sds((steps, rows, 2 * (width - 2 * HD)), BF16),
        in_specs=[VMEM] * 6 + [HBM] * 2,
        out_specs=VMEM,
        scratch_shapes=[
            pltpu.VMEM((steps, rows, HD), BF16),
            pltpu.VMEM((steps, rows, HD), BF16),
            pltpu.VMEM((2, rows) + keys.shape[1:], BF16),
            pltpu.VMEM((lengths.shape[0], HD), jnp.int32),
            DMA((2,)),
        ],
    )(own, other, cosine, sine, swapped, lengths.reshape(1, -1), keys, values)


def relay_kernel(own, along_x, after, out):
    rows = own.shape[0]
    out[:rows] = own[...]
    out[rows:] = along_x[rows:]


def relay(own, along_x, after):
    return call(
        relay_kernel,
        "relay",
        8,
        out_shape=sds(along_x.shape, BF16),
        in_specs=[VMEM] * 2 + [ANY],
        out_specs=VMEM,
    )(own, along_x, after)


def pick_kernel(own, along_x, along_y, *refs):
    outs, rows = refs[-4:], own.shape[0]
    blocks = [own[...], along_x[:rows], along_y[:rows], along_y[rows:]]
    where = lax.axis_index("fsdp") ^ lax.axis_index("tp")
    for k, out in enumerate(outs):
        for i, block in enumerate(blocks):

            @pl.when((where ^ k) == i)
            def _(out=out, block=block):
                out[...] = block


def pick(own, along_x, along_y, after):
    return call(
        pick_kernel,
        "pick",
        8,
        out_shape=(sds(own.shape, BF16),) * 4,
        in_specs=[VMEM] * 3 + [ANY] * len(after),
        out_specs=(VMEM,) * 4,
    )(own, along_x, along_y, *after)


def stack_kernel(*refs):
    rows = refs[0].shape[0]
    for n, ref in enumerate(refs[: refs[-1].shape[0] // rows]):
        refs[-1][n * rows : (n + 1) * rows] = ref[...]


def stack(blocks, after):
    rows, width = blocks[0].shape
    return call(
        stack_kernel,
        "stack",
        8,
        out_shape=sds((len(blocks) * rows, width), BF16),
        in_specs=[VMEM] * len(blocks) + [ANY] * len(after),
        out_specs=VMEM,
    )(*blocks, *after)


def assemble_kernel(*refs):
    weight = refs[-1]
    rows, width = refs[0].shape[0] // 4, refs[0].shape[1]
    for j in range(2):
        for i in range(4):
            shard, first = refs[2 * j + min(i, 1)], max(i - 1, 0) * 4
            quarter = lax.axis_index("fsdp") ^ i ^ lax.axis_index("tp")
            place = ((lax.axis_index("rep") ^ j) * 4 + quarter) * rows
            for k in range(4):
                weight[pl.ds(pl.multiple_of(place, 16), rows), k * width : (k + 1) * width] = (
                    shard[(first + k) * rows : (first + k + 1) * rows]
                )


def assemble(*shards):
    rows, width = shards[0].shape
    return call(
        assemble_kernel,
        "assemble",
        16,
        out_shape=sds((2 * rows, 4 * width), BF16),
        in_specs=[VMEM] * len(shards),
        out_specs=VMEM,
    )(*shards)


def output_kernel(weight, a0, a1, a2, a3, hidden, out, hidden_v, sem):
    width = weight.shape[1] // 4
    steps, half = a0.shape[:2]
    cols = out.shape[2]
    place = pl.ds(pl.multiple_of(lax.axis_index("tp") * cols, 128), cols)
    load = pltpu.make_async_copy(hidden.at[:, :, place], hidden_v, sem)
    load.start()
    flat = lambda ref: ref[...].reshape(steps * half, 2 * width)
    b1, b3 = flat(a1), flat(a3)
    top = nt_dot(flat(a0), weight[:, : 2 * width]) + nt_dot(flat(a2), weight[:, 2 * width :])
    low = (
        nt_dot(b1[:, :width], weight[:, width : 2 * width])
        + nt_dot(b1[:, width:], weight[:, :width])
        + nt_dot(b3[:, :width], weight[:, 3 * width :])
        + nt_dot(b3[:, width:], weight[:, 2 * width : 3 * width])
    )
    load.wait()
    for which, total in ((0, top), (1, low)):
        for s in range(steps):
            at = pl.ds(half_rows(which, half), half)
            mixed = total[s * half : (s + 1) * half]
            out[s, at, :] = (hidden_v[s, at, :].astype(F32) + mixed).astype(BF16)


def output(weight, parts, hidden):
    steps, rows, _ = hidden.shape
    shape = (steps, rows, weight.shape[0])
    return call(
        output_kernel,
        "output",
        24,
        out_shape=sds(shape, BF16),
        in_specs=[VMEM] * (1 + len(parts)) + [HBM],
        out_specs=VMEM,
        scratch_shapes=[pltpu.VMEM(shape, BF16), DMA],
    )(weight, *parts, hidden)


def shards(
    hidden_in,
    norm_gain,
    q_weight,
    q_bias,
    kv_weight,
    kv_bias,
    o_weight,
    q_delta,
    q_scale_exp,
    kv_delta,
    kv_scale_exp,
    o_delta,
    o_scale_exp,
    key_cache,
    value_cache,
    cache_lengths,
):
    steps, rows, model_width = hidden_in.shape
    q_width = q_weight.shape[0]
    half = rows // 2
    fsdp, tp, rep = (lax.axis_size(a) for a in ("fsdp", "tp", "rep"))
    shard_width = q_delta.shape[1]
    col_width = model_width // tp
    small = fsdp == 4 and tp == 4 and rep == 2 and shard_width % 128 == 0 and col_width % 128 == 0
    keys, values = key_cache[:, 0], value_cache[:, 0]

    fresh, far, *o_parts = begin(
        3 if small else 1, q_weight, kv_weight, o_weight, q_delta, q_scale_exp, kv_delta,
        kv_scale_exp, o_delta, o_scale_exp, keys, values,
    )
    swapped = swap(far, "tp", 1)
    normed, cosine, sine = prepare(hidden_in, norm_gain, cache_lengths, o_parts[0])

    if small:
        along_x, along_y = swap(fresh, "fsdp", 1), swap(fresh, "fsdp", 2)
        o_x = swap(o_parts[1], "fsdp", 1)
        first, second, both = halves(along_x, along_y, [cosine, o_x])
        last = [swap(first, "fsdp", 2), swap(second, "fsdp", 1)]
        o_parts = [o_parts[0], o_x, swap(relay(o_parts[2], o_x, first), "fsdp", 2)]
        near = [fresh, both]
        near += [swap(a, "rep", 1) for a in near]
        last += [swap(a, "rep", 1) for a in last]
        places = [[(0, 0)], [(1, 0), (2, 0)], [(0, 1)], [(1, 1), (2, 1)]]
        total = project(places, normed, near)
        own, other = finish(
            [(3, 0), (3, 1)], steps, normed, total, q_bias, kv_bias, cosine, sine, last
        )
    else:
        full = lax.all_gather(fresh, FR, axis=1, tiled=True)
        total = jnp.dot(normed, full.T, preferred_element_type=F32)
        own, other = finish([], steps, normed, total, q_bias, kv_bias, cosine, sine, [])

    received = swap(other, "tp", 1)
    attention = attend(own, received, cosine, sine, swapped, cache_lengths, keys, values)

    if small:
        picked = pick(*o_parts, [swapped])
        o_parts = [picked[0]] + [swap(picked[k], "tp", k) for k in (1, 2, 3)]
        parts = [attention] + [swap(attention, "tp", k) for k in (1, 2, 3)]
        stacked = stack(o_parts, [attention])
        others = stack([swap(stacked, "fsdp", i) for i in (1, 2, 3)], parts[1:])
        weight = assemble(stacked, others, swap(stacked, "rep", 1), swap(others, "rep", 1))
        return output(weight, parts, hidden_in)

    full_o = lax.all_gather(o_parts[0], FR, axis=0, tiled=True)
    own_cols = lax.all_to_all(
        full_o.reshape(tp, col_width, q_width), "tp", split_axis=0, concat_axis=2, tiled=True
    ).reshape(col_width, tp * q_width)
    everyone = lax.all_gather(attention, "tp", axis=0)
    everyone = everyone.reshape(tp // 2, 2, steps, half, 2, q_width)
    odd = everyone[:, 1][:, :, :, ::-1]
    everyone = jnp.stack([everyone[:, 0], odd], axis=0)
    features = everyone.transpose(2, 0, 3, 1, 4, 5).reshape(steps * rows, tp * q_width)
    mixed = jnp.dot(features, own_cols.T, preferred_element_type=F32)
    start = lax.axis_index("tp") * col_width
    residual = lax.dynamic_slice_in_dim(hidden_in, start, col_width, 2).astype(F32)
    return (residual + mixed.reshape(steps, rows, col_width)).astype(BF16)


def solution(mesh):
    placed = (
        P(None, ("fsdp", "rep"), None),
        P(),
        P("tp", None),
        P("tp"),
        P(None, "tp", None),
        P(None, "tp"),
        P(None, "tp"),
        P("tp", ("fsdp", "rep")),
        P("tp", ("fsdp", "rep")),
        P(None, "tp", ("fsdp", "rep")),
        P(None, "tp", ("fsdp", "rep")),
        P(("fsdp", "rep"), "tp"),
        P(("fsdp", "rep"), "tp"),
        P(("fsdp", "rep"), "tp", None, None),
        P(("fsdp", "rep"), "tp", None, None),
        P(("fsdp", "rep")),
    )
    return jax.shard_map(
        shards,
        mesh=mesh,
        in_specs=placed,
        out_specs=P(None, ("fsdp", "rep"), "tp"),
        check_vma=False,
    )
```

time: 207 us -> 72.5 us (0.35)
  waiting for transfers between devices: 110 us -> 26.6 us
  other arithmetic: 25.6 us -> 0 us
  starting transfers between devices: 6.82 us -> 27.8 us
  blocking collectives: 20.1 us -> 0 us
  local copies, waits for them, and re-layouts: 20.4 us -> 2.68 us
  Pallas kernels: 0 us -> 14.8 us
  between operations: 13.5 us -> 0.23 us
  matrix products: 10.5 us -> 0 us
    reduce_scatter x1 -> x0, waiting for transfers between devices: 93 us -> none  [shards(): lax.psum_scatter(partial_value, 'tp', scatter_dimension=2, tiled=True)]
    ppermute x5 -> x23, starting transfers between devices: 6.74 us -> 27.8 us  [swap(): lax.ppermute(x, axis, [(i, i ^ xor) for i in range(lax.axis_size(axis))])]
    ppermute x5 -> x23, waiting for transfers between devices: 6.1 us -> 26.6 us  [swap(): lax.ppermute(x, axis, [(i, i ^ xor) for i in range(lax.axis_size(axis))])]
    all_gather x2 -> x0, blocking collectives: 20.1 us -> none  [the longest x1 10.9 us: shards(): lax.all_gather(delta_factors, ('fsdp', 'rep'), axis=1, tiled=True)]
    convert_element_type x12 -> x0, other arithmetic: 18.1 us -> none  [the longest x2 9.46 us: refresh(): return (base_matrix.astype(jnp.float32) + change).astype(jnp.bfloat16)]
    pallas_call x0 -> x12, Pallas kernels: none -> 14.8 us  [the longest x1 4.02 us: begin(): call(functools.partial(begin_kernel, sliced, parts), 'begin', BEGIN_MIB,...]
    all_gather x2 -> x0, waiting for transfers between devices: 10.7 us -> none  [the longest x1 10.7 us: shards(): lax.all_gather(delta_rows, ('fsdp', 'rep'), axis=1, tiled=True)]
    dot_general x6 -> x0, matrix products: 10.5 us -> none  [the longest x1 4.91 us: shards(): jnp.dot(attention, fresh_o.T, preferred_element_type=jnp.float32)]
  transfers between devices with their start and end apart: 8 -> 23, of which waited for: 4 -> 8; matrix products, arithmetic and copies ran while one was open for 22% -> 0% of each run, Pallas kernels for 0% -> 11%
where the time goes in v2:
time: 72.5 us; the launch traced here: 72.2 us
  starting transfers between devices  27.8 us (38%)
  waiting for transfers between devices  26.6 us (37%)
  Pallas kernels  14.8 us (20%)
  local copies, waits for them, and re-layouts  2.68 us (4%)
    ppermute x23, starting transfers between devices, swap(): lax.ppermute(x, axis, [(i, i ^ xor) for i in range(lax.axis_size(axis))])  27.8 us
    ppermute x23, waiting for transfers between devices, swap(): lax.ppermute(x, axis, [(i, i ^ xor) for i in range(lax.axis_size(axis))])  26.6 us
    pallas_call x1, Pallas kernels, begin(): call(functools.partial(begin_kernel, sliced, parts), 'begin', BEGIN_MIB,...  4.02 us
    pallas_call x1, Pallas kernels, prepare(): call(prepare_kernel, 'prepare', 16, weight=10 * MB, out_shape=(sds((steps...  3.06 us
    pallas_call x1, Pallas kernels, output(): call(output_kernel, 'output', 24, out_shape=sds(shape, BF16), in_specs=[V...  2.83 us
    unnamed x22, local copies, waits for them, and re-layouts  2.67 us
    pallas_call x1, Pallas kernels, attend(): call(attend_kernel, 'attend', 24, out_shape=sds((steps, rows, 2 * (width...  2.3 us
  transfers between devices with their start and end apart: 23, of which 8 were waited for; matrix products, arithmetic and copies ran while one was open for 0% of the time, Pallas kernels for 11%

profile of v2, /device:TPU:0, one launch (start us, length us, event | category | flops | bytes accessed | tf_op | source)
XLA Modules:
  0.0 72.2 jit_solution(5761632831434777688)
XLA Ops:
  0.0 4.0 %begin.1 = (bf16[384,640]{1,0:T(8,128)(2,1)}, bf16[2,64,32,128]{3,2,1,0:T(8,128)(2,1)}, bf16[160,256]{1,0:T(8,128)(2,1)}, bf16[320,256]{1,0:T(8,128)(2,1)}, bf16[160,256]{1,0:T(8,128)(2,1)}) custom-call(bf16[256,5120]{1,0:T(8,128)(2,1)} %qw.1, bf16[2,64,5120]{2,1,0:T(8,128)(2,1)} %kvw.1, bf16[5120,256]{1,0:T(8,128)(2,1)} %ow.1, bf16[256,640]{1,0:T(8,128)(2,1)} %qd.1, ...), custom_call_target="tpu_custom_call" | custom-call | flops 1024 | bytes 1024 | tf_op jit(solution)/shard_map/begin/pallas_call | solution.py:128
  4.0 0.0 copy-start.10
  4.0 3.0 %collective-permute-start.1 = (bf16[384,640]{1,0:T(8,128)(2,1)}, bf16[384,640]{1,0:T(8,128)(2,1)S(1)}, u32[]{:S(2)}, u32[]{:S(2)}) collective-permute-start(bf16[384,640]{1,0:T(8,128)(2,1)} %get-tuple-element.25.refs_0_), channel_id=1, source_target_pairs={{0,8},{8,0},{16,24},{24,16},{1,9},{9,1},{17,25},{25,17},{2,10},{10... | collective-permute-start | bytes 1474568 | tf_op jit(solution)/shard_map/ppermute | solution.py:21
  7.0 1.5 %collective-permute-start.2 = (bf16[384,640]{1,0:T(8,128)(2,1)}, bf16[384,640]{1,0:T(8,128)(2,1)S(1)}, u32[]{:S(2)}, u32[]{:S(2)}) collective-permute-start(bf16[384,640]{1,0:T(8,128)(2,1)} %get-tuple-element.25.refs_0_), channel_id=1, source_target_pairs={{0,16},{8,24},{16,0},{24,8},{1,17},{9,25},{17,1},{25,9},{2,18},{10... | collective-permute-start | bytes 1474568 | tf_op jit(solution)/shard_map/ppermute | solution.py:21
  8.6 0.5 collective-permute-start
  9.1 1.6 %collective-permute-start.4 = (bf16[2,64,32,128]{3,2,1,0:T(8,128)(2,1)}, bf16[2,64,32,128]{3,2,1,0:T(8,128)(2,1)S(1)}, u32[]{:S(2)}, u32[]{:S(2)}) collective-permute-start(bf16[2,64,32,128]{3,2,1,0:T(8,128)(2,1)} %get-tuple-element.28), channel_id=1, source_target_pairs={{0,2},{2,0},{4,6},{6,4},{1,3},{3,1},{5,7},{7,5},{8,10},{10,8},{12,... | collective-permute-start | bytes 3145736 | tf_op jit(solution)/shard_map/ppermute | solution.py:21
  10.7 1.7 %copy-done = bf16[2,128,5120]{2,1,0:T(8,128)(2,1)S(1)} copy-done((bf16[2,128,5120]{2,1,0:T(8,128)(2,1)S(1)}, bf16[2,128,5120]{2,1,0:T(8,128)(2,1)}, u32[]{:S(2)}) %copy-start) | copy-done | bytes 2621464
  12.4 0.9 %copy-done.5 = bf16[160,256]{1,0:T(8,128)(2,1)S(1)} copy-done((bf16[160,256]{1,0:T(8,128)(2,1)S(1)}, bf16[160,256]{1,0:T(8,128)(2,1)}, u32[]{:S(2)}) %copy-start.5) | copy-done | bytes 81944
  13.3 3.1 %prepare.1 = (bf16[256,5120]{1,0:T(8,128)(2,1)S(1)}, f32[256,128]{1,0:T(8,128)S(1)}, f32[256,128]{1,0:T(8,128)S(1)}) custom-call(bf16[2,128,5120]{2,1,0:T(8,128)(2,1)S(1)} %copy-done, f32[1,5120]{1,0:T(1,128)S(1)} %bitcast.11, s32[1,128]{1,0:T(1,128)S(1)} %bitcast.12, bf16[160,256]{1,0:T(8,128)(2,1)S(1)} %copy-done.5), custom_call_target="tpu_custom_call" | custom-call | flops 1024 | bytes 10485760 | tf_op jit(solution)/shard_map/prepare/pallas_call | solution.py:181
  16.4 5.6 %collective-permute-done.refs_1_.along_x = bf16[320,256]{1,0:T(8,128)(2,1)S(1)} collective-permute-done((bf16[320,256]{1,0:T(8,128)(2,1)}, bf16[320,256]{1,0:T(8,128)(2,1)S(1)}, u32[]{:S(2)}, u32[]{:S(2)}) %collective-permute-start) | collective-permute-done | bytes 163872 | tf_op jit(solution)/shard_map/ppermute | solution.py:21
  22.0 0.0 collective-permute-done.2.along_y
  22.0 0.1 halves.1
  22.1 0.1 collective-permute-start.9
  22.2 0.5 collective-permute-start.8
  22.7 1.8 %collective-permute-start.10 = (bf16[192,640]{1,0:T(8,128)(2,1)S(1)}, bf16[192,640]{1,0:T(8,128)(2,1)S(1)}, u32[]{:S(2)}, u32[]{:S(2)}) collective-permute-start(bf16[192,640]{1,0:T(8,128)(2,1)S(1)} %get-tuple-element.27.after), channel_id=1, source_target_pairs={{0,16},{8,24},{16,0},{24,8},{1,17},{9,25},{17,1},{25,9},{2,18},{10... | collective-permute-start | bytes 737288 | tf_op jit(solution)/shard_map/ppermute | solution.py:21
  24.5 1.5 %collective-permute-start.11 = (bf16[192,640]{1,0:T(8,128)(2,1)S(1)}, bf16[192,640]{1,0:T(8,128)(2,1)S(1)}, u32[]{:S(2)}, u32[]{:S(2)}) collective-permute-start(bf16[192,640]{1,0:T(8,128)(2,1)S(1)} %get-tuple-element.36), channel_id=1, source_target_pairs={{0,8},{8,0},{16,24},{24,16},{1,9},{9,1},{17,25},{25,17},{2,10},{10... | collective-permute-start | bytes 737288 | tf_op jit(solution)/shard_map/ppermute | solution.py:21
  26.0 4.7 %collective-permute-done.10.refs_0_ = bf16[192,640]{1,0:T(8,128)(2,1)S(1)} collective-permute-done((bf16[192,640]{1,0:T(8,128)(2,1)S(1)}, bf16[192,640]{1,0:T(8,128)(2,1)S(1)}, u32[]{:S(2)}, u32[]{:S(2)}) %collective-permute-start.10) | collective-permute-done | bytes 245792 | tf_op jit(solution)/shard_map/ppermute | solution.py:21
  30.7 0.0 collective-permute-start.12
  30.7 1.5 %collective-permute-done.11.refs_1_ = bf16[192,640]{1,0:T(8,128)(2,1)S(1)} collective-permute-done((bf16[192,640]{1,0:T(8,128)(2,1)S(1)}, bf16[192,640]{1,0:T(8,128)(2,1)S(1)}, u32[]{:S(2)}, u32[]{:S(2)}) %collective-permute-start.11) | collective-permute-done | bytes 245792 | tf_op jit(solution)/shard_map/ppermute | solution.py:21
  32.2 0.9 %collective-permute-start.3 = (bf16[320,256]{1,0:T(8,128)(2,1)S(1)}, bf16[320,256]{1,0:T(8,128)(2,1)S(1)}, u32[]{:S(2)}, u32[]{:S(2)}) collective-permute-start(bf16[320,256]{1,0:T(8,128)(2,1)S(1)} %relay.1), channel_id=1, source_target_pairs={{0,16},{8,24},{16,0},{24,8},{1,17},{9,25},{17,1},{25,9},{2,18},{10... | collective-permute-start | bytes 491528 | tf_op jit(solution)/shard_map/ppermute | solution.py:21
  33.0 0.0 copy-start.9
  33.0 1.3 %project.1.total_in = f32[256,384]{1,0:T(8,128)S(1)} custom-call(bf16[256,5120]{1,0:T(8,128)(2,1)S(1)} %get-tuple-element.33.normed, bf16[384,640]{1,0:T(8,128)(2,1)S(1)} %copy-done.4, bf16[768,640]{1,0:T(8,128)(2,1)S(1)} %get-tuple-element.34.refs_1_, bf16[384,640]{1,0:T(8,128)(2,1)S(1)} %collective-permute-done.8.refs_2_, ...), custom_call_target="tpu_custom_call" | custom-call | flops 1024 | bytes 1024 | tf_op jit(solution)/shard_map/project/pallas_call | solution.py:237
  34.4 0.0 copy-start.2
  34.4 0.0 copy-start.3
  34.4 0.7 finish.1
  35.1 1.6 %collective-permute-start.14 = (bf16[2,64,512]{2,1,0:T(8,128)(2,1)S(1)}, bf16[2,64,512]{2,1,0:T(8,128)(2,1)S(1)}, u32[]{:S(2)}, u32[]{:S(2)}) collective-permute-start(bf16[2,64,512]{2,1,0:T(8,128)(2,1)S(1)} %get-tuple-element.38), channel_id=1, source_target_pairs={{0,2},{2,0},{4,6},{6,4},{1,3},{3,1},{5,7},{7,5},{8,10},{10,8},{12,... | collective-permute-start | bytes 393224 | tf_op jit(solution)/shard_map/ppermute | solution.py:21
  36.8 2.1 %collective-permute-done.3.along_y = bf16[320,256]{1,0:T(8,128)(2,1)S(1)} collective-permute-done((bf16[320,256]{1,0:T(8,128)(2,1)S(1)}, bf16[320,256]{1,0:T(8,128)(2,1)S(1)}, u32[]{:S(2)}, u32[]{:S(2)}) %collective-permute-start.3) | collective-permute-done | bytes 163872 | tf_op jit(solution)/shard_map/ppermute | solution.py:21
  38.8 0.1 pick.1
  38.9 1.6 %collective-permute-start.5 = (bf16[160,256]{1,0:T(8,128)(2,1)S(1)}, bf16[160,256]{1,0:T(8,128)(2,1)S(1)}, u32[]{:S(2)}, u32[]{:S(2)}) collective-permute-start(bf16[160,256]{1,0:T(8,128)(2,1)S(1)} %get-tuple-element.30), channel_id=1, source_target_pairs={{0,2},{2,0},{4,6},{6,4},{1,3},{3,1},{5,7},{7,5},{8,10},{10,8},{12,... | collective-permute-start | bytes 245768 | tf_op jit(solution)/shard_map/ppermute | solution.py:21
  40.6 2.6 %collective-permute-start.6 = (bf16[160,256]{1,0:T(8,128)(2,1)S(1)}, bf16[160,256]{1,0:T(8,128)(2,1)S(1)}, u32[]{:S(2)}, u32[]{:S(2)}) collective-permute-start(bf16[160,256]{1,0:T(8,128)(2,1)S(1)} %get-tuple-element.31), channel_id=1, source_target_pairs={{0,4},{2,6},{4,0},{6,2},{1,5},{3,7},{5,1},{7,3},{8,12},{10,14},{12... | collective-permute-start | bytes 245768 | tf_op jit(solution)/shard_map/ppermute | solution.py:21
  43.2 0.2 collective-permute-start.7
  43.4 2.3 %attend.1.refs_4_.a0 = bf16[2,64,512]{2,1,0:T(8,128)(2,1)S(1)} custom-call(bf16[2,64,512]{2,1,0:T(8,128)(2,1)S(1)} %get-tuple-element.37.own, bf16[2,64,512]{2,1,0:T(8,128)(2,1)S(1)} %collective-permute-done.14.other, f32[256,128]{1,0:T(8,128)S(1)} %get-tuple-element.26.refs_0_.cosine, f32[256,128]{1,0:T(8,128)S(1)} %get-tuple-element.35.sine, ...), custom_call_target="tpu_custom_call" | custom-call | flops 1024 | bytes 1024 | tf_op jit(solution)/shard_map/attend/pallas_call | solution.py:407
  45.7 3.9 %collective-permute-done.6.refs_2_ = bf16[160,256]{1,0:T(8,128)(2,1)S(1)} collective-permute-done((bf16[160,256]{1,0:T(8,128)(2,1)S(1)}, bf16[160,256]{1,0:T(8,128)(2,1)S(1)}, u32[]{:S(2)}, u32[]{:S(2)}) %collective-permute-start.6) | collective-permute-done | bytes 81952 | tf_op jit(solution)/shard_map/ppermute | solution.py:21
  49.7 1.6 %collective-permute-start.15 = (bf16[640,256]{1,0:T(8,128)(2,1)S(1)}, bf16[640,256]{1,0:T(8,128)(2,1)S(1)}, u32[]{:S(2)}, u32[]{:S(2)}) collective-permute-start(bf16[640,256]{1,0:T(8,128)(2,1)S(1)} %stack.2.refs_0_), channel_id=1, source_target_pairs={{0,8},{8,0},{16,24},{24,16},{1,9},{9,1},{17,25},{25,17},{2,10},{10... | collective-permute-start | bytes 983048 | tf_op jit(solution)/shard_map/ppermute | solution.py:21
  51.3 0.6 collective-permute-start.16
  51.8 1.4 %collective-permute-start.17 = (bf16[640,256]{1,0:T(8,128)(2,1)S(1)}, bf16[640,256]{1,0:T(8,128)(2,1)S(1)}, u32[]{:S(2)}, u32[]{:S(2)}) collective-permute-start(bf16[640,256]{1,0:T(8,128)(2,1)S(1)} %stack.2.refs_0_), channel_id=1, source_target_pairs={{0,24},{8,16},{16,8},{24,0},{1,25},{9,17},{17,9},{25,1},{2,26},{10... | collective-permute-start | bytes 983048 | tf_op jit(solution)/shard_map/ppermute | solution.py:21
  53.3 1.4 %collective-permute-start.18 = (bf16[2,64,512]{2,1,0:T(8,128)(2,1)S(1)}, bf16[2,64,512]{2,1,0:T(8,128)(2,1)S(1)}, u32[]{:S(2)}, u32[]{:S(2)}) collective-permute-start(bf16[2,64,512]{2,1,0:T(8,128)(2,1)S(1)} %attend.1.refs_4_.a0), channel_id=1, source_target_pairs={{0,2},{2,0},{4,6},{6,4},{1,3},{3,1},{5,7},{7,5},{8,10},{10,8},{12,... | collective-permute-start | bytes 393224 | tf_op jit(solution)/shard_map/ppermute | solution.py:21
  54.7 1.6 %collective-permute-start.19 = (bf16[2,64,512]{2,1,0:T(8,128)(2,1)S(1)}, bf16[2,64,512]{2,1,0:T(8,128)(2,1)S(1)}, u32[]{:S(2)}, u32[]{:S(2)}) collective-permute-start(bf16[2,64,512]{2,1,0:T(8,128)(2,1)S(1)} %attend.1.refs_4_.a0), channel_id=1, source_target_pairs={{0,4},{2,6},{4,0},{6,2},{1,5},{3,7},{5,1},{7,3},{8,12},{10,14},{12... | collective-permute-start | bytes 393224 | tf_op jit(solution)/shard_map/ppermute | solution.py:21
  56.3 2.2 %collective-permute-done.18.refs_3_.a1 = bf16[2,64,512]{2,1,0:T(8,128)(2,1)S(1)} collective-permute-done((bf16[2,64,512]{2,1,0:T(8,128)(2,1)S(1)}, bf16[2,64,512]{2,1,0:T(8,128)(2,1)S(1)}, u32[]{:S(2)}, u32[]{:S(2)}) %collective-permute-start.18) | collective-permute-done | bytes 131104 | tf_op jit(solution)/shard_map/ppermute | solution.py:21
  58.4 3.3 %collective-permute-start.20 = (bf16[2,64,512]{2,1,0:T(8,128)(2,1)S(1)}, bf16[2,64,512]{2,1,0:T(8,128)(2,1)S(1)}, u32[]{:S(2)}, u32[]{:S(2)}) collective-permute-start(bf16[2,64,512]{2,1,0:T(8,128)(2,1)S(1)} %attend.1.refs_4_.a0), channel_id=1, source_target_pairs={{0,6},{2,4},{4,2},{6,0},{1,7},{3,5},{5,3},{7,1},{8,14},{10,12},{12... | collective-permute-start | bytes 393224 | tf_op jit(solution)/shard_map/ppermute | solution.py:21
  61.7 4.1 %collective-permute-done.19.refs_4_.a2 = bf16[2,64,512]{2,1,0:T(8,128)(2,1)S(1)} collective-permute-done((bf16[2,64,512]{2,1,0:T(8,128)(2,1)S(1)}, bf16[2,64,512]{2,1,0:T(8,128)(2,1)S(1)}, u32[]{:S(2)}, u32[]{:S(2)}) %collective-permute-start.19) | collective-permute-done | bytes 131104 | tf_op jit(solution)/shard_map/ppermute | solution.py:21
  65.9 0.1 stack.3.refs_1_
  65.9 0.0 copy-start.1
  66.0 0.1 collective-permute-start.22
  66.0 0.5 collective-permute-start.21
  66.5 2.5 %collective-permute-done.21.refs_2_ = bf16[640,256]{1,0:T(8,128)(2,1)S(1)} collective-permute-done((bf16[640,256]{1,0:T(8,128)(2,1)S(1)}, bf16[640,256]{1,0:T(8,128)(2,1)S(1)}, u32[]{:S(2)}, u32[]{:S(2)}) %collective-permute-start.21) | collective-permute-done | bytes 327712 | tf_op jit(solution)/shard_map/ppermute | solution.py:21
  69.1 0.3 assemble.1.weight
  69.4 2.8 %output.1 = bf16[2,128,1280]{2,1,0:T(8,128)(2,1)} custom-call(bf16[1280,1024]{1,0:T(8,128)(2,1)S(1)} %assemble.1.weight, bf16[2,64,512]{2,1,0:T(8,128)(2,1)S(1)} %attend.1.refs_4_.a0, bf16[2,64,512]{2,1,0:T(8,128)(2,1)S(1)} %collective-permute-done.18.refs_3_.a1, bf16[2,64,512]{2,1,0:T(8,128)(2,1)S(1)} %collective-permute-done.19.refs_4_.a2, ...), custom_call_target="tpu_custom_call" | custom-call | flops 1024 | bytes 1024 | tf_op jit(solution)/shard_map/output/pallas_call | solution.py:535
  (33 shorter events, 0.1 us)
Async XLA Ops:
  0.0 10.7 %copy-start.7 = (f32[5120]{0:T(1024)S(1)}, f32[5120]{0:T(1024)}, u32[]{:S(2)}) copy-start(f32[5120]{0:T(1024)} %param.17) | copy-start | bytes 61444
  0.0 10.7 %copy-start.8 = (s32[128]{0:T(128)S(1)}, s32[128]{0:T(128)}, u32[]{:S(2)}) copy-start(s32[128]{0:T(128)} %param.31) | copy-start | bytes 1540
  4.0 29.0 %copy-start.10 = (bf16[256]{0:T(256)(128)(2,1)S(1)}, bf16[256]{0:T(256)(128)(2,1)}, u32[]{:S(2)}) copy-start(bf16[256]{0:T(256)(128)(2,1)} %param.19) | copy-start | bytes 1540
  4.0 17.9 %collective-permute-start.1 = (bf16[384,640]{1,0:T(8,128)(2,1)}, bf16[384,640]{1,0:T(8,128)(2,1)S(1)}, u32[]{:S(2)}, u32[]{:S(2)}) collective-permute-start(bf16[384,640]{1,0:T(8,128)(2,1)} %get-tuple-element.25.refs_0_), channel_id=1, source_target_pairs={{0,8},{8,0},{16,24},{24,16},{1,9},{9,1},{17,25},{25,17},{2,10},{10... | collective-permute-start | bytes 1474568 | tf_op jit(solution)/shard_map/ppermute | solution.py:21
  7.0 14.9 %collective-permute-start.2 = (bf16[384,640]{1,0:T(8,128)(2,1)}, bf16[384,640]{1,0:T(8,128)(2,1)S(1)}, u32[]{:S(2)}, u32[]{:S(2)}) collective-permute-start(bf16[384,640]{1,0:T(8,128)(2,1)} %get-tuple-element.25.refs_0_), channel_id=1, source_target_pairs={{0,16},{8,24},{16,0},{24,8},{1,17},{9,25},{17,1},{25,9},{2,18},{10... | collective-permute-start | bytes 1474568 | tf_op jit(solution)/shard_map/ppermute | solution.py:21
  8.6 13.4 %collective-permute-start = (bf16[320,256]{1,0:T(8,128)(2,1)}, bf16[320,256]{1,0:T(8,128)(2,1)S(1)}, u32[]{:S(2)}, u32[]{:S(2)}) collective-permute-start(bf16[320,256]{1,0:T(8,128)(2,1)} %get-tuple-element.23), channel_id=1, source_target_pairs={{0,8},{8,0},{16,24},{24,16},{1,9},{9,1},{17,25},{25,17},{2,10},{10... | collective-permute-start | bytes 491528 | tf_op jit(solution)/shard_map/ppermute | solution.py:21
  9.1 29.7 %collective-permute-start.4 = (bf16[2,64,32,128]{3,2,1,0:T(8,128)(2,1)}, bf16[2,64,32,128]{3,2,1,0:T(8,128)(2,1)S(1)}, u32[]{:S(2)}, u32[]{:S(2)}) collective-permute-start(bf16[2,64,32,128]{3,2,1,0:T(8,128)(2,1)} %get-tuple-element.28), channel_id=1, source_target_pairs={{0,2},{2,0},{4,6},{6,4},{1,3},{3,1},{5,7},{7,5},{8,10},{10,8},{12,... | collective-permute-start | bytes 3145736 | tf_op jit(solution)/shard_map/ppermute | solution.py:21
  10.7 1.7 %copy-start = (bf16[2,128,5120]{2,1,0:T(8,128)(2,1)S(1)}, bf16[2,128,5120]{2,1,0:T(8,128)(2,1)}, u32[]{:S(2)}) copy-start(bf16[2,128,5120]{2,1,0:T(8,128)(2,1)} %hidden.3) | copy-start | bytes 7864324
  12.4 0.9 %copy-start.5 = (bf16[160,256]{1,0:T(8,128)(2,1)S(1)}, bf16[160,256]{1,0:T(8,128)(2,1)}, u32[]{:S(2)}) copy-start(bf16[160,256]{1,0:T(8,128)(2,1)} %get-tuple-element.22.after.own) | copy-start | bytes 245764
  13.3 8.9 %copy-start.4 = (bf16[384,640]{1,0:T(8,128)(2,1)S(1)}, bf16[384,640]{1,0:T(8,128)(2,1)}, u32[]{:S(2)}) copy-start(bf16[384,640]{1,0:T(8,128)(2,1)} %get-tuple-element.25.refs_0_) | copy-start | bytes 1474564
  13.3 18.8 %copy-start.6 = (bf16[160,256]{1,0:T(8,128)(2,1)S(1)}, bf16[160,256]{1,0:T(8,128)(2,1)}, u32[]{:S(2)}) copy-start(bf16[160,256]{1,0:T(8,128)(2,1)} %get-tuple-element.24.own) | copy-start | bytes 245764
  22.1 10.9 %collective-permute-start.9 = (bf16[768,640]{1,0:T(8,128)(2,1)S(1)}, bf16[768,640]{1,0:T(8,128)(2,1)S(1)}, u32[]{:S(2)}, u32[]{:S(2)}) collective-permute-start(bf16[768,640]{1,0:T(8,128)(2,1)S(1)} %get-tuple-element.34.refs_1_), channel_id=1, source_target_pairs={{0,1},{1,0},{2,3},{3,2},{4,5},{5,4},{6,7},{7,6},{8,9},{9,8},{10,11... | collective-permute-start | bytes 2949128 | tf_op jit(solution)/shard_map/ppermute | solution.py:21
  22.2 10.0 %collective-permute-start.8 = (bf16[384,640]{1,0:T(8,128)(2,1)S(1)}, bf16[384,640]{1,0:T(8,128)(2,1)S(1)}, u32[]{:S(2)}, u32[]{:S(2)}) collective-permute-start(bf16[384,640]{1,0:T(8,128)(2,1)S(1)} %copy-done.4), channel_id=1, source_target_pairs={{0,1},{1,0},{2,3},{3,2},{4,5},{5,4},{6,7},{7,6},{8,9},{9,8},{10,11... | collective-permute-start | bytes 1474568 | tf_op jit(solution)/shard_map/ppermute | solution.py:21
  22.7 8.0 %collective-permute-start.10 = (bf16[192,640]{1,0:T(8,128)(2,1)S(1)}, bf16[192,640]{1,0:T(8,128)(2,1)S(1)}, u32[]{:S(2)}, u32[]{:S(2)}) collective-permute-start(bf16[192,640]{1,0:T(8,128)(2,1)S(1)} %get-tuple-element.27.after), channel_id=1, source_target_pairs={{0,16},{8,24},{16,0},{24,8},{1,17},{9,25},{17,1},{25,9},{2,18},{10... | collective-permute-start | bytes 737288 | tf_op jit(solution)/shard_map/ppermute | solution.py:21
  24.5 7.7 %collective-permute-start.11 = (bf16[192,640]{1,0:T(8,128)(2,1)S(1)}, bf16[192,640]{1,0:T(8,128)(2,1)S(1)}, u32[]{:S(2)}, u32[]{:S(2)}) collective-permute-start(bf16[192,640]{1,0:T(8,128)(2,1)S(1)} %get-tuple-element.36), channel_id=1, source_target_pairs={{0,8},{8,0},{16,24},{24,16},{1,9},{9,1},{17,25},{25,17},{2,10},{10... | collective-permute-start | bytes 737288 | tf_op jit(solution)/shard_map/ppermute | solution.py:21
  30.7 3.7 %collective-permute-start.12 = (bf16[192,640]{1,0:T(8,128)(2,1)S(1)}, bf16[192,640]{1,0:T(8,128)(2,1)S(1)}, u32[]{:S(2)}, u32[]{:S(2)}) collective-permute-start(bf16[192,640]{1,0:T(8,128)(2,1)S(1)} %collective-permute-done.10.refs_0_), channel_id=1, source_target_pairs={{0,1},{1,0},{2,3},{3,2},{4,5},{5,4},{6,7},{7,6},{8,9},{9,8},{10,11... | collective-permute-start | bytes 737288 | tf_op jit(solution)/shard_map/ppermute | solution.py:21
  32.1 2.3 %collective-permute-start.13 = (bf16[192,640]{1,0:T(8,128)(2,1)S(1)}, bf16[192,640]{1,0:T(8,128)(2,1)S(1)}, u32[]{:S(2)}, u32[]{:S(2)}) collective-permute-start(bf16[192,640]{1,0:T(8,128)(2,1)S(1)} %collective-permute-done.11.refs_1_), channel_id=1, source_target_pairs={{0,1},{1,0},{2,3},{3,2},{4,5},{5,4},{6,7},{7,6},{8,9},{9,8},{10,11... | collective-permute-start | bytes 737288 | tf_op jit(solution)/shard_map/ppermute | solution.py:21
  32.2 6.7 %collective-permute-start.3 = (bf16[320,256]{1,0:T(8,128)(2,1)S(1)}, bf16[320,256]{1,0:T(8,128)(2,1)S(1)}, u32[]{:S(2)}, u32[]{:S(2)}) collective-permute-start(bf16[320,256]{1,0:T(8,128)(2,1)S(1)} %relay.1), channel_id=1, source_target_pairs={{0,16},{8,24},{16,0},{24,8},{1,17},{9,25},{17,1},{25,9},{2,18},{10... | collective-permute-start | bytes 491528 | tf_op jit(solution)/shard_map/ppermute | solution.py:21
  33.0 1.4 %copy-start.9 = (bf16[2,64]{1,0:T(2,128)(2,1)S(1)}, bf16[2,64]{1,0:T(2,128)(2,1)}, u32[]{:S(2)}) copy-start(bf16[2,64]{1,0:T(2,128)(2,1)} %kvb.1) | copy-start | bytes 772
  34.4 9.0 %copy-start.2 = (bf16[128,1,32,128]{3,2,1,0:T(8,128)(2,1)S(1)}, bf16[128,1,32,128]{3,2,1,0:T(8,128)(2,1)}, u32[]{:S(2)}) copy-start(bf16[128,1,32,128]{3,2,1,0:T(8,128)(2,1)} %param.29) | copy-start | bytes 3145732
  34.4 9.0 %copy-start.3 = (bf16[128,1,32,128]{3,2,1,0:T(8,128)(2,1)S(1)}, bf16[128,1,32,128]{3,2,1,0:T(8,128)(2,1)}, u32[]{:S(2)}) copy-start(bf16[128,1,32,128]{3,2,1,0:T(8,128)(2,1)} %param.30) | copy-start | bytes 3145732
  35.1 8.3 %collective-permute-start.14 = (bf16[2,64,512]{2,1,0:T(8,128)(2,1)S(1)}, bf16[2,64,512]{2,1,0:T(8,128)(2,1)S(1)}, u32[]{:S(2)}, u32[]{:S(2)}) collective-permute-start(bf16[2,64,512]{2,1,0:T(8,128)(2,1)S(1)} %get-tuple-element.38), channel_id=1, source_target_pairs={{0,2},{2,0},{4,6},{6,4},{1,3},{3,1},{5,7},{7,5},{8,10},{10,8},{12,... | collective-permute-start | bytes 393224 | tf_op jit(solution)/shard_map/ppermute | solution.py:21
  38.9 6.8 %collective-permute-start.5 = (bf16[160,256]{1,0:T(8,128)(2,1)S(1)}, bf16[160,256]{1,0:T(8,128)(2,1)S(1)}, u32[]{:S(2)}, u32[]{:S(2)}) collective-permute-start(bf16[160,256]{1,0:T(8,128)(2,1)S(1)} %get-tuple-element.30), channel_id=1, source_target_pairs={{0,2},{2,0},{4,6},{6,4},{1,3},{3,1},{5,7},{7,5},{8,10},{10,8},{12,... | collective-permute-start | bytes 245768 | tf_op jit(solution)/shard_map/ppermute | solution.py:21
  40.6 9.1 %collective-permute-start.6 = (bf16[160,256]{1,0:T(8,128)(2,1)S(1)}, bf16[160,256]{1,0:T(8,128)(2,1)S(1)}, u32[]{:S(2)}, u32[]{:S(2)}) collective-permute-start(bf16[160,256]{1,0:T(8,128)(2,1)S(1)} %get-tuple-element.31), channel_id=1, source_target_pairs={{0,4},{2,6},{4,0},{6,2},{1,5},{3,7},{5,1},{7,3},{8,12},{10,14},{12... | collective-permute-start | bytes 245768 | tf_op jit(solution)/shard_map/ppermute | solution.py:21
  43.2 6.5 %collective-permute-start.7 = (bf16[160,256]{1,0:T(8,128)(2,1)S(1)}, bf16[160,256]{1,0:T(8,128)(2,1)S(1)}, u32[]{:S(2)}, u32[]{:S(2)}) collective-permute-start(bf16[160,256]{1,0:T(8,128)(2,1)S(1)} %get-tuple-element.32), channel_id=1, source_target_pairs={{0,6},{2,4},{4,2},{6,0},{1,7},{3,5},{5,3},{7,1},{8,14},{10,12},{12... | collective-permute-start | bytes 245768 | tf_op jit(solution)/shard_map/ppermute | solution.py:21
  49.7 16.2 %collective-permute-start.15 = (bf16[640,256]{1,0:T(8,128)(2,1)S(1)}, bf16[640,256]{1,0:T(8,128)(2,1)S(1)}, u32[]{:S(2)}, u32[]{:S(2)}) collective-permute-start(bf16[640,256]{1,0:T(8,128)(2,1)S(1)} %stack.2.refs_0_), channel_id=1, source_target_pairs={{0,8},{8,0},{16,24},{24,16},{1,9},{9,1},{17,25},{25,17},{2,10},{10... | collective-permute-start | bytes 983048 | tf_op jit(solution)/shard_map/ppermute | solution.py:21
  51.3 14.6 %collective-permute-start.16 = (bf16[640,256]{1,0:T(8,128)(2,1)S(1)}, bf16[640,256]{1,0:T(8,128)(2,1)S(1)}, u32[]{:S(2)}, u32[]{:S(2)}) collective-permute-start(bf16[640,256]{1,0:T(8,128)(2,1)S(1)} %stack.2.refs_0_), channel_id=1, source_target_pairs={{0,16},{8,24},{16,0},{24,8},{1,17},{9,25},{17,1},{25,9},{2,18},{10... | collective-permute-start | bytes 983048 | tf_op jit(solution)/shard_map/ppermute | solution.py:21
  51.8 14.0 %collective-permute-start.17 = (bf16[640,256]{1,0:T(8,128)(2,1)S(1)}, bf16[640,256]{1,0:T(8,128)(2,1)S(1)}, u32[]{:S(2)}, u32[]{:S(2)}) collective-permute-start(bf16[640,256]{1,0:T(8,128)(2,1)S(1)} %stack.2.refs_0_), channel_id=1, source_target_pairs={{0,24},{8,16},{16,8},{24,0},{1,25},{9,17},{17,9},{25,1},{2,26},{10... | collective-permute-start | bytes 983048 | tf_op jit(solution)/shard_map/ppermute | solution.py:21
  53.3 5.2 %collective-permute-start.18 = (bf16[2,64,512]{2,1,0:T(8,128)(2,1)S(1)}, bf16[2,64,512]{2,1,0:T(8,128)(2,1)S(1)}, u32[]{:S(2)}, u32[]{:S(2)}) collective-permute-start(bf16[2,64,512]{2,1,0:T(8,128)(2,1)S(1)} %attend.1.refs_4_.a0), channel_id=1, source_target_pairs={{0,2},{2,0},{4,6},{6,4},{1,3},{3,1},{5,7},{7,5},{8,10},{10,8},{12,... | collective-permute-start | bytes 393224 | tf_op jit(solution)/shard_map/ppermute | solution.py:21
  54.7 11.2 %collective-permute-start.19 = (bf16[2,64,512]{2,1,0:T(8,128)(2,1)S(1)}, bf16[2,64,512]{2,1,0:T(8,128)(2,1)S(1)}, u32[]{:S(2)}, u32[]{:S(2)}) collective-permute-start(bf16[2,64,512]{2,1,0:T(8,128)(2,1)S(1)} %attend.1.refs_4_.a0), channel_id=1, source_target_pairs={{0,4},{2,6},{4,0},{6,2},{1,5},{3,7},{5,1},{7,3},{8,12},{10,14},{12... | collective-permute-start | bytes 393224 | tf_op jit(solution)/shard_map/ppermute | solution.py:21
  58.4 7.4 %collective-permute-start.20 = (bf16[2,64,512]{2,1,0:T(8,128)(2,1)S(1)}, bf16[2,64,512]{2,1,0:T(8,128)(2,1)S(1)}, u32[]{:S(2)}, u32[]{:S(2)}) collective-permute-start(bf16[2,64,512]{2,1,0:T(8,128)(2,1)S(1)} %attend.1.refs_4_.a0), channel_id=1, source_target_pairs={{0,6},{2,4},{4,2},{6,0},{1,7},{3,5},{5,3},{7,1},{8,14},{10,12},{12... | collective-permute-start | bytes 393224 | tf_op jit(solution)/shard_map/ppermute | solution.py:21
  65.9 3.4 %copy-start.1 = (bf16[2,128,5120]{2,1,0:T(8,128)(2,1)S(1)}, bf16[2,128,5120]{2,1,0:T(8,128)(2,1)}, u32[]{:S(2)}) copy-start(bf16[2,128,5120]{2,1,0:T(8,128)(2,1)} %hidden.3) | copy-start | bytes 7864324
  66.0 3.1 %collective-permute-start.22 = (bf16[1920,256]{1,0:T(8,128)(2,1)S(1)}, bf16[1920,256]{1,0:T(8,128)(2,1)S(1)}, u32[]{:S(2)}, u32[]{:S(2)}) collective-permute-start(bf16[1920,256]{1,0:T(8,128)(2,1)S(1)} %stack.3.refs_1_), channel_id=1, source_target_pairs={{0,1},{1,0},{2,3},{3,2},{4,5},{5,4},{6,7},{7,6},{8,9},{9,8},{10,11... | collective-permute-start | bytes 2949128 | tf_op jit(solution)/shard_map/ppermute | solution.py:21
  66.0 3.0 %collective-permute-start.21 = (bf16[640,256]{1,0:T(8,128)(2,1)S(1)}, bf16[640,256]{1,0:T(8,128)(2,1)S(1)}, u32[]{:S(2)}, u32[]{:S(2)}) collective-permute-start(bf16[640,256]{1,0:T(8,128)(2,1)S(1)} %stack.2.refs_0_), channel_id=1, source_target_pairs={{0,1},{1,0},{2,3},{3,2},{4,5},{5,4},{6,7},{7,6},{8,9},{9,8},{10,11... | collective-permute-start | bytes 983048 | tf_op jit(solution)/shard_map/ppermute | solution.py:21

commit v3 on v2

--- a/solution.py
+++ b/solution.py
@@ -66,50 +66,54 @@
 def begin_kernel(
     sliced, parts, qw, kvw, ow, qd, kvd, od, kc, vc, qe, kve, oe, fresh, far, *refs
 ):
-    outs, (qw_v, kvw_v, ow_v, qd_v, kvd_v, od_v, sem) = refs[:parts], refs[parts:]
+    outs, refs = refs[:parts], refs[parts:]
+    qw_v, kvw_v, ow_v, qd_v, kvd_v, od_v, fresh_v, far_v, o_v, sem = refs
     rows, width = qd.shape
     cols = pl.ds(0 if sliced else pl.multiple_of(shard_index() * width, 128), width)
     far_rows = pl.ds(half_rows(1, far.shape[1]), far.shape[1])
     o_rows = od.shape[0]
     place = pl.ds(pl.multiple_of(shard_index() * o_rows, 16), o_rows)
-    loads = [
-        pltpu.make_async_copy(src, dst, sem.at[n])
-        for n, (src, dst) in enumerate(
-            [
-                (qw.at[:, cols], qw_v),
-                (qd, qd_v),
-                (kvw.at[:, :, cols], kvw_v),
-                (kvd, kvd_v),
-                (ow.at[place], ow_v),
-                (od, od_v),
-                (kc.at[far_rows], far.at[0]),
-                (vc.at[far_rows], far.at[1]),
-            ]
-        )
-    ]
-    for load in loads:
-        load.start()
-    loads[0].wait()
-    loads[1].wait()
-    fresh[:rows] = refreshed(qw_v[...], qd_v[...], qe[...])
-    loads[2].wait()
-    loads[3].wait()
+    copies = []
+
+    def copy(src, dst):
+        copies.append(pltpu.make_async_copy(src, dst, sem.at[len(copies)]))
+        copies[-1].start()
+
+    copy(qw.at[:, cols], qw_v)
+    copy(qd, qd_v)
+    copy(kvw.at[:, :, cols], kvw_v)
+    copy(kvd, kvd_v)
+    copy(kc.at[far_rows], far_v.at[0])
+    copy(vc.at[far_rows], far_v.at[1])
+    copy(ow.at[place], ow_v)
+    copy(od, od_v)
+    copies[0].wait()
+    copies[1].wait()
+    fresh_v[:rows] = refreshed(qw_v[...], qd_v[...], qe[...])
+    copy(fresh_v.at[:rows], fresh.at[:rows])
+    copies[2].wait()
+    copies[3].wait()
     narrow = kvd.shape[1]
     for n in range(2):
         part = slice(rows + n * narrow, rows + (n + 1) * narrow)
-        fresh[part] = refreshed(kvw_v[n], kvd_v[n], kve[:, n, :])
-    loads[4].wait()
-    loads[5].wait()
-    result = refreshed(ow_v[...], od_v[...], oe[...])
+        fresh_v[part] = refreshed(kvw_v[n], kvd_v[n], kve[:, n, :])
+    copy(fresh_v.at[rows:], fresh.at[rows:])
+    copies[4].wait()
+    copies[5].wait()
+    copy(far_v, far)
+    copies[6].wait()
+    copies[7].wait()
+    o_v[...] = refreshed(ow_v[...], od_v[...], oe[...])
+    quarter = o_rows // 4
     if parts == 1:
-        outs[0][...] = result
+        copy(o_v, outs[0])
     else:
-        quarter = [result[n * o_rows // 4 : (n + 1) * o_rows // 4] for n in range(4)]
-        outs[0][...] = quarter[0]
-        outs[1][...] = jnp.concatenate([quarter[1], quarter[3]], axis=0)
-        outs[2][...] = quarter[2]
-    loads[6].wait()
-    loads[7].wait()
+        copy(o_v.at[:quarter], outs[0])
+        copy(o_v.at[quarter : 2 * quarter], outs[1].at[:quarter])
+        copy(o_v.at[3 * quarter :], outs[1].at[quarter:])
+        copy(o_v.at[2 * quarter : 3 * quarter], outs[2])
+    for done in copies[8:]:
+        done.wait()
 
 
 def begin(
@@ -124,19 +128,21 @@
         q_weight = lax.dynamic_slice_in_dim(q_weight, start, width, 1)
         kv_weight = lax.dynamic_slice_in_dim(kv_weight, start, width, 2)
     sizes = (4,) if parts == 1 else (1, 2, 1)
+    fresh = sds((rows + 2 * narrow, width), BF16)
+    far = sds((2, keys.shape[0] // 2) + keys.shape[1:], BF16)
     pair = lambda a: [pltpu.VMEM(a.shape, BF16)]
     return call(
         functools.partial(begin_kernel, sliced, parts),
         "begin",
         BEGIN_MIB,
-        out_shape=(
-            sds((rows + 2 * narrow, width), BF16),
-            sds((2, keys.shape[0] // 2) + keys.shape[1:], BF16),
-        )
+        out_shape=(fresh, far)
         + tuple(sds((o_delta.shape[0] * n // 4, o_delta.shape[1]), BF16) for n in sizes),
         in_specs=[HBM] * 8 + [VMEM] * 3,
-        out_specs=(VMEM,) * (2 + parts),
-        scratch_shapes=(pair(q_delta) + pair(kv_delta) + pair(o_delta)) * 2 + [DMA((8,))],
+        out_specs=(ANY,) * (2 + parts),
+        scratch_shapes=(pair(q_delta) + pair(kv_delta) + pair(o_delta)) * 2
+        + [pltpu.VMEM(fresh.shape, BF16), pltpu.VMEM(far.shape, BF16)]
+        + pair(o_delta)
+        + [DMA((15,))],
     )(
         q_weight, kv_weight, o_weight, q_delta, kv_delta, o_delta, keys, values,
         q_exp.T, kv_exp.transpose(2, 0, 1), o_exp.T,
@@ -195,12 +201,10 @@
 
 
 def halves_kernel(along_x, along_y, *refs):
-    first, second, both = refs[-3:]
-    rows = along_x.shape[0]
-    first[...] = along_x[: rows // 2]
-    second[...] = along_y[rows // 2 :]
-    both[:rows] = along_x[...]
-    both[rows:] = along_y[...]
+    first, second = refs[-2:]
+    half = first.shape[0]
+    first[...] = along_x[:half]
+    second[...] = along_y[half:]
 
 
 def halves(along_x, along_y, after):
@@ -210,9 +214,9 @@
         halves_kernel,
         "halves",
         8,
-        out_shape=(out, out, sds((2 * rows, width), BF16)),
-        in_specs=[VMEM, VMEM] + [ANY] * len(after),
-        out_specs=(VMEM,) * 3,
+        out_shape=(out, out),
+        in_specs=[VMEM] * 2 + [ANY] * len(after),
+        out_specs=(VMEM,) * 2,
     )(along_x, along_y, *after)
 
 
@@ -223,22 +227,19 @@
     return nt_dot(normed[:, pl.ds(pl.multiple_of(owner * width, 128), width)], shard)
 
 
-def project_kernel(places, rows, normed, *refs):
-    total = None
-    for group, ref in zip(places, refs):
-        for n, place in enumerate(group):
-            part = term(place, normed, ref[n * rows : (n + 1) * rows])
-            total = part if total is None else total + part
+def project_kernel(places, normed, *refs):
+    total = term(places[0], normed, refs[0][...])
+    for place, ref in zip(places[1:], refs[1:]):
+        total += term(place, normed, ref[...])
     refs[-1][...] = total
 
 
 def project(places, normed, shards):
-    rows = shards[0].shape[0]
-    return call(
-        functools.partial(project_kernel, places, rows),
+    return call(
+        functools.partial(project_kernel, places),
         "project",
         16,
-        out_shape=sds((normed.shape[0], rows), F32),
+        out_shape=sds((normed.shape[0], shards[0].shape[0]), F32),
         in_specs=[VMEM] * (1 + len(shards)),
         out_specs=VMEM,
     )(normed, *shards)
@@ -248,7 +249,7 @@
     own, other, packed = refs[-3:]
     total = total_in[...]
     for n, place in enumerate(places):
-        shard = jnp.concatenate([refs[2 * n][...], refs[2 * n + 1][...]], axis=0)
+        shard = refs[n][...]
         total += term(place, normed, shard)
     span = qb.shape[1]
     for head in range(span // HD):
@@ -421,7 +422,8 @@
     )(own, other, cosine, sine, swapped, lengths.reshape(1, -1), keys, values)
 
 
-def relay_kernel(own, along_x, after, out):
+def relay_kernel(own, along_x, *refs):
+    out = refs[-1]
     rows = own.shape[0]
     out[:rows] = own[...]
     out[rows:] = along_x[rows:]
@@ -433,9 +435,9 @@
         "relay",
         8,
         out_shape=sds(along_x.shape, BF16),
-        in_specs=[VMEM] * 2 + [ANY],
+        in_specs=[VMEM] * 2 + [ANY] * len(after),
         out_specs=VMEM,
-    )(own, along_x, after)
+    )(own, along_x, *after)
 
 
 def pick_kernel(own, along_x, along_y, *refs):
@@ -462,18 +464,21 @@
 
 
 def stack_kernel(*refs):
-    rows = refs[0].shape[0]
-    for n, ref in enumerate(refs[: refs[-1].shape[0] // rows]):
-        refs[-1][n * rows : (n + 1) * rows] = ref[...]
+    place = 0
+    for ref in refs[:-1]:
+        rows = ref.shape[0]
+        if place < refs[-1].shape[0]:
+            refs[-1][place : place + rows] = ref[...]
+        place += rows
 
 
 def stack(blocks, after):
-    rows, width = blocks[0].shape
+    rows, width = sum(b.shape[0] for b in blocks), blocks[0].shape[1]
     return call(
         stack_kernel,
         "stack",
         8,
-        out_shape=sds((len(blocks) * rows, width), BF16),
+        out_shape=sds((rows, width), BF16),
         in_specs=[VMEM] * len(blocks) + [ANY] * len(after),
         out_specs=VMEM,
     )(*blocks, *after)
@@ -481,10 +486,12 @@
 
 def assemble_kernel(*refs):
     weight = refs[-1]
+    count = (len(refs) - 1) // 2
     rows, width = refs[0].shape[0] // 4, refs[0].shape[1]
     for j in range(2):
-        for i in range(4):
-            shard, first = refs[2 * j + min(i, 1)], max(i - 1, 0) * 4
+        shards = refs[j * count : (j + 1) * count]
+        blocks = [(ref, n * 4) for ref in shards for n in range(ref.shape[0] // (4 * rows))]
+        for i, (shard, first) in enumerate(blocks):
             quarter = lax.axis_index("fsdp") ^ i ^ lax.axis_index("tp")
             place = ((lax.axis_index("rep") ^ j) * 4 + quarter) * rows
             for k in range(4):
@@ -493,8 +500,9 @@
                 )
 
 
-def assemble(*shards):
-    rows, width = shards[0].shape
+def assemble(own, across):
+    rows, width = own[0].shape
+    shards = [*own, *across]
     return call(
         assemble_kernel,
         "assemble",
@@ -505,28 +513,37 @@
     )(*shards)
 
 
-def output_kernel(weight, a0, a1, a2, a3, hidden, out, hidden_v, sem):
+def output_kernel(weight, a0, a1, a2, a3, hidden, out, hidden_v, out_v, load_sem, store_sem):
     width = weight.shape[1] // 4
     steps, half = a0.shape[:2]
     cols = out.shape[2]
     place = pl.ds(pl.multiple_of(lax.axis_index("tp") * cols, 128), cols)
-    load = pltpu.make_async_copy(hidden.at[:, :, place], hidden_v, sem)
+    load = pltpu.make_async_copy(hidden.at[:, :, place], hidden_v, load_sem)
     load.start()
     flat = lambda ref: ref[...].reshape(steps * half, 2 * width)
-    b1, b3 = flat(a1), flat(a3)
-    top = nt_dot(flat(a0), weight[:, : 2 * width]) + nt_dot(flat(a2), weight[:, 2 * width :])
-    low = (
-        nt_dot(b1[:, :width], weight[:, width : 2 * width])
-        + nt_dot(b1[:, width:], weight[:, :width])
-        + nt_dot(b3[:, :width], weight[:, 3 * width :])
-        + nt_dot(b3[:, width:], weight[:, 2 * width : 3 * width])
-    )
-    load.wait()
-    for which, total in ((0, top), (1, low)):
-        for s in range(steps):
-            at = pl.ds(half_rows(which, half), half)
-            mixed = total[s * half : (s + 1) * half]
-            out[s, at, :] = (hidden_v[s, at, :].astype(F32) + mixed).astype(BF16)
+    turned = lambda ref: jnp.concatenate([flat(ref)[:, width:], flat(ref)[:, :width]], axis=1)
+    near = jnp.concatenate([flat(a0), flat(a2)], axis=1)
+    far = jnp.concatenate([turned(a1), turned(a3)], axis=1)
+    features = jnp.concatenate([near, far], axis=0)
+    tile = cols // store_sem.shape[0]
+    stores = []
+    for n in range(store_sem.shape[0]):
+        part = slice(n * tile, (n + 1) * tile)
+        total = nt_dot(features, weight[part])
+        if n == 0:
+            load.wait()
+        for which in range(2):
+            for s in range(steps):
+                at = pl.ds(half_rows(which, half), half)
+                first = (which * steps + s) * half
+                mixed = total[first : first + half]
+                out_v[s, at, part] = (hidden_v[s, at, part].astype(F32) + mixed).astype(BF16)
+        stores.append(
+            pltpu.make_async_copy(out_v.at[:, :, part], out.at[:, :, part], store_sem.at[n])
+        )
+        stores[-1].start()
+    for store in stores:
+        store.wait()
 
 
 def output(weight, parts, hidden):
@@ -538,8 +555,13 @@
         24,
         out_shape=sds(shape, BF16),
         in_specs=[VMEM] * (1 + len(parts)) + [HBM],
-        out_specs=VMEM,
-        scratch_shapes=[pltpu.VMEM(shape, BF16), DMA],
+        out_specs=ANY,
+        scratch_shapes=[
+            pltpu.VMEM(shape, BF16),
+            pltpu.VMEM(shape, BF16),
+            DMA,
+            DMA((max(1, shape[2] // 256),)),
+        ],
     )(weight, *parts, hidden)
 
 
@@ -580,14 +602,13 @@
     if small:
         along_x, along_y = swap(fresh, "fsdp", 1), swap(fresh, "fsdp", 2)
         o_x = swap(o_parts[1], "fsdp", 1)
-        first, second, both = halves(along_x, along_y, [cosine, o_x])
-        last = [swap(first, "fsdp", 2), swap(second, "fsdp", 1)]
-        o_parts = [o_parts[0], o_x, swap(relay(o_parts[2], o_x, first), "fsdp", 2)]
-        near = [fresh, both]
+        first, second = halves(along_x, along_y, [cosine])
+        last = stack([swap(first, "fsdp", 2), swap(second, "fsdp", 1)], [])
+        o_y = swap(relay(o_parts[2], o_x, [first]), "fsdp", 2)
+        near = [fresh, along_x, along_y]
         near += [swap(a, "rep", 1) for a in near]
-        last += [swap(a, "rep", 1) for a in last]
-        places = [[(0, 0)], [(1, 0), (2, 0)], [(0, 1)], [(1, 1), (2, 1)]]
-        total = project(places, normed, near)
+        total = project([(i, j) for j in (0, 1) for i in (0, 1, 2)], normed, near)
+        last = [last, swap(last, "rep", 1)]
         own, other = finish(
             [(3, 0), (3, 1)], steps, normed, total, q_bias, kv_bias, cosine, sine, last
         )
@@ -600,12 +621,12 @@
     attention = attend(own, received, cosine, sine, swapped, cache_lengths, keys, values)
 
     if small:
-        picked = pick(*o_parts, [swapped])
-        o_parts = [picked[0]] + [swap(picked[k], "tp", k) for k in (1, 2, 3)]
+        picked = pick(o_parts[0], o_x, o_y, [swapped])
+        blocks = [picked[0]] + [swap(picked[k], "tp", k) for k in (1, 2, 3)]
+        stacked = stack(blocks, [own])
         parts = [attention] + [swap(attention, "tp", k) for k in (1, 2, 3)]
-        stacked = stack(o_parts, [attention])
         others = stack([swap(stacked, "fsdp", i) for i in (1, 2, 3)], parts[1:])
-        weight = assemble(stacked, others, swap(stacked, "rep", 1), swap(others, "rep", 1))
+        weight = assemble([stacked, others], [swap(stacked, "rep", 1), swap(others, "rep", 1)])
         return output(weight, parts, hidden_in)
 
     full_o = lax.all_gather(o_parts[0], FR, axis=0, tiled=True)

time: 72.5 us -> 68.8 us (0.949)
  starting transfers between devices: 27.8 us -> 21.3 us
  waiting for transfers between devices: 26.6 us -> 30.8 us
  Pallas kernels: 14.8 us -> 13.6 us
    ppermute x23, starting transfers between devices: 27.8 us -> 21.3 us  [swap(): lax.ppermute(x, axis, [(i, i ^ xor) for i in range(lax.axis_size(axis))])]
    ppermute x23, waiting for transfers between devices: 26.6 us -> 30.8 us  [swap(): lax.ppermute(x, axis, [(i, i ^ xor) for i in range(lax.axis_size(axis))])]
    pallas_call x1, Pallas kernels: 2.83 us -> 1.9 us  [output(): call(output_kernel, 'output', 24, out_shape=sds(shape, BF16), in_specs=[V...]
    pallas_call x4 -> x5, Pallas kernels: 1.53 us -> 1.53 us  [the longest x1 1.36 us: project(): call(functools.partial(project_kernel, places), 'project', 16, out_shape=...]
    unnamed x22 -> x24, local copies, waits for them, and re-layouts: 2.67 us -> 2.68 us
  transfers between devices with their start and end apart: 23 -> 23, of which waited for: 8 -> 12; matrix products, arithmetic and copies ran while one was open for 0% -> 0% of each run, Pallas kernels for 11% -> 11%
where the time goes in v3:
time: 68.8 us; the launch traced here: 68.6 us
  waiting for transfers between devices  30.8 us (45%)
  starting transfers between devices  21.3 us (31%)
  Pallas kernels  13.6 us (20%)
  local copies, waits for them, and re-layouts  2.68 us (4%)
    ppermute x23, waiting for transfers between devices, swap(): lax.ppermute(x, axis, [(i, i ^ xor) for i in range(lax.axis_size(axis))])  30.8 us
    ppermute x23, starting transfers between devices, swap(): lax.ppermute(x, axis, [(i, i ^ xor) for i in range(lax.axis_size(axis))])  21.3 us
    pallas_call x1, Pallas kernels, begin(): call(functools.partial(begin_kernel, sliced, parts), 'begin', BEGIN_MIB,...  3.66 us
    pallas_call x1, Pallas kernels, prepare(): call(prepare_kernel, 'prepare', 16, weight=10 * MB, out_shape=(sds((steps...  3.06 us
    unnamed x24, local copies, waits for them, and re-layouts  2.68 us
    pallas_call x1, Pallas kernels, attend(): call(attend_kernel, 'attend', 24, out_shape=sds((steps, rows, 2 * (width...  2.3 us
    pallas_call x1, Pallas kernels, output(): call(output_kernel, 'output', 24, out_shape=sds(shape, BF16), in_specs=[V...  1.9 us
  transfers between devices with their start and end apart: 23, of which 12 were waited for; matrix products, arithmetic and copies ran while one was open for 0% of the time, Pallas kernels for 11%

profile of v3, /device:TPU:0, one launch (start us, length us, event | category | flops | bytes accessed | tf_op | source)
XLA Modules:
  0.0 68.6 jit_solution(10873942813531201165)
XLA Ops:
  0.0 3.7 %begin.1 = (bf16[384,640]{1,0:T(8,128)(2,1)}, bf16[2,64,32,128]{3,2,1,0:T(8,128)(2,1)}, bf16[160,256]{1,0:T(8,128)(2,1)}, bf16[320,256]{1,0:T(8,128)(2,1)}, bf16[160,256]{1,0:T(8,128)(2,1)}) custom-call(bf16[256,5120]{1,0:T(8,128)(2,1)} %qw.1, bf16[2,64,5120]{2,1,0:T(8,128)(2,1)} %kvw.1, bf16[5120,256]{1,0:T(8,128)(2,1)} %ow.1, bf16[256,640]{1,0:T(8,128)(2,1)} %qd.1, ...), custom_call_target="tpu_custom_call" | custom-call | flops 1024 | bytes 1024 | tf_op jit(solution)/shard_map/begin/pallas_call | solution.py:134
  3.7 3.0 %collective-permute-start.2 = (bf16[384,640]{1,0:T(8,128)(2,1)}, bf16[384,640]{1,0:T(8,128)(2,1)S(1)}, u32[]{:S(2)}, u32[]{:S(2)}) collective-permute-start(bf16[384,640]{1,0:T(8,128)(2,1)} %get-tuple-element.24.refs_0_), channel_id=1, source_target_pairs={{0,16},{8,24},{16,0},{24,8},{1,17},{9,25},{17,1},{25,9},{2,18},{10... | collective-permute-start | bytes 1474568 | tf_op jit(solution)/shard_map/ppermute | solution.py:21
  6.7 1.5 %collective-permute-start.1 = (bf16[384,640]{1,0:T(8,128)(2,1)}, bf16[384,640]{1,0:T(8,128)(2,1)S(1)}, u32[]{:S(2)}, u32[]{:S(2)}) collective-permute-start(bf16[384,640]{1,0:T(8,128)(2,1)} %get-tuple-element.24.refs_0_), channel_id=1, source_target_pairs={{0,8},{8,0},{16,24},{24,16},{1,9},{9,1},{17,25},{25,17},{2,10},{10... | collective-permute-start | bytes 1474568 | tf_op jit(solution)/shard_map/ppermute | solution.py:21
  8.2 1.6 %collective-permute-start.4 = (bf16[2,64,32,128]{3,2,1,0:T(8,128)(2,1)}, bf16[2,64,32,128]{3,2,1,0:T(8,128)(2,1)S(1)}, u32[]{:S(2)}, u32[]{:S(2)}) collective-permute-start(bf16[2,64,32,128]{3,2,1,0:T(8,128)(2,1)} %get-tuple-element.27), channel_id=1, source_target_pairs={{0,2},{2,0},{4,6},{6,4},{1,3},{3,1},{5,7},{7,5},{8,10},{10,8},{12,... | collective-permute-start | bytes 3145736 | tf_op jit(solution)/shard_map/ppermute | solution.py:21
  9.8 0.5 collective-permute-start
  10.3 1.7 %copy-done = bf16[2,128,5120]{2,1,0:T(8,128)(2,1)S(1)} copy-done((bf16[2,128,5120]{2,1,0:T(8,128)(2,1)S(1)}, bf16[2,128,5120]{2,1,0:T(8,128)(2,1)}, u32[]{:S(2)}) %copy-start) | copy-done | bytes 2621464
  12.1 0.9 %copy-done.5 = bf16[160,256]{1,0:T(8,128)(2,1)S(1)} copy-done((bf16[160,256]{1,0:T(8,128)(2,1)S(1)}, bf16[160,256]{1,0:T(8,128)(2,1)}, u32[]{:S(2)}) %copy-start.5) | copy-done | bytes 81944
  13.0 3.1 %prepare.1 = (bf16[256,5120]{1,0:T(8,128)(2,1)S(1)}, f32[256,128]{1,0:T(8,128)S(1)}, f32[256,128]{1,0:T(8,128)S(1)}) custom-call(bf16[2,128,5120]{2,1,0:T(8,128)(2,1)S(1)} %copy-done, f32[1,5120]{1,0:T(1,128)S(1)} %bitcast.11, s32[1,128]{1,0:T(1,128)S(1)} %bitcast.12, bf16[160,256]{1,0:T(8,128)(2,1)S(1)} %copy-done.5), custom_call_target="tpu_custom_call" | custom-call | flops 1024 | bytes 10485760 | tf_op jit(solution)/shard_map/prepare/pallas_call | solution.py:187
  16.0 0.0 copy-start.11
  16.0 2.1 %collective-permute-done.2.along_y.refs_2_ = bf16[384,640]{1,0:T(8,128)(2,1)S(1)} collective-permute-done((bf16[384,640]{1,0:T(8,128)(2,1)}, bf16[384,640]{1,0:T(8,128)(2,1)S(1)}, u32[]{:S(2)}, u32[]{:S(2)}) %collective-permute-start.2) | collective-permute-done | bytes 491552 | tf_op jit(solution)/shard_map/ppermute | solution.py:21
  18.1 2.9 %collective-permute-done.1.along_x.refs_1_ = bf16[384,640]{1,0:T(8,128)(2,1)S(1)} collective-permute-done((bf16[384,640]{1,0:T(8,128)(2,1)}, bf16[384,640]{1,0:T(8,128)(2,1)S(1)}, u32[]{:S(2)}, u32[]{:S(2)}) %collective-permute-start.1) | collective-permute-done | bytes 491552 | tf_op jit(solution)/shard_map/ppermute | solution.py:21
  21.1 0.1 collective-permute-start.11
  21.2 2.0 %collective-permute-start.12 = (bf16[192,640]{1,0:T(8,128)(2,1)S(1)}, bf16[192,640]{1,0:T(8,128)(2,1)S(1)}, u32[]{:S(2)}, u32[]{:S(2)}) collective-permute-start(bf16[192,640]{1,0:T(8,128)(2,1)S(1)} %get-tuple-element.34), channel_id=1, source_target_pairs={{0,8},{8,0},{16,24},{24,16},{1,9},{9,1},{17,25},{25,17},{2,10},{10... | collective-permute-start | bytes 737288 | tf_op jit(solution)/shard_map/ppermute | solution.py:21
  23.2 1.4 %collective-permute-done.along_x = bf16[320,256]{1,0:T(8,128)(2,1)S(1)} collective-permute-done((bf16[320,256]{1,0:T(8,128)(2,1)}, bf16[320,256]{1,0:T(8,128)(2,1)S(1)}, u32[]{:S(2)}, u32[]{:S(2)}) %collective-permute-start) | collective-permute-done | bytes 163872 | tf_op jit(solution)/shard_map/ppermute | solution.py:21
  24.6 0.2 collective-permute-start.3
  24.8 4.0 %collective-permute-done.11.refs_0_ = bf16[192,640]{1,0:T(8,128)(2,1)S(1)} collective-permute-done((bf16[192,640]{1,0:T(8,128)(2,1)S(1)}, bf16[192,640]{1,0:T(8,128)(2,1)S(1)}, u32[]{:S(2)}, u32[]{:S(2)}) %collective-permute-start.11) | collective-permute-done | bytes 245792 | tf_op jit(solution)/shard_map/ppermute | solution.py:21
  28.8 0.5 collective-permute-start.9
  29.4 1.2 %collective-permute-done.3.along_y = bf16[320,256]{1,0:T(8,128)(2,1)S(1)} collective-permute-done((bf16[320,256]{1,0:T(8,128)(2,1)S(1)}, bf16[320,256]{1,0:T(8,128)(2,1)S(1)}, u32[]{:S(2)}, u32[]{:S(2)}) %collective-permute-start.3) | collective-permute-done | bytes 163872 | tf_op jit(solution)/shard_map/ppermute | solution.py:21
  30.6 2.2 %collective-permute-done.4.refs_0_.swapped = bf16[2,64,32,128]{3,2,1,0:T(8,128)(2,1)S(1)} collective-permute-done((bf16[2,64,32,128]{3,2,1,0:T(8,128)(2,1)}, bf16[2,64,32,128]{3,2,1,0:T(8,128)(2,1)S(1)}, u32[]{:S(2)}, u32[]{:S(2)}) %collective-permute-start.4) | collective-permute-done | bytes 1048608 | tf_op jit(solution)/shard_map/ppermute | solution.py:21
  32.8 0.1 pick.1
  32.9 1.6 %collective-permute-start.5 = (bf16[160,256]{1,0:T(8,128)(2,1)S(1)}, bf16[160,256]{1,0:T(8,128)(2,1)S(1)}, u32[]{:S(2)}, u32[]{:S(2)}) collective-permute-start(bf16[160,256]{1,0:T(8,128)(2,1)S(1)} %get-tuple-element.29), channel_id=1, source_target_pairs={{0,2},{2,0},{4,6},{6,4},{1,3},{3,1},{5,7},{7,5},{8,10},{10,8},{12,... | collective-permute-start | bytes 245768 | tf_op jit(solution)/shard_map/ppermute | solution.py:21
  34.5 2.6 %collective-permute-start.6 = (bf16[160,256]{1,0:T(8,128)(2,1)S(1)}, bf16[160,256]{1,0:T(8,128)(2,1)S(1)}, u32[]{:S(2)}, u32[]{:S(2)}) collective-permute-start(bf16[160,256]{1,0:T(8,128)(2,1)S(1)} %get-tuple-element.30), channel_id=1, source_target_pairs={{0,4},{2,6},{4,0},{6,2},{1,5},{3,7},{5,1},{7,3},{8,12},{10,14},{12... | collective-permute-start | bytes 245768 | tf_op jit(solution)/shard_map/ppermute | solution.py:21
  37.1 0.2 collective-permute-start.7
  37.3 0.0 copy-start.10
  37.3 1.4 %project.1.total_in = f32[256,384]{1,0:T(8,128)S(1)} custom-call(bf16[256,5120]{1,0:T(8,128)(2,1)S(1)} %get-tuple-element.32.normed, bf16[384,640]{1,0:T(8,128)(2,1)S(1)} %copy-done.4, bf16[384,640]{1,0:T(8,128)(2,1)S(1)} %collective-permute-done.1.along_x.refs_1_, bf16[384,640]{1,0:T(8,128)(2,1)S(1)} %collective-permute-done.2.along_y.refs_2_, ...), custom_call_target="tpu_custom_call" | custom-call | flops 1024 | bytes 1024 | tf_op jit(solution)/shard_map/project/pallas_call | solution.py:238
  38.7 0.0 copy-start.2
  38.7 0.0 copy-start.3
  38.8 0.7 %finish.1 = (bf16[2,64,512]{2,1,0:T(8,128)(2,1)S(1)}, bf16[2,64,512]{2,1,0:T(8,128)(2,1)S(1)}) custom-call(bf16[256,5120]{1,0:T(8,128)(2,1)S(1)} %get-tuple-element.32.normed, f32[256,384]{1,0:T(8,128)S(1)} %project.1.total_in, bf16[1,256]{1,0:T(2,128)(2,1)S(1)} %reshape.12.qb, bf16[2,64]{1,0:T(2,128)(2,1)S(1)} %copy-done.10, ...), custom_call_target="tpu_custom_call" | custom-call | flops 1024 | bytes 1024 | tf_op jit(solution)/shard_map/finish/pallas_call | solution.py:278
  39.4 0.7 %collective-permute-start.17 = (bf16[2,64,512]{2,1,0:T(8,128)(2,1)S(1)}, bf16[2,64,512]{2,1,0:T(8,128)(2,1)S(1)}, u32[]{:S(2)}, u32[]{:S(2)}) collective-permute-start(bf16[2,64,512]{2,1,0:T(8,128)(2,1)S(1)} %get-tuple-element.36), channel_id=1, source_target_pairs={{0,2},{2,0},{4,6},{6,4},{1,3},{3,1},{5,7},{7,5},{8,10},{10,8},{12,... | collective-permute-start | bytes 393224 | tf_op jit(solution)/shard_map/ppermute | solution.py:21
  40.2 1.5 %collective-permute-done.6.refs_2_ = bf16[160,256]{1,0:T(8,128)(2,1)S(1)} collective-permute-done((bf16[160,256]{1,0:T(8,128)(2,1)S(1)}, bf16[160,256]{1,0:T(8,128)(2,1)S(1)}, u32[]{:S(2)}, u32[]{:S(2)}) %collective-permute-start.6) | collective-permute-done | bytes 81952 | tf_op jit(solution)/shard_map/ppermute | solution.py:21
  41.7 2.2 %collective-permute-done.7.refs_3_ = bf16[160,256]{1,0:T(8,128)(2,1)S(1)} collective-permute-done((bf16[160,256]{1,0:T(8,128)(2,1)S(1)}, bf16[160,256]{1,0:T(8,128)(2,1)S(1)}, u32[]{:S(2)}, u32[]{:S(2)}) %collective-permute-start.7) | collective-permute-done | bytes 81952 | tf_op jit(solution)/shard_map/ppermute | solution.py:21
  43.9 0.9 %collective-permute-start.14 = (bf16[640,256]{1,0:T(8,128)(2,1)S(1)}, bf16[640,256]{1,0:T(8,128)(2,1)S(1)}, u32[]{:S(2)}, u32[]{:S(2)}) collective-permute-start(bf16[640,256]{1,0:T(8,128)(2,1)S(1)} %stack.4.refs_0_), channel_id=1, source_target_pairs={{0,8},{8,0},{16,24},{24,16},{1,9},{9,1},{17,25},{25,17},{2,10},{10... | collective-permute-start | bytes 983048 | tf_op jit(solution)/shard_map/ppermute | solution.py:21
  44.8 0.5 collective-permute-start.15
  45.3 2.1 %collective-permute-start.16 = (bf16[640,256]{1,0:T(8,128)(2,1)S(1)}, bf16[640,256]{1,0:T(8,128)(2,1)S(1)}, u32[]{:S(2)}, u32[]{:S(2)}) collective-permute-start(bf16[640,256]{1,0:T(8,128)(2,1)S(1)} %stack.4.refs_0_), channel_id=1, source_target_pairs={{0,24},{8,16},{16,8},{24,0},{1,25},{9,17},{17,9},{25,1},{2,26},{10... | collective-permute-start | bytes 983048 | tf_op jit(solution)/shard_map/ppermute | solution.py:21
  47.5 2.3 %attend.1.a0 = bf16[2,64,512]{2,1,0:T(8,128)(2,1)S(1)} custom-call(bf16[2,64,512]{2,1,0:T(8,128)(2,1)S(1)} %get-tuple-element.35.refs_4_.own, bf16[2,64,512]{2,1,0:T(8,128)(2,1)S(1)} %collective-permute-done.17.other, f32[256,128]{1,0:T(8,128)S(1)} %get-tuple-element.25.refs_0_.cosine, f32[256,128]{1,0:T(8,128)S(1)} %get-tuple-element.33.sine, ...), custom_call_target="tpu_custom_call" | custom-call | flops 1024 | bytes 1024 | tf_op jit(solution)/shard_map/attend/pallas_call | solution.py:408
  49.8 0.1 collective-permute-start.18
  49.8 2.1 %collective-permute-start.19 = (bf16[2,64,512]{2,1,0:T(8,128)(2,1)S(1)}, bf16[2,64,512]{2,1,0:T(8,128)(2,1)S(1)}, u32[]{:S(2)}, u32[]{:S(2)}) collective-permute-start(bf16[2,64,512]{2,1,0:T(8,128)(2,1)S(1)} %attend.1.a0), channel_id=1, source_target_pairs={{0,4},{2,6},{4,0},{6,2},{1,5},{3,7},{5,1},{7,3},{8,12},{10,14},{12... | collective-permute-start | bytes 393224 | tf_op jit(solution)/shard_map/ppermute | solution.py:21
  52.0 4.4 %collective-permute-done.18.refs_3_.a1 = bf16[2,64,512]{2,1,0:T(8,128)(2,1)S(1)} collective-permute-done((bf16[2,64,512]{2,1,0:T(8,128)(2,1)S(1)}, bf16[2,64,512]{2,1,0:T(8,128)(2,1)S(1)}, u32[]{:S(2)}, u32[]{:S(2)}) %collective-permute-start.18) | collective-permute-done | bytes 131104 | tf_op jit(solution)/shard_map/ppermute | solution.py:21
  56.4 0.4 collective-permute-start.20
  56.8 2.0 %collective-permute-done.19.refs_4_.a2 = bf16[2,64,512]{2,1,0:T(8,128)(2,1)S(1)} collective-permute-done((bf16[2,64,512]{2,1,0:T(8,128)(2,1)S(1)}, bf16[2,64,512]{2,1,0:T(8,128)(2,1)S(1)}, u32[]{:S(2)}, u32[]{:S(2)}) %collective-permute-start.19) | collective-permute-done | bytes 131104 | tf_op jit(solution)/shard_map/ppermute | solution.py:21
  58.7 4.4 %collective-permute-done.20.refs_5_.a3 = bf16[2,64,512]{2,1,0:T(8,128)(2,1)S(1)} collective-permute-done((bf16[2,64,512]{2,1,0:T(8,128)(2,1)S(1)}, bf16[2,64,512]{2,1,0:T(8,128)(2,1)S(1)}, u32[]{:S(2)}, u32[]{:S(2)}) %collective-permute-start.20) | collective-permute-done | bytes 131104 | tf_op jit(solution)/shard_map/ppermute | solution.py:21
  63.1 0.1 stack.5.refs_1_
  63.2 0.0 copy-start.1
  63.2 0.1 collective-permute-start.22
  63.3 0.5 collective-permute-start.21
  63.8 2.5 %collective-permute-done.21.refs_2_ = bf16[640,256]{1,0:T(8,128)(2,1)S(1)} collective-permute-done((bf16[640,256]{1,0:T(8,128)(2,1)S(1)}, bf16[640,256]{1,0:T(8,128)(2,1)S(1)}, u32[]{:S(2)}, u32[]{:S(2)}) %collective-permute-start.21) | collective-permute-done | bytes 327712 | tf_op jit(solution)/shard_map/ppermute | solution.py:21
  66.3 0.3 assemble.1.weight
  66.7 1.9 %output.1 = bf16[2,128,1280]{2,1,0:T(8,128)(2,1)} custom-call(bf16[1280,1024]{1,0:T(8,128)(2,1)S(1)} %assemble.1.weight, bf16[2,64,512]{2,1,0:T(8,128)(2,1)S(1)} %attend.1.a0, bf16[2,64,512]{2,1,0:T(8,128)(2,1)S(1)} %collective-permute-done.18.refs_3_.a1, bf16[2,64,512]{2,1,0:T(8,128)(2,1)S(1)} %collective-permute-done.19.refs_4_.a2, ...), custom_call_target="tpu_custom_call" | custom-call | flops 1024 | bytes 1024 | tf_op jit(solution)/shard_map/output/pallas_call | solution.py:552
  (36 shorter events, 0.2 us)
Async XLA Ops:
  0.0 10.3 %copy-start.8 = (f32[5120]{0:T(1024)S(1)}, f32[5120]{0:T(1024)}, u32[]{:S(2)}) copy-start(f32[5120]{0:T(1024)} %param.17) | copy-start | bytes 61444
  0.0 10.3 %copy-start.9 = (s32[128]{0:T(128)S(1)}, s32[128]{0:T(128)}, u32[]{:S(2)}) copy-start(s32[128]{0:T(128)} %param.31) | copy-start | bytes 1540
  3.7 14.5 %collective-permute-start.2 = (bf16[384,640]{1,0:T(8,128)(2,1)}, bf16[384,640]{1,0:T(8,128)(2,1)S(1)}, u32[]{:S(2)}, u32[]{:S(2)}) collective-permute-start(bf16[384,640]{1,0:T(8,128)(2,1)} %get-tuple-element.24.refs_0_), channel_id=1, source_target_pairs={{0,16},{8,24},{16,0},{24,8},{1,17},{9,25},{17,1},{25,9},{2,18},{10... | collective-permute-start | bytes 1474568 | tf_op jit(solution)/shard_map/ppermute | solution.py:21
  6.7 14.4 %collective-permute-start.1 = (bf16[384,640]{1,0:T(8,128)(2,1)}, bf16[384,640]{1,0:T(8,128)(2,1)S(1)}, u32[]{:S(2)}, u32[]{:S(2)}) collective-permute-start(bf16[384,640]{1,0:T(8,128)(2,1)} %get-tuple-element.24.refs_0_), channel_id=1, source_target_pairs={{0,8},{8,0},{16,24},{24,16},{1,9},{9,1},{17,25},{25,17},{2,10},{10... | collective-permute-start | bytes 1474568 | tf_op jit(solution)/shard_map/ppermute | solution.py:21
  8.2 24.5 %collective-permute-start.4 = (bf16[2,64,32,128]{3,2,1,0:T(8,128)(2,1)}, bf16[2,64,32,128]{3,2,1,0:T(8,128)(2,1)S(1)}, u32[]{:S(2)}, u32[]{:S(2)}) collective-permute-start(bf16[2,64,32,128]{3,2,1,0:T(8,128)(2,1)} %get-tuple-element.27), channel_id=1, source_target_pairs={{0,2},{2,0},{4,6},{6,4},{1,3},{3,1},{5,7},{7,5},{8,10},{10,8},{12,... | collective-permute-start | bytes 3145736 | tf_op jit(solution)/shard_map/ppermute | solution.py:21
  9.8 14.8 %collective-permute-start = (bf16[320,256]{1,0:T(8,128)(2,1)}, bf16[320,256]{1,0:T(8,128)(2,1)S(1)}, u32[]{:S(2)}, u32[]{:S(2)}) collective-permute-start(bf16[320,256]{1,0:T(8,128)(2,1)} %get-tuple-element.22), channel_id=1, source_target_pairs={{0,8},{8,0},{16,24},{24,16},{1,9},{9,1},{17,25},{25,17},{2,10},{10... | collective-permute-start | bytes 491528 | tf_op jit(solution)/shard_map/ppermute | solution.py:21
  10.3 1.7 %copy-start = (bf16[2,128,5120]{2,1,0:T(8,128)(2,1)S(1)}, bf16[2,128,5120]{2,1,0:T(8,128)(2,1)}, u32[]{:S(2)}) copy-start(bf16[2,128,5120]{2,1,0:T(8,128)(2,1)} %hidden.3) | copy-start | bytes 7864324
  12.1 0.9 %copy-start.5 = (bf16[160,256]{1,0:T(8,128)(2,1)S(1)}, bf16[160,256]{1,0:T(8,128)(2,1)}, u32[]{:S(2)}) copy-start(bf16[160,256]{1,0:T(8,128)(2,1)} %get-tuple-element.21.after.own) | copy-start | bytes 245764
  12.9 11.6 %copy-start.7 = (bf16[160,256]{1,0:T(8,128)(2,1)S(1)}, bf16[160,256]{1,0:T(8,128)(2,1)}, u32[]{:S(2)}) copy-start(bf16[160,256]{1,0:T(8,128)(2,1)} %get-tuple-element.23.own) | copy-start | bytes 245764
  13.0 11.8 %copy-start.4 = (bf16[384,640]{1,0:T(8,128)(2,1)S(1)}, bf16[384,640]{1,0:T(8,128)(2,1)}, u32[]{:S(2)}) copy-start(bf16[384,640]{1,0:T(8,128)(2,1)} %get-tuple-element.24.refs_0_) | copy-start | bytes 1474564
  13.0 19.8 %copy-start.6 = (bf16[160,256]{1,0:T(8,128)(2,1)S(1)}, bf16[160,256]{1,0:T(8,128)(2,1)}, u32[]{:S(2)}) copy-start(bf16[160,256]{1,0:T(8,128)(2,1)} %get-tuple-element.21.after.own) | copy-start | bytes 245764
  16.0 21.3 %copy-start.11 = (bf16[256]{0:T(256)(128)(2,1)S(1)}, bf16[256]{0:T(256)(128)(2,1)}, u32[]{:S(2)}) copy-start(bf16[256]{0:T(256)(128)(2,1)} %param.19) | copy-start | bytes 1540
  21.1 7.7 %collective-permute-start.11 = (bf16[192,640]{1,0:T(8,128)(2,1)S(1)}, bf16[192,640]{1,0:T(8,128)(2,1)S(1)}, u32[]{:S(2)}, u32[]{:S(2)}) collective-permute-start(bf16[192,640]{1,0:T(8,128)(2,1)S(1)} %get-tuple-element.26.refs_0_), channel_id=1, source_target_pairs={{0,16},{8,24},{16,0},{24,8},{1,17},{9,25},{17,1},{25,9},{2,18},{10... | collective-permute-start | bytes 737288 | tf_op jit(solution)/shard_map/ppermute | solution.py:21
  21.2 7.6 %collective-permute-start.12 = (bf16[192,640]{1,0:T(8,128)(2,1)S(1)}, bf16[192,640]{1,0:T(8,128)(2,1)S(1)}, u32[]{:S(2)}, u32[]{:S(2)}) collective-permute-start(bf16[192,640]{1,0:T(8,128)(2,1)S(1)} %get-tuple-element.34), channel_id=1, source_target_pairs={{0,8},{8,0},{16,24},{24,16},{1,9},{9,1},{17,25},{25,17},{2,10},{10... | collective-permute-start | bytes 737288 | tf_op jit(solution)/shard_map/ppermute | solution.py:21
  24.6 6.0 %collective-permute-start.3 = (bf16[320,256]{1,0:T(8,128)(2,1)S(1)}, bf16[320,256]{1,0:T(8,128)(2,1)S(1)}, u32[]{:S(2)}, u32[]{:S(2)}) collective-permute-start(bf16[320,256]{1,0:T(8,128)(2,1)S(1)} %relay.1), channel_id=1, source_target_pairs={{0,16},{8,24},{16,0},{24,8},{1,17},{9,25},{17,1},{25,9},{2,18},{10... | collective-permute-start | bytes 491528 | tf_op jit(solution)/shard_map/ppermute | solution.py:21
  24.8 9.7 %collective-permute-start.8 = (bf16[384,640]{1,0:T(8,128)(2,1)S(1)}, bf16[384,640]{1,0:T(8,128)(2,1)S(1)}, u32[]{:S(2)}, u32[]{:S(2)}) collective-permute-start(bf16[384,640]{1,0:T(8,128)(2,1)S(1)} %copy-done.4), channel_id=1, source_target_pairs={{0,1},{1,0},{2,3},{3,2},{4,5},{5,4},{6,7},{7,6},{8,9},{9,8},{10,11... | collective-permute-start | bytes 1474568 | tf_op jit(solution)/shard_map/ppermute | solution.py:21
  28.8 8.3 %collective-permute-start.10 = (bf16[384,640]{1,0:T(8,128)(2,1)S(1)}, bf16[384,640]{1,0:T(8,128)(2,1)S(1)}, u32[]{:S(2)}, u32[]{:S(2)}) collective-permute-start(bf16[384,640]{1,0:T(8,128)(2,1)S(1)} %collective-permute-done.2.along_y.refs_2_), channel_id=1, source_target_pairs={{0,1},{1,0},{2,3},{3,2},{4,5},{5,4},{6,7},{7,6},{8,9},{9,8},{10,11... | collective-permute-start | bytes 1474568 | tf_op jit(solution)/shard_map/ppermute | solution.py:21
  28.8 8.5 %collective-permute-start.9 = (bf16[384,640]{1,0:T(8,128)(2,1)S(1)}, bf16[384,640]{1,0:T(8,128)(2,1)S(1)}, u32[]{:S(2)}, u32[]{:S(2)}) collective-permute-start(bf16[384,640]{1,0:T(8,128)(2,1)S(1)} %collective-permute-done.1.along_x.refs_1_), channel_id=1, source_target_pairs={{0,1},{1,0},{2,3},{3,2},{4,5},{5,4},{6,7},{7,6},{8,9},{9,8},{10,11... | collective-permute-start | bytes 1474568 | tf_op jit(solution)/shard_map/ppermute | solution.py:21
  30.6 8.2 %collective-permute-start.13 = (bf16[384,640]{1,0:T(8,128)(2,1)S(1)}, bf16[384,640]{1,0:T(8,128)(2,1)S(1)}, u32[]{:S(2)}, u32[]{:S(2)}) collective-permute-start(bf16[384,640]{1,0:T(8,128)(2,1)S(1)} %stack.3.refs_0_), channel_id=1, source_target_pairs={{0,1},{1,0},{2,3},{3,2},{4,5},{5,4},{6,7},{7,6},{8,9},{9,8},{10,11... | collective-permute-start | bytes 1474568 | tf_op jit(solution)/shard_map/ppermute | solution.py:21
  32.9 7.3 %collective-permute-start.5 = (bf16[160,256]{1,0:T(8,128)(2,1)S(1)}, bf16[160,256]{1,0:T(8,128)(2,1)S(1)}, u32[]{:S(2)}, u32[]{:S(2)}) collective-permute-start(bf16[160,256]{1,0:T(8,128)(2,1)S(1)} %get-tuple-element.29), channel_id=1, source_target_pairs={{0,2},{2,0},{4,6},{6,4},{1,3},{3,1},{5,7},{7,5},{8,10},{10,8},{12,... | collective-permute-start | bytes 245768 | tf_op jit(solution)/shard_map/ppermute | solution.py:21
  34.5 7.2 %collective-permute-start.6 = (bf16[160,256]{1,0:T(8,128)(2,1)S(1)}, bf16[160,256]{1,0:T(8,128)(2,1)S(1)}, u32[]{:S(2)}, u32[]{:S(2)}) collective-permute-start(bf16[160,256]{1,0:T(8,128)(2,1)S(1)} %get-tuple-element.30), channel_id=1, source_target_pairs={{0,4},{2,6},{4,0},{6,2},{1,5},{3,7},{5,1},{7,3},{8,12},{10,14},{12... | collective-permute-start | bytes 245768 | tf_op jit(solution)/shard_map/ppermute | solution.py:21
  37.1 6.8 %collective-permute-start.7 = (bf16[160,256]{1,0:T(8,128)(2,1)S(1)}, bf16[160,256]{1,0:T(8,128)(2,1)S(1)}, u32[]{:S(2)}, u32[]{:S(2)}) collective-permute-start(bf16[160,256]{1,0:T(8,128)(2,1)S(1)} %get-tuple-element.31), channel_id=1, source_target_pairs={{0,6},{2,4},{4,2},{6,0},{1,7},{3,5},{5,3},{7,1},{8,14},{10,12},{12... | collective-permute-start | bytes 245768 | tf_op jit(solution)/shard_map/ppermute | solution.py:21
  37.3 1.4 %copy-start.10 = (bf16[2,64]{1,0:T(2,128)(2,1)S(1)}, bf16[2,64]{1,0:T(2,128)(2,1)}, u32[]{:S(2)}) copy-start(bf16[2,64]{1,0:T(2,128)(2,1)} %kvb.1) | copy-start | bytes 772
  38.7 8.7 %copy-start.2 = (bf16[128,1,32,128]{3,2,1,0:T(8,128)(2,1)S(1)}, bf16[128,1,32,128]{3,2,1,0:T(8,128)(2,1)}, u32[]{:S(2)}) copy-start(bf16[128,1,32,128]{3,2,1,0:T(8,128)(2,1)} %param.29) | copy-start | bytes 3145732
  38.7 8.7 %copy-start.3 = (bf16[128,1,32,128]{3,2,1,0:T(8,128)(2,1)S(1)}, bf16[128,1,32,128]{3,2,1,0:T(8,128)(2,1)}, u32[]{:S(2)}) copy-start(bf16[128,1,32,128]{3,2,1,0:T(8,128)(2,1)} %param.30) | copy-start | bytes 3145732
  39.4 8.0 %collective-permute-start.17 = (bf16[2,64,512]{2,1,0:T(8,128)(2,1)S(1)}, bf16[2,64,512]{2,1,0:T(8,128)(2,1)S(1)}, u32[]{:S(2)}, u32[]{:S(2)}) collective-permute-start(bf16[2,64,512]{2,1,0:T(8,128)(2,1)S(1)} %get-tuple-element.36), channel_id=1, source_target_pairs={{0,2},{2,0},{4,6},{6,4},{1,3},{3,1},{5,7},{7,5},{8,10},{10,8},{12,... | collective-permute-start | bytes 393224 | tf_op jit(solution)/shard_map/ppermute | solution.py:21
  43.9 19.2 %collective-permute-start.14 = (bf16[640,256]{1,0:T(8,128)(2,1)S(1)}, bf16[640,256]{1,0:T(8,128)(2,1)S(1)}, u32[]{:S(2)}, u32[]{:S(2)}) collective-permute-start(bf16[640,256]{1,0:T(8,128)(2,1)S(1)} %stack.4.refs_0_), channel_id=1, source_target_pairs={{0,8},{8,0},{16,24},{24,16},{1,9},{9,1},{17,25},{25,17},{2,10},{10... | collective-permute-start | bytes 983048 | tf_op jit(solution)/shard_map/ppermute | solution.py:21
  44.8 18.3 %collective-permute-start.15 = (bf16[640,256]{1,0:T(8,128)(2,1)S(1)}, bf16[640,256]{1,0:T(8,128)(2,1)S(1)}, u32[]{:S(2)}, u32[]{:S(2)}) collective-permute-start(bf16[640,256]{1,0:T(8,128)(2,1)S(1)} %stack.4.refs_0_), channel_id=1, source_target_pairs={{0,16},{8,24},{16,0},{24,8},{1,17},{9,25},{17,1},{25,9},{2,18},{10... | collective-permute-start | bytes 983048 | tf_op jit(solution)/shard_map/ppermute | solution.py:21
  45.3 17.8 %collective-permute-start.16 = (bf16[640,256]{1,0:T(8,128)(2,1)S(1)}, bf16[640,256]{1,0:T(8,128)(2,1)S(1)}, u32[]{:S(2)}, u32[]{:S(2)}) collective-permute-start(bf16[640,256]{1,0:T(8,128)(2,1)S(1)} %stack.4.refs_0_), channel_id=1, source_target_pairs={{0,24},{8,16},{16,8},{24,0},{1,25},{9,17},{17,9},{25,1},{2,26},{10... | collective-permute-start | bytes 983048 | tf_op jit(solution)/shard_map/ppermute | solution.py:21
  49.8 6.6 %collective-permute-start.18 = (bf16[2,64,512]{2,1,0:T(8,128)(2,1)S(1)}, bf16[2,64,512]{2,1,0:T(8,128)(2,1)S(1)}, u32[]{:S(2)}, u32[]{:S(2)}) collective-permute-start(bf16[2,64,512]{2,1,0:T(8,128)(2,1)S(1)} %attend.1.a0), channel_id=1, source_target_pairs={{0,2},{2,0},{4,6},{6,4},{1,3},{3,1},{5,7},{7,5},{8,10},{10,8},{12,... | collective-permute-start | bytes 393224 | tf_op jit(solution)/shard_map/ppermute | solution.py:21
  49.8 8.9 %collective-permute-start.19 = (bf16[2,64,512]{2,1,0:T(8,128)(2,1)S(1)}, bf16[2,64,512]{2,1,0:T(8,128)(2,1)S(1)}, u32[]{:S(2)}, u32[]{:S(2)}) collective-permute-start(bf16[2,64,512]{2,1,0:T(8,128)(2,1)S(1)} %attend.1.a0), channel_id=1, source_target_pairs={{0,4},{2,6},{4,0},{6,2},{1,5},{3,7},{5,1},{7,3},{8,12},{10,14},{12... | collective-permute-start | bytes 393224 | tf_op jit(solution)/shard_map/ppermute | solution.py:21
  56.4 6.8 %collective-permute-start.20 = (bf16[2,64,512]{2,1,0:T(8,128)(2,1)S(1)}, bf16[2,64,512]{2,1,0:T(8,128)(2,1)S(1)}, u32[]{:S(2)}, u32[]{:S(2)}) collective-permute-start(bf16[2,64,512]{2,1,0:T(8,128)(2,1)S(1)} %attend.1.a0), channel_id=1, source_target_pairs={{0,6},{2,4},{4,2},{6,0},{1,7},{3,5},{5,3},{7,1},{8,14},{10,12},{12... | collective-permute-start | bytes 393224 | tf_op jit(solution)/shard_map/ppermute | solution.py:21
  63.2 3.4 %copy-start.1 = (bf16[2,128,5120]{2,1,0:T(8,128)(2,1)S(1)}, bf16[2,128,5120]{2,1,0:T(8,128)(2,1)}, u32[]{:S(2)}) copy-start(bf16[2,128,5120]{2,1,0:T(8,128)(2,1)} %hidden.3) | copy-start | bytes 7864324
  63.2 3.1 %collective-permute-start.22 = (bf16[1920,256]{1,0:T(8,128)(2,1)S(1)}, bf16[1920,256]{1,0:T(8,128)(2,1)S(1)}, u32[]{:S(2)}, u32[]{:S(2)}) collective-permute-start(bf16[1920,256]{1,0:T(8,128)(2,1)S(1)} %stack.5.refs_1_), channel_id=1, source_target_pairs={{0,1},{1,0},{2,3},{3,2},{4,5},{5,4},{6,7},{7,6},{8,9},{9,8},{10,11... | collective-permute-start | bytes 2949128 | tf_op jit(solution)/shard_map/ppermute | solution.py:21
  63.3 3.0 %collective-permute-start.21 = (bf16[640,256]{1,0:T(8,128)(2,1)S(1)}, bf16[640,256]{1,0:T(8,128)(2,1)S(1)}, u32[]{:S(2)}, u32[]{:S(2)}) collective-permute-start(bf16[640,256]{1,0:T(8,128)(2,1)S(1)} %stack.4.refs_0_), channel_id=1, source_target_pairs={{0,1},{1,0},{2,3},{3,2},{4,5},{5,4},{6,7},{7,6},{8,9},{9,8},{10,11... | collective-permute-start | bytes 983048 | tf_op jit(solution)/shard_map/ppermute | solution.py:21
